TPU v7x, 32 devices: a whole 2x2x4 slice. The times are simulated.
32 devices in a mesh: rows: 8 (over z, y), seq: 4 (over x, core).
Axes of the slice: x: 2, y: 2, z: 4, core: 2. Of those that a mesh axis runs over, the one named last changes fastest.
Arguments:
- frames: bfloat16 [16, 1024, 768], P('rows', 'seq'), may hold values from -6 to 6
- utterance_lengths: int32 [16, 8], P('rows'), may hold values from 1 to 893, as said below
- tap_dir: bfloat16 [128, 48, 768], replicated, may hold values from -6 to 6
- tap_scale: float32 [128], replicated, may hold values from 1.5 to 4
- conv_bias: float32 [768], replicated, may hold values from -3 to 3
- pos_gain: float32 [768], replicated, may hold values from 0.5 to 1.5
- pos_shift: float32 [768], replicated, may hold values from -2 to 2
- query_weight: bfloat16 [768, 768], replicated, may hold values from -0.3125 to 0.3125
- query_bias: float32 [768], replicated, may hold values from -2 to 2
- key_weight: bfloat16 [768, 768], replicated, may hold values from -0.3125 to 0.3125
- value_weight: bfloat16 [768, 768], replicated, may hold values from -0.21875 to 0.21875
- value_bias: float32 [768], replicated, may hold values from -2 to 2
- proj_weight: bfloat16 [768, 768], replicated, may hold values from -0.625 to 0.625
- proj_bias: float32 [768], replicated, may hold values from -2 to 2
- attend_gain: float32 [768], replicated, may hold values from 0.5 to 1.5
- attend_shift: float32 [768], replicated, may hold values from -2 to 2
- inner_weight: bfloat16 [768, 3072], replicated, may hold values from -0.21875 to 0.21875
- inner_bias: float32 [3072], replicated, may hold values from -2 to 2
- outer_weight: bfloat16 [3072, 768], replicated, may hold values from -0.109375 to 0.109375
- outer_bias: float32 [768], replicated, may hold values from -2 to 2
- final_gain: float32 [768], replicated, may hold values from 0.5 to 1.5
- final_shift: float32 [768], replicated, may hold values from -2 to 2
- out_grad: bfloat16 [16, 1024, 768], P('rows', 'seq'), may hold values from -6 to 6
Outputs:
- layer_out: bfloat16 [16, 1024, 768], P('rows', 'seq')
- frames_grad: bfloat16 [16, 1024, 768], P('rows', 'seq')
- tap_dir_grad: float32 [128, 48, 768], P(None, None, 'seq')
- tap_scale_grad: float32 [128], P('seq')
- conv_bias_grad: float32 [768], P('seq')
- pos_gain_grad: float32 [768], P('seq')
- pos_shift_grad: float32 [768], P('seq')
- query_weight_grad: float32 [768, 768], P(None, 'seq')
- query_bias_grad: float32 [768], P('seq')
- key_weight_grad: float32 [768, 768], P(None, 'seq')
- value_weight_grad: float32 [768, 768], P(None, 'seq')
- value_bias_grad: float32 [768], P('seq')
- proj_weight_grad: float32 [768, 768], P(None, 'seq')
- proj_bias_grad: float32 [768], P('seq')
- attend_gain_grad: float32 [768], P('seq')
- attend_shift_grad: float32 [768], P('seq')
- inner_weight_grad: float32 [768, 3072], P(None, 'seq')
- inner_bias_grad: float32 [3072], P('seq')
- outer_weight_grad: float32 [3072, 768], P(None, 'seq')
- outer_bias_grad: float32 [768], P('seq')
- final_gain_grad: float32 [768], P('seq')
- final_shift_grad: float32 [768], P('seq')
Inputs may be any that keep to these rules, and one draw needn't show every extreme that they name: `utterance_lengths`: each row's 8 lengths sum to 1024. One utterance of each row, among its first four, has exactly the largest length, starts within the row's first 256 frames and ends within its last 256; every other utterance has at most 32 frames.
All inputs are finite; a program needn't handle non-finite values.
Results may differ from a plain program's by a relative error of at most 0.018.
Values may be sent and summed in bfloat16 or wider, within the bound.
No kernel may reach another device: no remote copies, remote signals or barrier semaphores. Data moves between devices by JAX's collectives and lax.ppermute only.
A program may use at most 256 MiB of HBM per device.

v0:
```python
import jax
import jax.numpy as jnp
from jax import lax
from jax.sharding import PartitionSpec as P

HEADS = 12
HEAD_DIM = 64
GROUPS = 16


epsilon = 1e-05
tap_block = 8
big_negative = -1e30


def with_halo(cells, sides, width):
    for axis, dim in sides:
        count = lax.axis_size(axis)
        ends = count - 1
        head = lax.slice_in_dim(cells, 0, width, axis=dim)
        tail = lax.slice_in_dim(cells, cells.shape[dim] - width, cells.shape[dim], axis=dim)
        cells = jnp.concatenate(
            [
                lax.ppermute(tail, axis, [(i, (i + 1) % count) for i in range(ends)]),
                cells,
                lax.ppermute(head, axis, [((i + 1) % count, i) for i in range(ends)]),
            ],
            axis=dim,
        )
    return cells


def layer_norm(values, gain, shift):
    centred = values - jnp.mean(values, axis=-1, keepdims=True)
    spread = jnp.mean(centred * centred, axis=-1, keepdims=True)
    return centred * lax.rsqrt(spread + epsilon) * gain + shift


def normed_taps(tap_dir, tap_scale):
    norms = jnp.sqrt(jnp.sum(tap_dir * tap_dir, axis=(1, 2)))
    return tap_dir * (tap_scale / norms)[:, None, None]


def gelu(values):
    return jax.nn.gelu(values, approximate=False)


def matmul(left, right):
    return jnp.dot(left, right, preferred_element_type=jnp.float32)


def weight_grad(left, right):
    return jnp.einsum("rti,rto->io", left, right, preferred_element_type=jnp.float32)


def input_grad(grad_out, weight):
    return jnp.einsum("rto,io->rti", grad_out, weight, preferred_element_type=jnp.float32)


def column_sum(values):
    return jnp.sum(values.astype(jnp.float32), axis=(0, 1))


def local(
    frames,
    utterance_lengths,
    tap_dir,
    tap_scale,
    conv_bias,
    pos_gain,
    pos_shift,
    query_weight,
    query_bias,
    key_weight,
    value_weight,
    value_bias,
    proj_weight,
    proj_bias,
    attend_gain,
    attend_shift,
    inner_weight,
    inner_bias,
    outer_weight,
    outer_bias,
    final_gain,
    final_shift,
    out_grad,
):
    rows_here, time_here, width = frames.shape
    seq_count = lax.axis_size("seq")
    seq_place = lax.axis_index("seq")
    total_len = time_here * seq_count
    taps_count = tap_dir.shape[0]
    half = taps_count // 2
    channel = width // GROUPS
    local_heads = HEADS // seq_count
    scale_factor = HEAD_DIM ** (-0.5)
    ends = jnp.cumsum(utterance_lengths, axis=1, dtype=jnp.int32)

    def segments_at(places):
        inside = (places >= 0) & (places < total_len)
        found = jnp.sum((places[None, :, None] >= ends[:, None, :]).astype(jnp.int32), axis=2)
        return jnp.where(inside[None, :], found, -1)

    local_segs = segments_at(seq_place * time_here + jnp.arange(time_here, dtype=jnp.int32))
    padded_segs = segments_at(
        seq_place * time_here - half + jnp.arange(time_here + 2 * half, dtype=jnp.int32)
    )
    whole_segs = segments_at(jnp.arange(total_len, dtype=jnp.int32))
    taps_low = normed_taps(tap_dir.astype(jnp.float32), tap_scale).astype(jnp.bfloat16)
    block_count = taps_count // tap_block
    tap_groups = taps_low.reshape(block_count, tap_block, channel, GROUPS, channel)
    block_ids = jnp.arange(block_count, dtype=jnp.int32)

    def masked_window(source, start_list):
        pieces = [lax.dynamic_slice_in_dim(source, start, time_here, 1) for start in start_list]
        marks = [
            lax.dynamic_slice_in_dim(padded_segs, start, time_here, 1) == local_segs
            for start in start_list
        ]
        stacked = jnp.stack(pieces, axis=2)
        allowed = jnp.stack(marks, axis=2)
        stacked = jnp.where(allowed[..., None], stacked, jnp.zeros((), source.dtype))
        return stacked.reshape(rows_here, time_here, tap_block, GROUPS, channel)

    padded = with_halo(frames, (("seq", 1),), half)

    def conv_step(running, block_index):
        starts = [block_index * tap_block + offset for offset in range(tap_block)]
        window_x = masked_window(padded, starts)
        weights = lax.dynamic_index_in_dim(tap_groups, block_index, 0, keepdims=False)
        return (
            running
            + jnp.einsum("rtjgc,jcgo->rtgo", window_x, weights, preferred_element_type=jnp.float32),
            None,
        )

    conv_sum, _ = lax.scan(
        conv_step, jnp.zeros((rows_here, time_here, GROUPS, channel), jnp.float32), block_ids
    )
    conv_pre = conv_sum.reshape(rows_here, time_here, width) + conv_bias
    first_sum = frames.astype(jnp.float32) + gelu(conv_pre)
    mixed = layer_norm(first_sum, pos_gain, pos_shift)
    mixed_low = mixed.astype(jnp.bfloat16)
    queries = ((matmul(mixed_low, query_weight) + query_bias) * scale_factor).astype(jnp.bfloat16)
    keys_time = matmul(mixed_low, key_weight).astype(jnp.bfloat16)
    values_time = (matmul(mixed_low, value_weight) + value_bias).astype(jnp.bfloat16)
    head_q, head_k, head_v = (
        lax.all_to_all(queries, "seq", split_axis=2, concat_axis=1, tiled=True),
        lax.all_to_all(keys_time, "seq", split_axis=2, concat_axis=1, tiled=True),
        lax.all_to_all(values_time, "seq", split_axis=2, concat_axis=1, tiled=True),
    )
    head_shape = (rows_here, total_len, local_heads, HEAD_DIM)
    head_q = head_q.reshape(head_shape)
    head_k = head_k.reshape(head_shape)
    head_v = head_v.reshape(head_shape)
    query_rows = min(512, total_len)
    query_blocks = total_len // query_rows
    query_ids = jnp.arange(query_blocks, dtype=jnp.int32)

    def block_scores(block_index):
        start = block_index * query_rows
        block_q = lax.dynamic_slice_in_dim(head_q, start, query_rows, 1)
        block_segs = lax.dynamic_slice_in_dim(whole_segs, start, query_rows, 1)
        scores = jnp.einsum("rqhe,rkhe->rhqk", block_q, head_k, preferred_element_type=jnp.float32)
        allowed = (block_segs[:, :, None] == whole_segs[:, None, :])[:, None]
        return (block_q, jnp.where(allowed, scores, big_negative))

    def forward_block(block_index):
        block_q, scores = block_scores(block_index)
        peak = jnp.max(scores, axis=-1, keepdims=True)
        raised = jnp.exp(scores - peak)
        totals = jnp.sum(raised, axis=-1, keepdims=True)
        weights = (raised / totals).astype(jnp.bfloat16)
        attended = jnp.einsum(
            "rhqk,rkhe->rqhe", weights, head_v, preferred_element_type=jnp.float32
        )
        return (attended.astype(jnp.bfloat16), (peak + jnp.log(totals))[..., 0])

    attended_blocks, log_totals = lax.map(forward_block, query_ids)
    attended_heads = jnp.moveaxis(attended_blocks, 0, 1).reshape(
        rows_here, total_len, local_heads * HEAD_DIM
    )
    attended_time = lax.all_to_all(attended_heads, "seq", split_axis=1, concat_axis=2, tiled=True)
    second_sum = mixed + matmul(attended_time, proj_weight) + proj_bias
    middle = layer_norm(second_sum, attend_gain, attend_shift)
    middle_low = middle.astype(jnp.bfloat16)
    inner = matmul(middle_low, inner_weight) + inner_bias
    activated = gelu(inner).astype(jnp.bfloat16)
    third_sum = middle + matmul(activated, outer_weight) + outer_bias
    layer_out = layer_norm(third_sum, final_gain, final_shift).astype(jnp.bfloat16)
    _, final_pull = jax.vjp(layer_norm, third_sum, final_gain, final_shift)
    d_third, grad_final_gain, grad_final_shift = final_pull(out_grad.astype(jnp.float32))
    d_outer = d_third.astype(jnp.bfloat16)
    grad_outer_weight = weight_grad(activated, d_outer)
    grad_outer_bias = column_sum(d_outer)
    _, inner_pull = jax.vjp(gelu, inner)
    d_inner = inner_pull(input_grad(d_outer, outer_weight))[0].astype(jnp.bfloat16)
    grad_inner_weight = weight_grad(middle_low, d_inner)
    grad_inner_bias = column_sum(d_inner)
    d_middle = d_third + input_grad(d_inner, inner_weight)
    _, middle_pull = jax.vjp(layer_norm, second_sum, attend_gain, attend_shift)
    d_second, grad_attend_gain, grad_attend_shift = middle_pull(d_middle)
    d_proj = d_second.astype(jnp.bfloat16)
    grad_proj_weight = weight_grad(attended_time, d_proj)
    grad_proj_bias = column_sum(d_proj)
    d_attended = input_grad(d_proj, proj_weight).astype(jnp.bfloat16)
    head_grad = lax.all_to_all(d_attended, "seq", split_axis=2, concat_axis=1, tiled=True).reshape(
        head_shape
    )

    def backward_block(carry, block_index):
        key_sum, value_sum = carry
        block_q, scores = block_scores(block_index)
        block_grad = lax.dynamic_slice_in_dim(head_grad, block_index * query_rows, query_rows, 1)
        block_log = lax.dynamic_index_in_dim(log_totals, block_index, 0, keepdims=False)
        probs = jnp.exp(scores - block_log[..., None])
        value_sum = value_sum + jnp.einsum(
            "rhqk,rqhe->rkhe",
            probs.astype(jnp.bfloat16),
            block_grad,
            preferred_element_type=jnp.float32,
        )
        d_probs = jnp.einsum(
            "rqhe,rkhe->rhqk", block_grad, head_v, preferred_element_type=jnp.float32
        )
        centre = jnp.sum(probs * d_probs, axis=-1, keepdims=True)
        d_scores = (probs * (d_probs - centre)).astype(jnp.bfloat16)
        block_dq = jnp.einsum(
            "rhqk,rkhe->rqhe", d_scores, head_k, preferred_element_type=jnp.float32
        )
        key_sum = key_sum + jnp.einsum(
            "rhqk,rqhe->rkhe", d_scores, block_q, preferred_element_type=jnp.float32
        )
        return ((key_sum, value_sum), block_dq.astype(jnp.bfloat16))

    start_sums = (jnp.zeros(head_shape, jnp.float32), jnp.zeros(head_shape, jnp.float32))
    (key_grad_sum, value_grad_sum), dq_blocks = lax.scan(backward_block, start_sums, query_ids)
    flat_shape = (rows_here, total_len, local_heads * HEAD_DIM)
    dq_heads = jnp.moveaxis(dq_blocks, 0, 1).reshape(flat_shape)
    dk_heads = key_grad_sum.astype(jnp.bfloat16).reshape(flat_shape)
    dv_heads = value_grad_sum.astype(jnp.bfloat16).reshape(flat_shape)
    d_queries, d_keys, d_values = (
        lax.all_to_all(dq_heads, "seq", split_axis=1, concat_axis=2, tiled=True),
        lax.all_to_all(dk_heads, "seq", split_axis=1, concat_axis=2, tiled=True),
        lax.all_to_all(dv_heads, "seq", split_axis=1, concat_axis=2, tiled=True),
    )
    grad_query_weight = weight_grad(mixed_low, d_queries) * scale_factor
    grad_query_bias = column_sum(d_queries) * scale_factor
    grad_key_weight = weight_grad(mixed_low, d_keys)
    grad_value_weight = weight_grad(mixed_low, d_values)
    grad_value_bias = column_sum(d_values)
    d_mixed = (
        d_second
        + input_grad(d_queries, query_weight) * scale_factor
        + input_grad(d_keys, key_weight)
        + input_grad(d_values, value_weight)
    )
    _, mixed_pull = jax.vjp(layer_norm, first_sum, pos_gain, pos_shift)
    d_first, grad_pos_gain, grad_pos_shift = mixed_pull(d_mixed)
    _, conv_pull = jax.vjp(gelu, conv_pre)
    d_conv = conv_pull(d_first)[0].astype(jnp.bfloat16)
    grad_conv_bias = column_sum(d_conv)
    padded_grad = with_halo(d_conv, (("seq", 1),), half)
    grad_rows = d_conv.reshape(rows_here, time_here, GROUPS, channel)

    def grad_step(running, block_index):
        starts_x = [block_index * tap_block + offset for offset in range(tap_block)]
        window_x = masked_window(padded, starts_x)
        tap_part = jnp.einsum(
            "rtjgc,rtgo->jcgo", window_x, grad_rows, preferred_element_type=jnp.float32
        )
        starts_g = [taps_count - block_index * tap_block - offset for offset in range(tap_block)]
        window_g = masked_window(padded_grad, starts_g)
        weights = lax.dynamic_index_in_dim(tap_groups, block_index, 0, keepdims=False)
        running = running + jnp.einsum(
            "rtjgo,jcgo->rtgc", window_g, weights, preferred_element_type=jnp.float32
        )
        return (running, tap_part)

    conv_back, tap_parts = lax.scan(
        grad_step, jnp.zeros((rows_here, time_here, GROUPS, channel), jnp.float32), block_ids
    )
    frames_grad = (d_first + conv_back.reshape(rows_here, time_here, width)).astype(jnp.bfloat16)
    tap_grad = tap_parts.reshape(taps_count, channel, width)
    _, norm_pull = jax.vjp(normed_taps, tap_dir.astype(jnp.float32), tap_scale)
    grad_tap_dir, grad_tap_scale = norm_pull(tap_grad)
    shares = (
        lax.psum_scatter(
            grad_tap_dir.astype(jnp.bfloat16), "seq", scatter_dimension=2, tiled=True
        ).astype(jnp.float32),
        lax.psum_scatter(
            grad_tap_scale.astype(jnp.bfloat16), "seq", scatter_dimension=0, tiled=True
        ).astype(jnp.float32),
        lax.psum_scatter(
            grad_conv_bias.astype(jnp.bfloat16), "seq", scatter_dimension=0, tiled=True
        ).astype(jnp.float32),
        lax.psum_scatter(
            grad_pos_gain.astype(jnp.bfloat16), "seq", scatter_dimension=0, tiled=True
        ).astype(jnp.float32),
        lax.psum_scatter(
            grad_pos_shift.astype(jnp.bfloat16), "seq", scatter_dimension=0, tiled=True
        ).astype(jnp.float32),
        lax.psum_scatter(
            grad_query_weight.astype(jnp.bfloat16), "seq", scatter_dimension=1, tiled=True
        ).astype(jnp.float32),
        lax.psum_scatter(
            grad_query_bias.astype(jnp.bfloat16), "seq", scatter_dimension=0, tiled=True
        ).astype(jnp.float32),
        lax.psum_scatter(
            grad_key_weight.astype(jnp.bfloat16), "seq", scatter_dimension=1, tiled=True
        ).astype(jnp.float32),
        lax.psum_scatter(
            grad_value_weight.astype(jnp.bfloat16), "seq", scatter_dimension=1, tiled=True
        ).astype(jnp.float32),
        lax.psum_scatter(
            grad_value_bias.astype(jnp.bfloat16), "seq", scatter_dimension=0, tiled=True
        ).astype(jnp.float32),
        lax.psum_scatter(
            grad_proj_weight.astype(jnp.bfloat16), "seq", scatter_dimension=1, tiled=True
        ).astype(jnp.float32),
        lax.psum_scatter(
            grad_proj_bias.astype(jnp.bfloat16), "seq", scatter_dimension=0, tiled=True
        ).astype(jnp.float32),
        lax.psum_scatter(
            grad_attend_gain.astype(jnp.bfloat16), "seq", scatter_dimension=0, tiled=True
        ).astype(jnp.float32),
        lax.psum_scatter(
            grad_attend_shift.astype(jnp.bfloat16), "seq", scatter_dimension=0, tiled=True
        ).astype(jnp.float32),
        lax.psum_scatter(
            grad_inner_weight.astype(jnp.bfloat16), "seq", scatter_dimension=1, tiled=True
        ).astype(jnp.float32),
        lax.psum_scatter(
            grad_inner_bias.astype(jnp.bfloat16), "seq", scatter_dimension=0, tiled=True
        ).astype(jnp.float32),
        lax.psum_scatter(
            grad_outer_weight.astype(jnp.bfloat16), "seq", scatter_dimension=1, tiled=True
        ).astype(jnp.float32),
        lax.psum_scatter(
            grad_outer_bias.astype(jnp.bfloat16), "seq", scatter_dimension=0, tiled=True
        ).astype(jnp.float32),
        lax.psum_scatter(
            grad_final_gain.astype(jnp.bfloat16), "seq", scatter_dimension=0, tiled=True
        ).astype(jnp.float32),
        lax.psum_scatter(
            grad_final_shift.astype(jnp.bfloat16), "seq", scatter_dimension=0, tiled=True
        ).astype(jnp.float32),
    )
    totals = lax.psum(
        (
            shares[0],
            shares[1],
            shares[2],
            shares[3],
            shares[4],
            shares[5],
            shares[6],
            shares[7],
            shares[8],
            shares[9],
            shares[10],
            shares[11],
            shares[12],
            shares[13],
            shares[14],
            shares[15],
            shares[16],
            shares[17],
            shares[18],
            shares[19],
        ),
        "rows",
    )
    return (layer_out, frames_grad) + tuple(totals)


def solution(mesh):
    return jax.shard_map(
        local,
        mesh=mesh,
        in_specs=(
            P("rows", "seq", None),
            P("rows", None),
            P(),
            P(),
            P(),
            P(),
            P(),
            P(),
            P(),
            P(),
            P(),
            P(),
            P(),
            P(),
            P(),
            P(),
            P(),
            P(),
            P(),
            P(),
            P(),
            P(),
            P("rows", "seq", None),
        ),
        out_specs=(
            P("rows", "seq", None),
            P("rows", "seq", None),
            P(None, None, "seq"),
            P("seq"),
            P("seq"),
            P("seq"),
            P("seq"),
            P(None, "seq"),
            P("seq"),
            P(None, "seq"),
            P(None, "seq"),
            P("seq"),
            P(None, "seq"),
            P("seq"),
            P("seq"),
            P("seq"),
            P(None, "seq"),
            P("seq"),
            P(None, "seq"),
            P("seq"),
            P("seq"),
            P("seq"),
        ),
        check_vma=False,
    )
```

profile of v0, /device:TPU:0, one launch (start us, length us, event | category | flops | bytes accessed | tf_op | source)
XLA Modules:
  0.0 1739.2 jit_solution(13274159676290101899)
XLA Ops:
  12.7 6.5 fusion.48
  19.6 10.9 fusion.49
  30.5 35.4 %reshape.435 = bf16[16,8,48,16,48]{4,3,2,1,0:T(8,128)(2,1)} reshape(bf16[128,48,768]{2,1,0:T(8,128)(2,1)} %fusion.49) | data formatting | bytes 18874368 | tf_op jit(solution)/shard_map/reshape | solution.py:112
  67.7 283.1 %while.58 = (s32[]{:T(128)}, f32[2,256,16,48]{1,3,0,2:T(8,128)}, s32[16]{0:T(128)S(1)}, bf16[16,8,48,16,48]{4,3,2,1,0:T(8,128)(2,1)}, s32[2,384]{1,0:T(2,128)S(1...) while((s32[]{:T(128)}, f32[2,256,16,48]{1,3,0,2:T(8,128)}, ...), condition=%wide.region_5.6_spmd.clone, body=%wide.region_4.5_spmd.clone.sunk | while | flops 305926176 | bytes 52540196 | solution.py:138
  364.6 6.1 all-to-all-start.2
  374.6 7.8 all-to-all-done.2
  390.0 7.5 all-to-all-done.1
  404.9 9.0 all-to-all-done
  419.9 28.1 %while.57 = (s32[]{:T(128)}, bf16[2,2,512,3,64]{2,4,3,1,0:T(8,128)(2,1)}, f32[2,2,3,512]{3,2,1,0:T(4,128)}, s32[2]{0:T(128)}, s32[2,1024]{1,0:T(2,128)S(1)}, /*i...) while((s32[]{:T(128)}, ...), condition=%wide.region_12.13_spmd, body=%wide.region_9.12_spmd.sunk | while | flops 834860032 | bytes 50929976 | solution.py:180
  458.2 18.9 %all_to_all.132 = bf16[2,1024,192]{2,0,1:T(2,128)(2,1)} all-to-all(bf16[2,1024,192]{2,0,1:T(2,128)(2,1)} %copy.317), channel_id=1, replica_groups=mesh['rows'=8,'seq'=4] {'seq'}, dimensions={1} | all-to-all | bytes 1572864 | tf_op jit(solution)/shard_map/all_to_all | solution.py:184
  485.3 7.0 fusion.79
  492.3 14.6 multiply_convert_fusion.1
  514.3 9.3 fusion.115
  523.6 7.2 multiply_reduce_fusion.1
  543.7 8.3 all-to-all-done.4
  558.6 58.4 %while.59 = (s32[]{:T(128)}, f32[2,1024,3,64]{1,3,2,0:T(8,128)S(1)}, f32[2,1024,3,64]{1,3,2,0:T(8,128)}, bf16[2,2,512,3,64]{2,4,3,1,0:T(8,128)(2,1)}, s32[2]{0:T...) while((s32[]{:T(128)}, ...), condition=%wide.region_23.24_spmd.clone, body=%wide.region_21.23_spmd.clone.sunk | while | flops 2053829632 | bytes 125026720 | solution.py:238
  570.4 6.8 multiply_reduce_fusion.9
  577.1 6.7 multiply_convert_fusion.5
  600.1 6.8 multiply_reduce_fusion.9
  606.9 6.7 multiply_convert_fusion.5
  620.6 18.8 %all_to_all.133 = bf16[2,1024,192]{2,0,1:T(2,128)(2,1)} all-to-all(bf16[2,1024,192]{2,0,1:T(2,128)(2,1)} %copy.333), channel_id=1, replica_groups=mesh['rows'=8,'seq'=4] {'seq'}, dimensions={1} | all-to-all | bytes 1572864 | tf_op jit(solution)/shard_map/all_to_all | solution.py:246
  649.4 19.0 %all_to_all.134 = bf16[2,1024,192]{2,0,1:T(2,128)(2,1)S(1)} all-to-all(bf16[2,1024,192]{2,0,1:T(2,128)(2,1)S(1)} %copy.329), channel_id=1, replica_groups=mesh['rows'=8,'seq'=4] {'seq'}, dimensions={1} | all-to-all | bytes 1572864 | tf_op jit(solution)/shard_map/all_to_all | solution.py:245
  678.8 17.8 %all_to_all.135 = bf16[2,1024,192]{2,0,1:T(2,128)(2,1)S(1)} all-to-all(bf16[2,1024,192]{2,0,1:T(2,128)(2,1)S(1)} %copy.325), channel_id=1, replica_groups=mesh['rows'=8,'seq'=4] {'seq'}, dimensions={1} | all-to-all | bytes 1572864 | tf_op jit(solution)/shard_map/all_to_all | solution.py:244
  702.3 6.5 bitcast_convert_fusion.1
  731.8 376.4 %while.60 = (s32[]{:T(128)}, f32[2,256,16,48]{1,3,0,2:T(8,128)}, f32[16,8,48,16,48]{4,3,2,1,0:T(8,128)}, s32[16]{0:T(128)S(1)}, bf16[16,8,48,16,48]{4,3,2,1,0:T(...) while((s32[]{:T(128)}, f32[2,256,16,48]{1,3,0,2:T(8,128)}, ...), condition=%wide.region_27.28_spmd.clone, body=%wide.region_26.27_spmd.clone.sunk | while | flops 611065920 | bytes 89924968 | solution.py:281
  737.4 6.5 constant_dynamic-slice_fusion.63
  761.3 6.5 constant_dynamic-slice_fusion.63
  784.8 6.5 constant_dynamic-slice_fusion.63
  808.9 6.5 constant_dynamic-slice_fusion.63
  832.5 6.5 constant_dynamic-slice_fusion.63
  855.9 6.5 constant_dynamic-slice_fusion.63
  879.3 6.5 constant_dynamic-slice_fusion.63
  902.8 6.5 constant_dynamic-slice_fusion.63
  926.3 6.5 constant_dynamic-slice_fusion.63
  949.7 6.5 constant_dynamic-slice_fusion.63
  973.1 6.5 constant_dynamic-slice_fusion.63
  996.6 6.5 constant_dynamic-slice_fusion.63
  1020.0 6.5 constant_dynamic-slice_fusion.63
  1043.5 6.5 constant_dynamic-slice_fusion.63
  1066.9 6.5 constant_dynamic-slice_fusion.63
  1090.4 6.5 constant_dynamic-slice_fusion.63
  1108.2 40.1 %reshape.447 = f32[128,48,768]{2,1,0:T(8,128)} reshape(f32[16,8,48,16,48]{4,3,2,1,0:T(8,128)} %get-tuple-element.445) | data formatting | bytes 37748736 | tf_op jit(solution)/shard_map/reshape | solution.py:285
  1148.3 12.0 fusion.50
  1165.5 6.7 fusion.47
  1172.2 14.0 copy.344
  1196.7 14.9 all-reduce.14
  1214.8 53.4 %reduce-scatter.8.cloned.1.call-done = bf16[128,48,192]{0,1,2:T(8,128)(2,1)} async-done(((bf16[128,48,768]{0,1,2:T(8,128)(2,1)}), bf16[128,48,192]{0,1,2:T(8,128)(2,1)}) %reduce-scatter.8.cloned.1.call-update) | async-done | bytes 2359312 | tf_op jit(solution)/shard_map/reduce_scatter | solution.py:289
  1268.1 457.7 %all-reduce.16 = (f32[128,48,192]{0,1,2:T(8,128)}, f32[32]{0:T(128)}, f32[192]{0:T(256)}, f32[192]{0:T(256)}, f32[192]{0:T(256)}, /*index=5*/f32[768,192]{0,1:T(...) all-reduce(bf16[128,48,192]{0,1,2:T(8,128)(2,1)} %reduce-scatter.8., ...), channel_id=1, replica_groups=mesh['rows'=8,'seq'=4] {'rows'}, use_global_device_ids=true, to_apply=%region_30.31 | all-reduce | flops 2952032 | bytes 17718016 | tf_op jit(solution)/shard_map/psum | solution.py:350
  (1426 shorter events, 684.0 us)
Async XLA Ops:
  7.2 354.8 %copy-start = (bf16[768,768]{1,0:T(8,128)(2,1)S(1)}, bf16[768,768]{1,0:T(8,128)(2,1)}, u32[]{:S(2)}) copy-start(bf16[768,768]{1,0:T(8,128)(2,1)} %param.41) | copy-start | bytes 3538948
  8.9 57.1 %collective-permute-start = (bf16[2,64,768]{1,2,0:T(8,128)(2,1)S(1)}, bf16[2,64,768]{1,2,0:T(8,128)(2,1)S(1)}, u32[]{:S(2)}, u32[]{:S(2)}) collective-permute-start(bf16[2,64,768]{1,2,0:T(8,128)(2,1)S(1)} %get-tuple-element.978), channel_id=1, source_target_pairs={{0,1},{1,2},{2,3},{4,5},{5,6},{6,7},{8,9},{9,10},{10,11},{12,13},{... | collective-permute-start | bytes 589832 | tf_op jit(solution)/shard_map/ppermute | solution.py:24
  11.3 54.7 %collective-permute-start.1 = (bf16[2,64,768]{1,2,0:T(8,128)(2,1)S(1)}, bf16[2,64,768]{1,2,0:T(8,128)(2,1)}, u32[]{:S(2)}, u32[]{:S(2)}) collective-permute-start(bf16[2,64,768]{1,2,0:T(8,128)(2,1)S(1)} %get-tuple-element.979), channel_id=1, source_target_pairs={{1,0},{2,1},{3,2},{5,4},{6,5},{7,6},{9,8},{10,9},{11,10},{13,12},{... | collective-permute-start | bytes 589832 | tf_op jit(solution)/shard_map/ppermute | solution.py:26
  12.7 6.6 copy-start.104
  12.7 6.9 copy-start.105
  19.2 11.3 copy-start.100
  19.4 11.1 copy-start.78
  19.6 10.9 copy-start.102
  356.0 4.8 copy-start.20
  360.9 121.6 %copy-start.62 = (f32[2,256]{1,0:T(2,128)}, f32[2,256]{1,0:T(2,128)S(1)}, u32[]{:S(2)}) copy-start(f32[2,256]{1,0:T(2,128)S(1)} %broadcast_multiply_fusion.2) | copy-start | bytes 6148
  362.0 8.7 copy-start.53
  364.6 17.8 %all-to-all-start.2 = ((bf16[2,256,768]{1,0,2:T(2,128)(2,1)}), bf16[2,256,768]{1,0,2:T(2,128)(2,1)S(1)}, u32[]{:S(2)}, u32[]{:S(2)}) async-start(bf16[2,256,768]{1,0,2:T(2,128)(2,1)} %copy.313), calls=%async_computation.2 | async-start | bytes 1572864 | tf_op jit(solution)/shard_map/all_to_all | solution.py:151
  372.7 13.1 copy-start.112
  382.3 15.1 all-to-all-start.1
  388.2 14.0 copy-start.79
  397.5 16.4 all-to-all-start
  448.0 6.6 copy-start.5
  448.0 6.6 copy-start.11
  477.2 5.3 copy-start.9
  482.6 24.4 %slice-start = ((s8[4718592]{0:T(1024)(128)(4,1)}), s8[4194304]{0:T(1024)(128)(4,1)S(1)}, s32[]{:S(2)}) async-start(s8[4718592]{0:T(1024)(128)(4,1)} %bitcast.450), calls=%async_computation.22 | async-start | bytes 8388608
  483.7 23.3 %copy-start.29 = (f32[2,256,768]{2,1,0:T(8,128)}, f32[2,256,768]{2,1,0:T(8,128)S(1)}, u32[]{:S(2)}) copy-start(f32[2,256,768]{2,1,0:T(8,128)S(1)} %get-tuple-element.985) | copy-start | bytes 4718596
  483.7 47.1 %copy-start.72 = (f32[2,256]{1,0:T(2,128)}, f32[2,256]{1,0:T(2,128)S(1)}, u32[]{:S(2)}) copy-start(f32[2,256]{1,0:T(2,128)S(1)} %broadcast_multiply_fusion.1) | copy-start | bytes 6148
  485.3 45.6 %copy-start.89 = (f32[2,256]{1,0:T(2,128)}, f32[2,256]{1,0:T(2,128)S(1)}, u32[]{:S(2)}) copy-start(f32[2,256]{1,0:T(2,128)S(1)} %fusion.99) | copy-start | bytes 6148
  485.3 21.7 %slice-start.1 = ((s8[4718592]{0:T(1024)(128)(4,1)}), s8[524288]{0:T(1024)(128)(4,1)S(1)}, s32[]{:S(2)}) async-start(s8[4718592]{0:T(1024)(128)(4,1)} %bitcast.450), calls=%async_computation.23 | async-start | bytes 1048576
  492.3 14.7 copy-start.114
  514.3 9.3 copy-start.57
  514.3 9.3 copy-start.30
  536.0 15.9 all-to-all-start.4
  540.3 674.4 %reduce-scatter.16.cloned.1.call-start = ((), (), s32[]{:S(2)}) async-start(), calls=%async_computation.19 | async-start | bytes 1474560 | tf_op jit(solution)/shard_map/reduce_scatter | solution.py:319
  543.6 671.1 %reduce-scatter.14.cloned.1.call-start = ((), (), s32[]{:S(2)}) async-start(), calls=%async_computation.18 | async-start | bytes 1474560 | tf_op jit(solution)/shard_map/reduce_scatter | solution.py:313
  566.2 4.2 copy-start.12
  577.1 6.7 copy-start.35
  594.8 5.4 copy-start.12
  606.9 6.7 copy-start.35
  645.9 568.8 %reduce-scatter.12.cloned.1.call-start = ((), (), s32[]{:S(2)}) async-start(), calls=%async_computation.17 | async-start | bytes 1474560 | tf_op jit(solution)/shard_map/reduce_scatter | solution.py:310
  673.7 541.0 %reduce-scatter.10.cloned.1.call-start = ((), (), s32[]{:S(2)}) async-start(), calls=%async_computation.16 | async-start | bytes 1474560 | tf_op jit(solution)/shard_map/reduce_scatter | solution.py:304
  702.2 512.6 %reduce-scatter.18.cloned.1.call-start = ((), (), s32[]{:S(2)}) async-start(), calls=%async_computation.20 | async-start | bytes 5898240 | tf_op jit(solution)/shard_map/reduce_scatter | solution.py:331
  708.8 506.0 %reduce-scatter.20.cloned.1.call-start = ((), (), s32[]{:S(2)}) async-start(), calls=%async_computation.21 | async-start | bytes 5898240 | tf_op jit(solution)/shard_map/reduce_scatter | solution.py:337
  720.1 8.7 collective-permute-start.2
  721.4 7.4 collective-permute-start.3
  727.5 540.6 %reduce-scatter.8.cloned.1.call-start = ((), (), s32[]{:S(2)}) async-start(), calls=%async_computation.15 | async-start | bytes 11796480 | tf_op jit(solution)/shard_map/reduce_scatter | solution.py:289
  1108.2 52.1 %copy-start.106 = (f32[128]{0:T(128)S(1)}, f32[128]{0:T(128)}, u32[]{:S(2)}) copy-start(f32[128]{0:T(128)} %param.34) | copy-start | bytes 1540
  1148.3 12.0 copy-start.101
  1148.3 14.5 copy-start.3
  1148.3 17.2 copy-start.4
  1148.3 17.2 copy-start.103
  1193.4 18.8 %copy-start.17 = (f32[2,256,768]{2,1,0:T(8,128)S(1)}, f32[2,256,768]{2,1,0:T(8,128)}, u32[]{:S(2)}) copy-start(f32[2,256,768]{2,1,0:T(8,128)} %copy-done.16) | copy-start | bytes 4718596
  1193.4 18.8 %copy-start.71 = (f32[2,256]{1,0:T(2,128)S(1)}, f32[2,256]{1,0:T(2,128)}, u32[]{:S(2)}) copy-start(f32[2,256]{1,0:T(2,128)} %copy-done.70) | copy-start | bytes 6148
  (186 other events, 323.4 us)
Sparse Core Ops, SparseCore 0:
  543.7 27.3 reduce-scatter.15
  646.1 27.7 reduce-scatter.13
  676.4 26.6 reduce-scatter.11
  705.7 28.2 reduce-scatter.9
  736.9 47.9 reduce-scatter.17
  787.5 47.8 reduce-scatter.19
  1186.4 81.6 reduce-scatter.7
where the time goes:
time: 1750 us; the launch traced here: 1740 us
  local copies, waits for them, and re-layouts  664 us (38%)
  blocking collectives  547 us (31%)
  matrix products  184 us (11%)
  other arithmetic  119 us (7%)
  loops' own time  96.5 us (6%)
  waiting for transfers between devices  86.1 us (5%)
  starting transfers between devices  25 us (1%)
  between operations  17.9 us (1%)
    psum x1, blocking collectives, local(): lax.psum((shares[0], shares[1], shares[2], shares[3], shares[4], shares[5...  458 us
    dynamic_slice x32, local copies, waits for them, and re-layouts, masked_window(): lax.dynamic_slice_in_dim(source, start, time_here, 1)  155 us
    while x564, local copies, waits for them, and re-layouts  121 us
    dynamic_slice x32, local copies, waits for them, and re-layouts, conv_step(): lax.dynamic_index_in_dim(tap_groups, block_index, 0, keepdims=False)  93.3 us
    dynamic_update_slice x16, local copies, waits for them, and re-layouts, local(): lax.scan(grad_step, jnp.zeros((rows_here, time_here, GROUPS, channel), jn...  56 us
    reduce_scatter x1, waiting for transfers between devices, local(): lax.psum_scatter(grad_tap_dir.astype(jnp.bfloat16), 'seq', scatter_dimens...  53.4 us
    another operation x1, loops' own time, local(): lax.scan(grad_step, jnp.zeros((rows_here, time_here, GROUPS, channel), jn...  45.7 us
    another operation x1, loops' own time, local(): lax.scan(conv_step, jnp.zeros((rows_here, time_here, GROUPS, channel), jn...  43.9 us
  transfers between devices with their start and end apart: 15, of which 5 were waited for; matrix products, arithmetic and copies ran while one was open for 31% of the time, Pallas kernels for 0%

commit v1 on v0

v1 whole, which is shorter than its diff:
```python
import jax, jax.numpy as jnp
from jax import lax
from jax.sharding import PartitionSpec as P
from jax.experimental import pallas as pl
from jax.experimental.pallas import tpu as pltpu
F32=jnp.float32; BF=jnp.bfloat16
CH=48; PH=4; LW=PH*CH
NJ=33; SEGL=48; XROWS=(SEGL+NJ-1)*16; MROWS=SEGL*16
VM=60*1024*1024

def dot(a,b): return jnp.dot(a,b,preferred_element_type=F32)
def dot_nt(a,b): return lax.dot_general(a,b,(((1,),(1,)),((),())),preferred_element_type=F32)
def dot_tn(a,b): return lax.dot_general(a,b,(((0,),(0,)),((),())),preferred_element_type=F32)

def erf_gelu_parts(v):
    phi=0.5*(1.0+lax.erf(v*0.7071067811865476))
    return phi

WROWS=6400
def build_w_kernel(t_ref, w_ref, tp, rs):
    g=pl.program_id(0)
    rows=t_ref.shape[0]
    @pl.when(g==0)
    def _():
        tp[0:144,:]=jnp.zeros((144,LW),BF)
        tp[144:144+rows,:]=t_ref[...]
        tp[144+rows:,:]=jnp.zeros((256,LW),BF)
    src=lax.broadcasted_iota(jnp.int32,(LW,256),0); l=lax.broadcasted_iota(jnp.int32,(LW,256),1)
    pick=((src==48*g+lax.rem(l,48))&(l<LW)).astype(F32).astype(BF)
    n=640
    lane=lax.broadcasted_iota(jnp.int32,(n,256),1)
    for i in range(WROWS//n):
        r0=i*n
        R=dot(tp[r0:r0+n+144,:],pick).astype(BF)
        lo=jnp.where(lane[:,:128]<96,jnp.where(lane[:,:128]<48,R[144:144+n,:128],R[96:96+n,:128]),R[48:48+n,:128])
        hi=jnp.where(lane[:,128:]<144,R[48:48+n,128:],R[0:n,128:])
        w_ref[0,r0:r0+n,:128]=lo
        w_ref[0,r0:r0+n,128:]=hi

def build_w(taps2):
    rows=taps2.shape[0]
    return pl.pallas_call(build_w_kernel,grid=(4,),
        in_specs=[pl.BlockSpec((rows,LW),lambda g:(0,0))],
        out_specs=pl.BlockSpec((1,WROWS,256),lambda g:(g,0,0)),
        out_shape=jax.ShapeDtypeStruct((4,WROWS,256),BF),
        scratch_shapes=[pltpu.VMEM((rows+144+256,LW),BF),pltpu.VMEM((640+144,256),BF)],
        compiler_params=pltpu.CompilerParams(vmem_limit_bytes=VM))(taps2)

def sload(ref,start,n,stride):
    return jnp.concatenate([ref[0,pl.ds(start,n,stride=stride),:],ref[1,pl.ds(start,n,stride=stride),:]],axis=1)[:,:LW]
def sstore(ref,start,n,stride,v):
    ref[0,pl.ds(start,n,stride=stride),:]=v[:,:128]
    ref[1,pl.ds(start,n,stride=stride),:]=jnp.concatenate([v[:,128:],jnp.zeros((n,64),v.dtype)],axis=1)
def fload(ref,start,n):
    return jnp.concatenate([ref[0,pl.ds(start,n),:],ref[1,pl.ds(start,n),:]],axis=1)[:,:LW]
def fstore(ref,start,n,v):
    ref[0,pl.ds(start,n),:]=v[:,:128]
    ref[1,pl.ds(start,n),:]=jnp.concatenate([v[:,128:],jnp.zeros((n,64),v.dtype)],axis=1)

def pick_matrix(g,a):
    ch=lax.broadcasted_iota(jnp.int32,(LW,LW),0); l=lax.broadcasted_iota(jnp.int32,(LW,LW),1)
    return ((ch==48*g+(l-48*a))&(l>=48*a)&(l<48*a+48)).astype(F32).astype(BF)

def lane_times():
    sub=lax.broadcasted_iota(jnp.int32,(16,LW),0); l=lax.broadcasted_iota(jnp.int32,(16,LW),1)
    a=(l>=48).astype(jnp.int32)+(l>=96).astype(jnp.int32)+(l>=144).astype(jnp.int32)
    return 4*sub+a

def bounds(seg_ref,r,q):
    lo=seg_ref[r,q-1] if q>0 else 0
    return lo,seg_ref[r,q]

def respace(seg_ref,pair,src,xr,xsf):
    xsf[0,1280:1296,:]=jnp.zeros((16,128),F32); xsf[1,1280:1296,:]=jnp.zeros((16,128),F32)
    tin=lane_times()
    for r in range(2):
        bl=[bounds(seg_ref,pair*2+r,q) for q in range(8)]
        for B in range(26):
            v=jnp.zeros((16,LW),F32)
            for q in range(8):
                bb=B-1-q
                if 0<=bb<16:
                    t=tin+64*bb
                    v=jnp.where((t>=bl[q][0])&(t<bl[q][1]),src[pl.ds(r*256+16*bb,16),:],v)
            xr[r,pl.ds(16*B,16),:]=v
        for sp in range(8):
            sstore(xsf,r*8+sp,80,16,xr[r,pl.ds(48*sp,80),:])

def unspace(seg_ref,pair,acc,yr,emit):
    tin=lane_times()
    for r in range(2):
        bl=[bounds(seg_ref,pair*2+r,q) for q in range(8)]
        for sp in range(8):
            yr[r,pl.ds(48*sp,48),:]=sload(acc,r*8+sp,48,16)
        for bb in range(16):
            v=jnp.zeros((16,LW),F32)
            t=tin+64*bb
            for q in range(8):
                v=jnp.where((t>=bl[q][0])&(t<bl[q][1]),yr[r,pl.ds(16*(bb+q),16),:],v)
            emit(r*256+16*bb,v)

def conv_fwd_kernel(seg_ref,idx_ref,x0_ref,x1_ref,x2_ref,x3_ref,w_ref,bias_ref,first_ref,pre_ref,xs_ref,xt,xa,x4,xr,xsf,acc,yr,facc,accv,pk):
    pair=pl.program_id(0); g=pl.program_id(1)
    @pl.when(g==0)
    def _():
        for m,x_ref in enumerate((x0_ref,x1_ref,x2_ref,x3_ref)):
            k=pl.multiple_of((idx_ref[0]^m)*256,256)
            for r in range(2):
                fstore(xt,r*1024+k,256,x_ref[r].astype(F32))
        for a in range(4):
            xa[a]=sload(xt,a,512,4).astype(BF)
    v=dot(xa[0],pick_matrix(g,0))
    for a in range(1,4):
        v=v+dot(xa[a],pick_matrix(g,a))
    x4[...]=v
    respace(seg_ref,pair,x4,xr,xsf)
    n=XROWS
    zt=jnp.zeros((n+16,64),F32)
    va=xsf[0,0:n+16,:]; vb=xsf[1,0:n+16,:]
    z0=jnp.concatenate([zt,va[:,:64]],axis=1); z1=jnp.concatenate([va[:,64:],vb[:,:64]],axis=1)
    pk[n:n+32,:]=jnp.zeros((32,384),BF)
    pk[0:n,0:128]=va[0:n].astype(BF)
    pk[0:n,128:256]=(vb[0:n]+z0[16:]).astype(BF)
    pk[0:n,256:384]=z1[16:].astype(BF)
    xs_ref[0,0,:,0:384]=pk[0:n]
    xs_ref[0,0,:,384:768]=pk[32:32+n]
    s=dot(xs_ref[0,0,512:512+MROWS,0:256],w_ref[0,6144:6400,:])
    for J in range(8):
        s=s+dot(xs_ref[0,0,64*J:64*J+MROWS,:],w_ref[0,768*J:768*J+768,:])
    accv[...]=s
    bias=bias_ref[0]
    def emit(row,v):
        pre_ref[0,0,pl.ds(row,16),:]=v+bias
    acc[0]=accv[:,:128]; acc[1]=accv[:,128:]
    unspace(seg_ref,pair,acc,yr,emit)
    pre=pre_ref[0,0]
    fs=(x4[...]+pre*erf_gelu_parts(pre)).astype(BF)
    for a in range(4):
        f=dot_nt(fs,pick_matrix(g,a))
        @pl.when(g==0)
        def _(): facc[a]=f
        @pl.when(g>0)
        def _(): facc[a]=facc[a]+f
    @pl.when(g==3)
    def _():
        for a in range(4):
            sstore(xt,a,512,4,facc[a])
        first_ref[...]=fload(xt,0,2048).astype(BF)

def conv_fwd(ends,idx,xs4,w,bias4):
    R=xs4[0].shape[0]; pairs=R//2
    return pl.pallas_call(conv_fwd_kernel,grid=(pairs,4),
        in_specs=[pl.BlockSpec(memory_space=pltpu.SMEM)]*2+[pl.BlockSpec((2,256,LW),lambda p,g:(p,0,0))]*4+[
                  pl.BlockSpec((1,WROWS,256),lambda p,g:(g,0,0)),
                  pl.BlockSpec((1,1,LW),lambda p,g:(g,0,0))],
        out_specs=[pl.BlockSpec((2048,LW),lambda p,g:(p,0)),
                   pl.BlockSpec((1,1,512,LW),lambda p,g:(p,g,0,0)),
                   pl.BlockSpec((1,1,XROWS,768),lambda p,g:(p,g,0,0))],
        out_shape=[jax.ShapeDtypeStruct((R*1024,LW),BF),
                   jax.ShapeDtypeStruct((pairs,4,512,LW),F32),
                   jax.ShapeDtypeStruct((pairs,4,XROWS,768),BF)],
        scratch_shapes=[pltpu.VMEM((2,2048,128),F32),pltpu.VMEM((4,512,LW),BF),pltpu.VMEM((512,LW),F32),
            pltpu.VMEM((2,416,LW),F32),pltpu.VMEM((2,XROWS+16,128),F32),pltpu.VMEM((2,MROWS,128),F32),pltpu.VMEM((2,384,LW),F32),
            pltpu.VMEM((4,512,LW),F32),pltpu.VMEM((MROWS,256),F32),pltpu.VMEM((XROWS+32,384),BF)],
        compiler_params=pltpu.CompilerParams(vmem_limit_bytes=VM))(ends,idx,*xs4,w,bias4)

def tap_kernel(seg_ref,e0_ref,e1_ref,first_ref,stat_ref,mom_ref,gain_ref,pre_ref,xs_ref,tap_ref,ds_ref,d4_ref,bias_ref,vec_ref,xt,xa,dc,xr,xsf,A):
    pair=pl.program_id(0); g=pl.program_id(1)
    @pl.when(g==0)
    def _():
        gain=gain_ref[...]
        sg=jnp.zeros((1,LW),F32); sh=jnp.zeros((1,LW),F32)
        for t in range(8):
            rows=slice(256*t,256*t+256)
            e=e0_ref[rows]+e1_ref[rows].astype(F32)
            st=stat_ref[rows]
            mean=st[:,0:1]; rstd=st[:,1:2]
            mom=jnp.concatenate([mom_ref[t],jnp.zeros((120,256),F32)],axis=0).T*(1.0/768)
            xhat=(first_ref[rows].astype(F32)-mean)*rstd
            sg=sg+jnp.sum(e*xhat,axis=0,keepdims=True); sh=sh+jnp.sum(e,axis=0,keepdims=True)
            fstore(xt,256*t,256,rstd*(e*gain-mom[:,0:1]-xhat*mom[:,1:2]))
        vec_ref[0,0:1]=sg; vec_ref[0,1:2]=sh; vec_ref[0,2:8]=jnp.zeros((6,LW),F32)
        for a in range(4):
            xa[a]=sload(xt,a,512,4).astype(BF)
    v=dot(xa[0],pick_matrix(g,0))
    for a in range(1,4):
        v=v+dot(xa[a],pick_matrix(g,a))
    d4_ref[0,0]=v.astype(BF)
    pre=pre_ref[0,0]
    cdf=erf_gelu_parts(pre)
    slope=cdf+pre*(jnp.exp(-0.5*pre*pre)*0.3989422804014327)
    d=v*slope
    dc[...]=d
    bias_ref[0,0]=jnp.sum(d,axis=0,keepdims=True)
    respace(seg_ref,pair,dc,xr,xsf)
    ds_ref[0,0,:,0:128]=xsf[0,0:XROWS].astype(BF); ds_ref[0,0,:,128:256]=xsf[1,0:XROWS].astype(BF)
    DT=fload(xsf,256,MROWS).astype(BF).T
    for J in range(8):
        A[:,768*J:768*J+768]=dot(DT,xs_ref[0,0,64*J:64*J+MROWS,:])
    A[:,6144:6400]=dot(DT,xs_ref[0,0,512:512+MROWS,0:256])
    n=6144
    o=A[0:48,0:n]
    for b in range(1,4):
        o=o+A[48*b:48*b+48,48*b:48*b+n]
    for J in range(8):
        tap_ref[0,0,48*J:48*J+48]=o[:,768*J:768*J+768].astype(BF)

def tap_grads(ends,e0,e1,first,stat,mom,gain,pre,xs):
    R=e0.shape[0]//1024; pairs=R//2
    return pl.pallas_call(tap_kernel,grid=(pairs,4),
        in_specs=[pl.BlockSpec(memory_space=pltpu.SMEM),
                  pl.BlockSpec((2048,LW),lambda p,g:(p,0)),
                  pl.BlockSpec((2048,LW),lambda p,g:(p,0)),
                  pl.BlockSpec((2048,LW),lambda p,g:(p,0)),
                  pl.BlockSpec((2048,128),lambda p,g:(p,0)),
                  pl.BlockSpec((8,8,256),lambda p,g:(p,0,0)),
                  pl.BlockSpec((1,LW),lambda p,g:(0,0)),
                  pl.BlockSpec((1,1,512,LW),lambda p,g:(p,g,0,0)),
                  pl.BlockSpec((1,1,XROWS,768),lambda p,g:(p,g,0,0))],
        out_specs=[pl.BlockSpec((1,1,384,768),lambda p,g:(p,g,0,0)),
                   pl.BlockSpec((1,1,XROWS,256),lambda p,g:(p,g,0,0)),
                   pl.BlockSpec((1,1,512,LW),lambda p,g:(p,g,0,0)),
                   pl.BlockSpec((1,1,1,LW),lambda p,g:(p,g,0,0)),
                   pl.BlockSpec((1,8,LW),lambda p,g:(p,0,0))],
        out_shape=[jax.ShapeDtypeStruct((pairs,4,384,768),BF),
                   jax.ShapeDtypeStruct((pairs,4,XROWS,256),BF),
                   jax.ShapeDtypeStruct((pairs,4,512,LW),BF),
                   jax.ShapeDtypeStruct((pairs,4,1,LW),F32),jax.ShapeDtypeStruct((pairs,8,LW),F32)],
        scratch_shapes=[pltpu.VMEM((2,2048,128),F32),pltpu.VMEM((4,512,LW),BF),pltpu.VMEM((512,LW),F32),
            pltpu.VMEM((2,416,LW),F32),pltpu.VMEM((2,XROWS+16,128),F32),pltpu.VMEM((LW,6400),F32)],
        compiler_params=pltpu.CompilerParams(vmem_limit_bytes=VM))(ends,e0,e1,first,stat,mom,gain,pre,xs)

def back_kernel(seg_ref,idx_ref,ds_ref,d4_ref,w_ref,out_ref,xt,acc,yr,fs,facc,accv):
    pair=pl.program_id(0); g=pl.program_id(1)
    s=None
    for j in range(NJ):
        p=dot_nt(ds_ref[0,0,16*(NJ-1-j):16*(NJ-1-j)+MROWS,:],w_ref[0,LW*j:LW*j+256,:])
        s=p if s is None else s+p
    accv[...]=s
    def emit(row,v):
        fs[pl.ds(row,16),:]=(v+d4_ref[0,0,pl.ds(row,16),:].astype(F32)).astype(BF)
    acc[0]=accv[:,:128]; acc[1]=accv[:,128:]
    unspace(seg_ref,pair,acc,yr,emit)
    for a in range(4):
        f=dot_nt(fs[...],pick_matrix(g,a))
        @pl.when(g==0)
        def _(): facc[a]=f
        @pl.when(g>0)
        def _(): facc[a]=facc[a]+f
    @pl.when(g==3)
    def _():
        for a in range(4):
            sstore(xt,a,512,4,facc[a])
        for r in range(2):
            for k in range(4):
                out_ref[idx_ref[0]^k,r]=fload(xt,r*1024+k*256,256).astype(BF)

def conv_back(ends,idx,ds,d4,w):
    pairs=ds.shape[0]; R=2*pairs
    return pl.pallas_call(back_kernel,grid=(pairs,4),
        in_specs=[pl.BlockSpec(memory_space=pltpu.SMEM),pl.BlockSpec(memory_space=pltpu.SMEM),
                  pl.BlockSpec((1,1,XROWS,256),lambda p,g:(p,g,0,0)),
                  pl.BlockSpec((1,1,512,LW),lambda p,g:(p,g,0,0)),
                  pl.BlockSpec((1,WROWS,256),lambda p,g:(g,0,0))],
        out_specs=pl.BlockSpec((4,2,256,LW),lambda p,g:(0,p,0,0)),
        out_shape=jax.ShapeDtypeStruct((4,R,256,LW),BF),
        scratch_shapes=[pltpu.VMEM((2,2048,128),F32),pltpu.VMEM((2,MROWS,128),F32),pltpu.VMEM((2,384,LW),F32),
            pltpu.VMEM((512,LW),BF),pltpu.VMEM((4,512,LW),F32),pltpu.VMEM((MROWS,256),F32)],
        compiler_params=pltpu.CompilerParams(vmem_limit_bytes=VM))(ends,idx,ds,d4,w)


def qkv_kernel(f0,f1,f2,f3,w_ref,bias_ref,gain_ref,shift_ref,q_ref,k_ref,v_ref,ml_ref,stat_ref):
    fs=[f[...].astype(F32) for f in (f0,f1,f2,f3)]
    mean=sum(jnp.sum(f,axis=1,keepdims=True) for f in fs)*(1.0/768)
    cs=[f-mean for f in fs]
    var=sum(jnp.sum(c*c,axis=1,keepdims=True) for c in cs)*(1.0/768)
    rstd=lax.rsqrt(var+1e-5)
    n=mean.shape[0]
    pad=jnp.zeros((n,64),BF)
    out=None
    for m in range(4):
        ml=(cs[m]*rstd*gain_ref[m]+shift_ref[m]).astype(BF)
        ml_ref[m]=ml
        p=dot(jnp.concatenate([ml,pad],axis=1),w_ref[m])
        out=p if out is None else out+p
    out=(out+bias_ref[...]).astype(BF)
    q_ref[...]=out[:,0:192]; k_ref[...]=out[:,256:448]; v_ref[...]=out[:,512:704]
    lane=lax.broadcasted_iota(jnp.int32,(n,128),1)
    stat_ref[...]=jnp.where(lane==0,mean,jnp.where(lane==1,rstd,0.0))

def qkv(fs,w,bias,gain,shift):
    N=fs[0].shape[0]; B=512
    row=pl.BlockSpec((B,LW),lambda i:(i,0))
    full=lambda a: pl.BlockSpec(a.shape,lambda i:(0,)*a.ndim)
    return pl.pallas_call(qkv_kernel,grid=(N//B,),
        in_specs=[row]*4+[full(w),full(bias),full(gain),full(shift)],
        out_specs=[row]*3+[pl.BlockSpec((4,B,LW),lambda i:(0,i,0)),pl.BlockSpec((B,128),lambda i:(i,0))],
        out_shape=[jax.ShapeDtypeStruct((N,LW),BF)]*3+[jax.ShapeDtypeStruct((4,N,LW),BF),jax.ShapeDtypeStruct((N,128),F32)],
        compiler_params=pltpu.CompilerParams(vmem_limit_bytes=VM))(*fs,w,bias,gain,shift)

def seg_vec(seg_ref,r,shape,axis,start):
    t=lax.broadcasted_iota(jnp.int32,shape,axis)+start
    v=jnp.zeros(shape,jnp.int32)
    for i in range(8):
        v=v+(t>=seg_ref[r,i]).astype(jnp.int32)
    return v

def attn_kernel(idx_ref,seg_ref,q_ref,k_ref,v_ref,o_ref,lse_ref):
    r=pl.program_id(0); kb=pl.program_id(1)
    sq=seg_vec(seg_ref,r,(256,1),0,kb*256); sk=seg_vec(seg_ref,r,(1,1024),1,0)
    same=sq==sk
    outs=[]; rows=[]
    for h in range(3):
        c=slice(64*h,64*h+64)
        s=jnp.where(same,dot_nt(q_ref[:,c],k_ref[:,c]),-1e30)
        mx=jnp.max(s,axis=1,keepdims=True)
        p=jnp.exp(s-mx)
        tot=jnp.sum(p,axis=1,keepdims=True)
        outs.append(dot(p.astype(BF),v_ref[:,c])/tot)
        rows.append(jnp.broadcast_to(mx+jnp.log(tot),(256,128)).T[0:1,:])
    o_ref[0,0]=jnp.concatenate(outs,axis=1).astype(BF)
    lse_ref[0,0]=jnp.concatenate(rows+[jnp.zeros((5,256),F32)],axis=0)

def attn(idx,ends,q,k,v):
    R=ends.shape[0]
    return pl.pallas_call(attn_kernel,
        grid_spec=pltpu.PrefetchScalarGridSpec(num_scalar_prefetch=2,grid=(R,4),
        in_specs=[pl.BlockSpec((256,LW),lambda r,b,i,s:(4*r+b,0)),pl.BlockSpec((1024,LW),lambda r,b,i,s:(r,0)),pl.BlockSpec((1024,LW),lambda r,b,i,s:(r,0))],
        out_specs=[pl.BlockSpec((1,1,256,LW),lambda r,b,i,s:(b^i[0],r,0,0)),pl.BlockSpec((1,1,8,256),lambda r,b,i,s:(r,b,0,0))]),
        out_shape=[jax.ShapeDtypeStruct((4,R,256,LW),BF),jax.ShapeDtypeStruct((R,4,8,256),F32)],
        compiler_params=pltpu.CompilerParams(vmem_limit_bytes=VM))(idx,ends,q,k,v)

def attn_bwd_kernel(idx_ref,seg_ref,q_ref,k_ref,v_ref,o_ref,do_ref,lse_ref,dq_ref,dk_ref,dv_ref,dks,dvs):
    r=pl.program_id(0); kb=pl.program_id(1)
    sq=seg_vec(seg_ref,r,(1,256),1,kb*256); sk=seg_vec(seg_ref,r,(1024,1),0,0)
    same=sk==sq
    @pl.when(kb==0)
    def _():
        dks[...]=jnp.zeros_like(dks); dvs[...]=jnp.zeros_like(dvs)
    dqs=[]; ks=[]; vs=[]
    for h in range(3):
        c=slice(64*h,64*h+64)
        q=q_ref[:,c]; k=k_ref[:,c]; do=do_ref[0,0,:,c]
        delta=jnp.sum(do.astype(F32)*o_ref[0,0,:,c].astype(F32),axis=1,keepdims=True)
        delta=jnp.broadcast_to(delta,(256,128)).T[0:1,:]
        st=jnp.where(same,dot_nt(k,q)-lse_ref[0,0,h:h+1,:],-1e30)
        p=jnp.exp(st)
        dp=dot_nt(v_ref[:,c],do)
        ds=(p*(dp-delta)).astype(BF)
        vs.append(dot(p.astype(BF),do)); ks.append(dot(ds,q)); dqs.append(dot_tn(ds,k))
    dks[...]+=jnp.concatenate(ks,axis=1); dvs[...]+=jnp.concatenate(vs,axis=1)
    dq_ref[...]=jnp.concatenate(dqs,axis=1).astype(BF)
    @pl.when(kb==3)
    def _():
        dk_ref[...]=dks[...].astype(BF); dv_ref[...]=dvs[...].astype(BF)

def attn_bwd(idx,ends,q,k,v,o,dos,lse):
    R=ends.shape[0]
    blk=pl.BlockSpec((256,LW),lambda r,b,i,s:(4*r+b,0)); full=pl.BlockSpec((1024,LW),lambda r,b,i,s:(r,0))
    x4=pl.BlockSpec((1,1,256,LW),lambda r,b,i,s:(b^i[0],r,0,0))
    return pl.pallas_call(attn_bwd_kernel,
        grid_spec=pltpu.PrefetchScalarGridSpec(num_scalar_prefetch=2,grid=(R,4),
        in_specs=[blk,full,full,x4,x4,pl.BlockSpec((1,1,8,256),lambda r,b,i,s:(r,b,0,0))],
        out_specs=[blk,full,full],scratch_shapes=[pltpu.VMEM((1024,LW),F32)]*2),
        out_shape=[jax.ShapeDtypeStruct((R*1024,LW),BF)]*3,
        compiler_params=pltpu.CompilerParams(vmem_limit_bytes=VM))(idx,ends,q,k,v,o,dos,lse)

def pad3(a,b,c):
    z=jnp.zeros((a.shape[0],64),BF)
    return jnp.concatenate([a,z,b,z,c,z],axis=1)

def dmix_kernel(idx_ref,dq_ref,dk_ref,dv_ref,w_ref,sec_ref,f0,f1,f2,f3,stat_ref,gain_ref,p0,p1,p2,p3,mom_ref):
    kb=pl.program_id(1)
    d=pad3(dq_ref[...],dk_ref[...],dv_ref[...])
    st=stat_ref[...]; mean=st[:,0:1]; rstd=st[:,1:2]
    mine=(kb==idx_ref[0]).astype(F32)
    m1=None
    for m,(f,p) in enumerate(zip((f0,f1,f2,f3),(p0,p1,p2,p3))):
        part=dot_nt(d,w_ref[m])[:,:LW]
        part=part+mine*sec_ref[m,0]
        p[...]=part.astype(p.dtype)
        eg=part*gain_ref[m]
        xh=(f[...].astype(F32)-mean)*rstd
        a=jnp.sum(eg,axis=1,keepdims=True); b=jnp.sum(eg*xh,axis=1,keepdims=True)
        m1=(a,b) if m1 is None else (m1[0]+a,m1[1]+b)
    lane=lax.broadcasted_iota(jnp.int32,(256,128),1)
    mom_ref[0]=jnp.where(lane==0,m1[0],jnp.where(lane==1,m1[1],0.0)).T[0:8,:]

def dmix(idx,dq,dk,dv,w,sec,fs,stat,gain):
    N=dq.shape[0]; R=N//1024
    blk=pl.BlockSpec((256,LW),lambda r,b,i:(4*r+b,0))
    full=lambda a: pl.BlockSpec(a.shape,lambda r,b,i:(0,)*a.ndim)
    return pl.pallas_call(dmix_kernel,
        grid_spec=pltpu.PrefetchScalarGridSpec(num_scalar_prefetch=1,grid=(R,4),
        in_specs=[blk]*3+[full(w),pl.BlockSpec((4,1,256,LW),lambda r,b,i:(0,r,0,0))]+[blk]*4+[pl.BlockSpec((256,128),lambda r,b,i:(4*r+b,0)),full(gain)],
        out_specs=[blk]*4+[pl.BlockSpec((1,8,256),lambda r,b,i:(4*r+b,0,0))]),
        out_shape=[jax.ShapeDtypeStruct((N,LW),F32)]+[jax.ShapeDtypeStruct((N,LW),BF)]*3+[jax.ShapeDtypeStruct((4*R,8,256),F32)],
        compiler_params=pltpu.CompilerParams(vmem_limit_bytes=VM))(idx,dq,dk,dv,w,sec,*fs,stat,gain)

def qkvw_kernel(dq_ref,dk_ref,dv_ref,ml_ref,out_ref,bias_ref,acc):
    i=pl.program_id(0)
    d=pad3(dq_ref[...],dk_ref[...],dv_ref[...])
    dt=d.T
    @pl.when(i==0)
    def _(): acc[...]=jnp.zeros_like(acc); bias_ref[...]=jnp.zeros_like(bias_ref)
    bias_ref[...]+=jnp.broadcast_to(jnp.sum(d.astype(F32),axis=0,keepdims=True),bias_ref.shape)
    pad=jnp.zeros((d.shape[0],64),BF)
    for m in range(4):
        acc[m]+=dot(dt,jnp.concatenate([ml_ref[m],pad],axis=1))
    @pl.when(i==pl.num_programs(0)-1)
    def _():
        for t in range(3):
            for m in range(4):
                out_ref[t,m]=acc[m,256*t:256*t+192,:LW].astype(BF)

def qkvw(dq,dk,dv,ml):
    N=dq.shape[0]; B=512
    row=pl.BlockSpec((B,LW),lambda i:(i,0))
    return pl.pallas_call(qkvw_kernel,grid=(N//B,),
        in_specs=[row]*3+[pl.BlockSpec((4,B,LW),lambda i:(0,i,0))],
        out_specs=[pl.BlockSpec((3,4,LW,LW),lambda i:(0,0,0,0)),pl.BlockSpec((8,768),lambda i:(0,0))],
        out_shape=[jax.ShapeDtypeStruct((3,4,LW,LW),BF),jax.ShapeDtypeStruct((8,768),F32)],
        scratch_shapes=[pltpu.VMEM((4,768,256),F32)],
        compiler_params=pltpu.CompilerParams(vmem_limit_bytes=VM))(dq,dk,dv,ml)


def swap(x, axis, bit):
    return lax.ppermute(x, axis, [(i, i ^ bit) for i in range(lax.axis_size(axis))])


def halve(x, axis, bit):
    on = (lax.axis_index(axis) & bit) != 0
    h = x.shape[0] // 2
    lo, hi = x[:h], x[h:]
    got = swap(jnp.where(on, lo, hi), axis, bit)
    return (jnp.where(on, hi, lo).astype(F32) + got.astype(F32)).astype(BF)


def double(x, axis, bit):
    on = (lax.axis_index(axis) & bit) != 0
    got = swap(x, axis, bit)
    return jnp.concatenate([jnp.where(on, got, x), jnp.where(on, x, got)], axis=0)


def sum_rows(x):
    n = lax.axis_size("rows")
    bits = [1 << i for i in range(n.bit_length() - 1)]
    orders = (bits, bits[1::-1] + bits[2:])
    count = x.shape[0]
    step = 2 * n * 8
    full = -(-count // step) * step
    if full != count:
        x = jnp.concatenate([x, jnp.zeros((full - count,) + x.shape[1:], x.dtype)], axis=0)
    parts = [x[: full // 2], x[full // 2 :]]
    for s in range(len(bits)):
        parts = [halve(p, "rows", o[s]) for p, o in zip(parts, orders)]
    for s in reversed(range(len(bits))):
        parts = [double(p, "rows", o[s]) for p, o in zip(parts, orders)]
    return jnp.concatenate(parts, axis=0)[:count]


def gather_seq(x):
    far = swap(x, "seq", 2)
    near = swap(x, "seq", 1)
    return [x, near, far, swap(far, "seq", 1)]


def trade(blocks):
    return [blocks[0], swap(blocks[1], "seq", 1), swap(blocks[2], "seq", 2), swap(blocks[3], "seq", 3)]


def scatter_parts(blocks):
    three = swap(blocks[3], "seq", 1)
    one = swap(blocks[1], "seq", 1)
    far = (blocks[2].astype(F32) + three.astype(F32)).astype(BF)
    return blocks[0].astype(F32) + one.astype(F32), swap(far, "seq", 2)


def assemble(blocks, index):
    low = (index & 1) != 0
    high = (index & 2) != 0
    b = [jnp.where(low, blocks[m ^ 1], blocks[m]) for m in range(4)]
    return [jnp.where(high, b[m ^ 2], b[m]) for m in range(4)]


def cut(x, start, size, axis):
    return lax.dynamic_slice_in_dim(x, start, size, axis)


def layer_norm(values, gain, shift):
    centred = values - jnp.mean(values, axis=-1, keepdims=True)
    spread = jnp.mean(centred * centred, axis=-1, keepdims=True)
    return centred * lax.rsqrt(spread + 1e-5) * gain + shift


def gelu(values):
    return jax.nn.gelu(values, approximate=False)


def local(
    frames,
    utterance_lengths,
    tap_dir,
    tap_scale,
    conv_bias,
    pos_gain,
    pos_shift,
    query_weight,
    query_bias,
    key_weight,
    value_weight,
    value_bias,
    proj_weight,
    proj_bias,
    attend_gain,
    attend_shift,
    inner_weight,
    inner_bias,
    outer_weight,
    outer_bias,
    final_gain,
    final_shift,
    out_grad,
):
    R = frames.shape[0]
    index = lax.axis_index("seq")
    idx = jnp.full((1,), index, jnp.int32)
    ends = jnp.cumsum(utterance_lengths, axis=1, dtype=jnp.int32)
    order = [index ^ m for m in range(4)]
    own = index * LW

    sent = trade([cut(frames, b * LW, LW, 2) for b in order])
    norms = jnp.sqrt(jnp.sum(jnp.square(tap_dir.astype(F32)), axis=(1, 2)))
    coef = tap_scale / norms
    dir_own = cut(tap_dir, own, LW, 2).astype(F32)
    taps = (dir_own * coef[:, None, None]).astype(BF).reshape(128 * 48, LW)
    w = build_w(taps)
    bias4 = jnp.tile(cut(conv_bias, own, LW, 0).reshape(4, 1, 48), (1, 4, 1)).reshape(4, 1, LW)
    first, pre, xs = conv_fwd(ends, idx, sent, w, bias4)
    firsts = gather_seq(first)

    def xor_rows(a):
        return jnp.stack([cut(a, b * LW, LW, 0) for b in order])

    def pad_to(a, axis, size):
        widths = [(0, 0)] * a.ndim
        widths[axis] = (0, size - a.shape[axis])
        return jnp.pad(a, widths)

    own_cols = [
        pad_to(cut(a, own, LW, 1), 1, 256)
        for a in (query_weight * jnp.asarray(0.125, BF), key_weight, value_weight)
    ]
    w_qkv = pad_to(xor_rows(jnp.concatenate(own_cols, axis=1)), 1, 256)
    b_qkv = jnp.concatenate(
        [
            pad_to(cut(query_bias, own, LW, 0) * 0.125, 0, 512),
            pad_to(cut(value_bias, own, LW, 0), 0, 256),
        ]
    )[None]
    gain_x = xor_rows(pos_gain)[:, None]
    shift_x = xor_rows(pos_shift)[:, None]
    q, k, v, mixed_low, stat = qkv(firsts, w_qkv, b_qkv, gain_x, shift_x)
    att, lse = attn(idx, ends, q, k, v)
    att_blocks = trade([att[m] for m in range(4)])

    mine = [cut(f.reshape(R, 4, 256, LW), index, 1, 1)[:, 0] for f in firsts]
    first_mine = jnp.concatenate(assemble(mine, index), axis=-1).astype(F32).reshape(R * 256, 768)
    mixed = layer_norm(first_mine, pos_gain, pos_shift)
    attended = jnp.concatenate(assemble(att_blocks, index), axis=-1).reshape(R * 256, 768)
    second_sum = mixed + dot(attended, proj_weight) + proj_bias
    middle = layer_norm(second_sum, attend_gain, attend_shift)
    middle_low = middle.astype(BF)
    inner = dot(middle_low, inner_weight) + inner_bias
    activated = gelu(inner).astype(BF)
    third_sum = middle + dot(activated, outer_weight) + outer_bias
    layer_out, final_pull = jax.vjp(layer_norm, third_sum, final_gain, final_shift)
    d_third, g_final_gain, g_final_shift = final_pull(out_grad.reshape(R * 256, 768).astype(F32))
    layer_out = layer_out.astype(BF).reshape(R, 256, 768)
    d_outer = d_third.astype(BF)
    _, inner_pull = jax.vjp(gelu, inner)
    d_inner = inner_pull(dot_nt(d_outer, outer_weight))[0].astype(BF)
    d_middle = d_third + dot_nt(d_inner, inner_weight)
    _, middle_pull = jax.vjp(layer_norm, second_sum, attend_gain, attend_shift)
    d_second, g_attend_gain, g_attend_shift = middle_pull(d_middle)
    d_proj = d_second.astype(BF)
    d_attended = dot_nt(d_proj, proj_weight).astype(BF).reshape(R, 256, 768)
    do_blocks = trade([cut(d_attended, b * LW, LW, 2) for b in order])
    dos = jnp.stack(do_blocks)
    early = jnp.concatenate(
        [
            g_final_gain,
            g_final_shift,
            jnp.sum(d_outer.astype(F32), axis=0),
            jnp.sum(d_inner.astype(F32), axis=0),
            g_attend_gain,
            g_attend_shift,
            jnp.sum(d_proj.astype(F32), axis=0),
        ]
    )
    g_outer = dot_tn(d_outer, activated).astype(BF)
    g_inner = dot_tn(middle_low, d_inner).astype(BF)
    g_proj = dot_tn(d_proj, attended).astype(BF)

    def bulk(b):
        o = cut(g_outer, b * LW, LW, 0)
        return jnp.concatenate(
            [cut(g_inner, b * 768, 768, 1)]
            + [o[:, 768 * i : 768 * i + 768] for i in range(4)]
            + [cut(g_proj, b * LW, LW, 0)],
            axis=0,
        )

    near, far = scatter_parts([bulk(b) for b in order])
    bulk_sum = sum_rows((near + far.astype(F32)).astype(BF))
    t_inner = bulk_sum[:768].astype(F32)
    t_outer = jnp.concatenate([bulk_sum[768 + LW * i : 768 + LW * i + LW].T for i in range(4)]).astype(F32)
    t_proj = bulk_sum[1536:1728].T.astype(F32)

    dq, dk, dv = attn_bwd(idx, ends, q, k, v, att, dos, lse)
    second_x = jnp.stack([cut(d_second.reshape(R, 256, 768), b * LW, LW, 2) for b in order])
    *parts, moments = dmix(idx, dq, dk, dv, w_qkv, second_x, firsts, stat, gain_x)
    e_near, e_far = scatter_parts(parts)
    m1 = moments + swap(moments, "seq", 1)
    moments = m1 + swap(m1, "seq", 2)
    g_qkv, b_grads = qkvw(dq, dk, dv, mixed_low)
    qkv_sum = sum_rows(g_qkv.reshape(3 * 4 * LW, LW)).reshape(3, 4, LW, LW)
    qkv_std = assemble([qkv_sum[:, m] for m in range(4)], index)
    t_qkv = jnp.concatenate([jnp.swapaxes(b, 1, 2) for b in qkv_std], axis=1).astype(F32)

    tap_part, ds, d4, conv_b, vec = tap_grads(
        ends, e_near, e_far, first, stat, moments, cut(pos_gain, own, LW, 0)[None], pre, xs
    )
    if R > 2:
        tap_part = jnp.sum(tap_part.astype(F32), axis=0).astype(BF)
    tap_sum = sum_rows(tap_part.reshape(1536, 768)).reshape(4, 8, 48, 768)
    back = trade_out(conv_back(ends, idx, ds, d4, w))
    frames_grad = jnp.concatenate(assemble(back, index), axis=-1)
    tap_grad = tap_sum.transpose(1, 3, 0, 2).reshape(128, 48, LW).astype(F32)
    dots = lax.psum(jnp.sum(tap_grad * dir_own, axis=(1, 2)), "seq")
    g_tap_dir = coef[:, None, None] * (tap_grad - dir_own * (dots / (norms * norms))[:, None, None])
    g_tap_scale = cut(dots / norms, index * 32, 32, 0)

    late = jnp.concatenate(
        [
            jnp.sum(conv_b, axis=(0, 2)).reshape(4, 4, 48).sum(1).reshape(LW),
            jnp.sum(vec[:, 0], axis=0),
            jnp.sum(vec[:, 1], axis=0),
            b_grads[0, 0:LW] * 0.125,
            b_grads[0, 512 : 512 + LW],
        ]
    )
    late = lax.psum(late, "rows")
    early = lax.psum(early, ("rows", "seq"))

    def share(a, start, size):
        return cut(a, start + index * size, size, 0)

    return (
        layer_out,
        frames_grad,
        g_tap_dir,
        g_tap_scale,
        late[0:LW],
        late[LW : 2 * LW],
        late[2 * LW : 3 * LW],
        t_qkv[0] * 0.125,
        late[3 * LW : 4 * LW],
        t_qkv[1],
        t_qkv[2],
        late[4 * LW : 5 * LW],
        t_proj,
        share(early, 6912, LW),
        share(early, 5376, LW),
        share(early, 6144, LW),
        t_inner,
        share(early, 2304, 768),
        t_outer,
        share(early, 1536, LW),
        share(early, 0, LW),
        share(early, 768, LW),
    )


def trade_out(x):
    return trade([x[m] for m in range(4)])


def solution(mesh):
    split = P("rows", "seq", None)
    col = P(None, "seq")
    one = P("seq")
    return jax.shard_map(
        local,
        mesh=mesh,
        in_specs=(split, P("rows", None)) + (P(),) * 20 + (split,),
        out_specs=(split, split, P(None, None, "seq"), one, one, one, one)
        + (col, one, col, col, one, col, one, one, one, col, one, col, one, one, one),
        check_vma=False,
    )
```

time: 1750 us -> 717 us (0.41)
  local copies, waits for them, and re-layouts: 664 us -> 111 us
  blocking collectives: 547 us -> 66.5 us
  Pallas kernels: 0 us -> 174 us
  matrix products: 184 us -> 44.3 us
  waiting for transfers between devices: 86.1 us -> 183 us
  loops' own time: 96.5 us -> 0 us
  other arithmetic: 119 us -> 90.2 us
    psum x1 -> x3, blocking collectives: 458 us -> 66.5 us  [the longest x1 41.2 us: local(): early = lax.psum(early, ('rows', 'seq'))]
    dynamic_slice x120 -> x9, local copies, waits for them, and re-layouts: 297 us -> 12.9 us  [cut(): return lax.dynamic_slice_in_dim(x, start, size, axis)]
    ppermute x4 -> x59, waiting for transfers between devices: 0.01 us -> 183 us  [swap(): lax.ppermute(x, axis, [(i, i ^ bit) for i in range(lax.axis_size(axis))])]
    pallas_call x0 -> x9, Pallas kernels: none -> 174 us  [the longest x1 35.1 us: conv_fwd(): pl.pallas_call(conv_fwd_kernel, grid=(pairs, 4), in_specs=[pl.BlockSpec(m...]
    dot_general x80 -> x9, matrix products: 184 us -> 44.3 us  [the longest x3 22.2 us: dot(): return jnp.dot(a, b, preferred_element_type=F32)]
    while x566 -> x0, local copies, waits for them, and re-layouts: 127 us -> none
    another operation x4 -> x0, loops' own time: 96.5 us -> none  [the longest x1 45.7 us: local(): lax.scan(grad_step, jnp.zeros((rows_here, time_here, GROUPS, channel), jn...]
    reshape x14 -> x6, local copies, waits for them, and re-layouts: 101 us -> 6.98 us  [the longest x3 5.72 us: local(): mine = [cut(f.reshape(R, 4, 256, LW), index, 1, 1)[:, 0] for f in firsts]]
  transfers between devices with their start and end apart: 15 -> 59, of which waited for: 5 -> 34; matrix products, arithmetic and copies ran while one was open for 31% -> 24% of each run, Pallas kernels for 0% -> 16%
where the time goes in v1:
time: 717 us; the launch traced here: 711 us
  waiting for transfers between devices  183 us (26%)
  Pallas kernels  174 us (24%)
  local copies, waits for them, and re-layouts  111 us (15%)
  other arithmetic  90.2 us (13%)
  blocking collectives  66.5 us (9%)
  matrix products  44.3 us (6%)
  starting transfers between devices  39.8 us (6%)
    ppermute x59, waiting for transfers between devices, swap(): lax.ppermute(x, axis, [(i, i ^ bit) for i in range(lax.axis_size(axis))])  183 us
    psum x1, blocking collectives, local(): early = lax.psum(early, ('rows', 'seq'))  41.2 us
    ppermute x59, starting transfers between devices, swap(): lax.ppermute(x, axis, [(i, i ^ bit) for i in range(lax.axis_size(axis))])  39.8 us
    unnamed x104, local copies, waits for them, and re-layouts  38.5 us
    pallas_call x1, Pallas kernels, conv_fwd(): pl.pallas_call(conv_fwd_kernel, grid=(pairs, 4), in_specs=[pl.BlockSpec(m...  35.1 us
    pallas_call x1, Pallas kernels, attn_bwd(): pl.pallas_call(attn_bwd_kernel, grid_spec=pltpu.PrefetchScalarGridSpec(nu...  30.2 us
    pallas_call x1, Pallas kernels, conv_back(): pl.pallas_call(back_kernel, grid=(pairs, 4), in_specs=[pl.BlockSpec(memor...  27.9 us
    pallas_call x1, Pallas kernels, tap_grads(): pl.pallas_call(tap_kernel, grid=(pairs, 4), in_specs=[pl.BlockSpec(memory...  24.3 us
  transfers between devices with their start and end apart: 59, of which 34 were waited for; matrix products, arithmetic and copies ran while one was open for 24% of the time, Pallas kernels for 16%

profile of v1, /device:TPU:0, one launch (start us, length us, event | category | flops | bytes accessed | tf_op | source)
XLA Modules:
  0.0 711.1 jit_solution(16985067350799729810)
XLA Ops:
  6.3 5.6 constant_dynamic-slice_fusion.5
  12.0 6.5 multiply_reduce_fusion
  18.5 9.3 %copy.193 = bf16[128,48,192]{1,0,2:T(8,128)(2,1)} copy(bf16[128,48,192]{2,1,0:T(8,128)(2,1)} %constant_dynamic-slice_fusion.5) | data formatting | bytes 4718592
  28.3 8.3 %fusion = bf16[128,48,192]{1,0,2:T(8,128)(2,1)} fusion(bf16[128,48,192]{1,0,2:T(8,128)(2,1)} %copy.193, f32[128]{0:T(128)S(1)} %sqrt_divide_fusion.1), kind=kLoop, calls=%fused_computation.4 | loop fusion | flops 3538944 | bytes 4719104 | tf_op jit(solution)/shard_map/convert_element_type | solution.py:536
  37.3 9.0 %copy.160 = bf16[128,48,192]{2,1,0:T(8,128)(2,1)} copy(bf16[128,48,192]{1,0,2:T(8,128)(2,1)} %fusion) | data formatting | bytes 4718592 | tf_op jit(solution)/shard_map/convert_element_type | solution.py:536
  46.3 9.2 %shard_map.390.w_ref = bf16[4,6400,256]{2,1,0:T(8,128)(2,1)} custom-call(bf16[6144,192]{1,0:T(8,128)(2,1)} %bitcast.173), custom_call_target="tpu_custom_call" | custom-call | tf_op jit(solution)/shard_map/pallas_call | solution.py:42
  58.7 35.1 %shard_map.391 = (bf16[2048,192]{1,0:T(8,128)(2,1)}, f32[1,4,512,192]{3,2,1,0:T(8,128)}, bf16[1,4,1280,768]{3,2,1,0:T(8,128)(2,1)}) custom-call(s32[2,8]{1,0:T(2,128)} %reduce_window_sum.11.seg_ref, s32[1]{0:T(128)} %bitcast.idx_ref, bf16[2,256,192]{2,1,0:T(8,128)(2,1)} %get-tuple-element.304.x0_ref, bf16[2,256,192]{2,1,0:T(8,128)(2,1)} %copy-done.9, ...), custom_call_target="tpu_custom_call" | custom-call | tf_op jit(solution)/shard_map/pallas_call | solution.py:152
  103.2 12.2 %collective-permute-done.3 = bf16[2048,192]{0,1:T(8,128)(2,1)S(1)} collective-permute-done((bf16[2048,192]{0,1:T(8,128)(2,1)S(1)}, bf16[2048,192]{0,1:T(8,128)(2,1)S(1)}, u32[]{:S(2)}, u32[]{:S(2)}) %collective-permute-start.3) | collective-permute-done | bytes 786464 | tf_op jit(solution)/shard_map/ppermute | solution.py:428
  123.7 9.8 %shard_map.392 = (bf16[2048,192]{1,0:T(8,128)(2,1)}, bf16[2048,192]{1,0:T(8,128)(2,1)}, bf16[2048,192]{1,0:T(8,128)(2,1)}, bf16[4,2048,192]{2,1,0:T(8,128)(2,1)}, f32[2048,128]{1,0:T(8,128)}) custom-call(bf16[2048,192]{1,0:T(8,128)(2,1)} %get-tuple-element.47.f0.first_ref, bf16[2048,192]{1,0:T(8,128)(2,1)} %copy.192.f1, bf16[2048,192]{1,0:T(8,128)(2,1)} %copy.191.f2, ...), custom_call_target="tpu_custom_call" | custom-call | tf_op jit(solution)/shard_map/pallas_call | solution.py:295
  133.5 17.7 %shard_map.393 = (bf16[4,2,256,192]{3,2,1,0:T(8,128)(2,1)}, f32[2,4,8,256]{3,2,1,0:T(8,128)}) custom-call(s32[1]{0:T(128)} %bitcast.idx_ref, s32[2,8]{1,0:T(2,128)} %reduce_window_sum.11.seg_ref, bf16[2048,192]{1,0:T(8,128)(2,1)} %get-tuple-element.48.q_ref, bf16[2048,192]{1,0:T(8,128)(2,1)} %get-tuple-element.49.k_ref, ...), custom_call_target="tpu_custom_call" | custom-call | tf_op jit(solution)/shard_map/pallas_call | solution.py:326
  160.6 6.0 collective-permute-done.7
  169.9 18.3 %multiply_convert_fusion = (bf16[512,3072]{1,0:T(8,128)(2,1)S(1)}, f32[512,3072]{1,0:T(8,128)}, f32[512,3072]{1,0:T(8,128)}) fusion(f32[3072]{0:T(1024)S(1)} %copy-done.26, bf16[768,3072]{1,0:T(8,128)(2,1)S(1)} %bitcast.215, f32[512,768]{1,0:T(8,128)S(1)} %get-tuple-element.365, f32[768]{0:T(1024)S(1)} %copy-done.29, f32[768]{0:T(1024)S(1)} %copy-done.20, ...), kind=kOutput, calls=%fused_computation.12 | convolution fusion | flops 2521694208 | bytes 22042624 | tf_op jit(solution)/shard_map/dot_general | solution.py:11
  194.0 9.0 %convert_reduce_fusion = (f32[3072]{0:T(1024)S(1)}, bf16[512,3072]{1,0:T(8,128)(2,1)}) fusion(f32[512,3072]{1,0:T(8,128)} %get-tuple-element.220, f32[512,3072]{1,0:T(8,128)} %get-tuple-element.366, f32[3072]{0:T(1024)S(1)} %copy-done.26, bf16[512,768]{1,0:T(8,128)(2,1)S(1)} %get-tuple-element.214, bf16[3072,768]{1,0:T(8,128)(2,1)S(1)} %bitcast.213), kind=kOutput, calls=%fused_computation.10 | convolution fusion | flops 2442654720 | bytes 21258240 | tf_op jit(solution)/shard_map/dot_general | solution.py:12
  203.0 5.2 multiply_reduce_fusion.1
  238.8 41.2 %psum.23 = f32[7680]{0:T(1024)S(1)} all-reduce(f32[7680]{0:T(1024)} %constant_dynamic-update-slice_fusion.3), channel_id=1, replica_groups=mesh['rows'=8,'seq'=4] {'rows','seq'}, use_global_device_ids=true, to_apply=%region_23.24 | all-reduce | flops 7680 | bytes 61440 | tf_op jit(solution)/shard_map/psum | solution.py:654
  285.2 30.2 %shard_map.394 = (bf16[2048,192]{1,0:T(8,128)(2,1)}, bf16[2048,192]{1,0:T(8,128)(2,1)}, bf16[2048,192]{1,0:T(8,128)(2,1)}) custom-call(s32[1]{0:T(128)} %bitcast.idx_ref, s32[2,8]{1,0:T(2,128)} %reduce_window_sum.11.seg_ref, bf16[2048,192]{1,0:T(8,128)(2,1)} %get-tuple-element.48.q_ref, bf16[2048,192]{1,0:T(8,128)(2,1)} %get-tuple-element.49.k_ref, ...), custom_call_target="tpu_custom_call" | custom-call | tf_op jit(solution)/shard_map/pallas_call | solution.py:361
  315.4 11.5 %shard_map.395 = (f32[2048,192]{1,0:T(8,128)}, bf16[2048,192]{1,0:T(8,128)(2,1)}, bf16[2048,192]{1,0:T(8,128)(2,1)}, bf16[2048,192]{1,0:T(8,128)(2,1)}, f32[8,8,256]{2,1,0:T(8,128)}) custom-call(s32[1]{0:T(128)} %bitcast.idx_ref, bf16[2048,192]{1,0:T(8,128)(2,1)} %get-tuple-element.53.dq_ref, bf16[2048,192]{1,0:T(8,128)(2,1)} %get-tuple-element.54.dk_ref, ...), custom_call_target="tpu_custom_call" | custom-call | tf_op jit(solution)/shard_map/pallas_call | solution.py:393
  329.7 8.1 %shard_map.398 = (bf16[3,4,192,192]{3,2,1,0:T(8,128)(2,1)}, f32[8,768]{1,0:T(8,128)}) custom-call(bf16[2048,192]{1,0:T(8,128)(2,1)} %get-tuple-element.53.dq_ref, bf16[2048,192]{1,0:T(8,128)(2,1)} %get-tuple-element.54.dk_ref, bf16[2048,192]{1,0:T(8,128)(2,1)} %get-tuple-element.55.dv_ref, bf16[4,2048,192]{2,1,0:T(8,128)(2,1)} %get-tuple-element.69.ml_ref), custom_call_target="tpu_custom_call" | custom-call | tf_op jit(solution)/shard_map/pallas_call | solution.py:419
  349.7 5.9 collective-permute-done.38
  368.6 5.0 collective-permute-done.34
  375.0 7.0 collective-permute-done.40
  382.1 6.6 collective-permute-done.35
  388.8 6.1 collective-permute-done.41
  395.3 4.8 collective-permute-done.36
  400.7 4.5 collective-permute-done.42
  405.8 5.6 collective-permute-done.37
  411.8 5.8 collective-permute-done.43
  437.4 24.3 %shard_map.396 = (bf16[1,4,384,768]{3,2,1,0:T(8,128)(2,1)}, bf16[1,4,1280,256]{3,2,1,0:T(8,128)(2,1)}, bf16[1,4,512,192]{3,2,1,0:T(8,128)(2,1)}, f32[1,4,1,192]{3,2,1,0:T(1,128)}, f32[1,8,192]{2,1,0:T(8,128)}) custom-call(s32[2,8]{1,0:T(2,128)} %reduce_window_sum.11.seg_ref, f32[2048,192]{1,0:T(8,128)} %convert_add_fusion.e0_ref, ...), custom_call_target="tpu_custom_call" | custom-call | tf_op jit(solution)/shard_map/pallas_call | solution.py:210
  466.8 27.9 %shard_map.397 = bf16[4,2,256,192]{3,2,1,0:T(8,128)(2,1)} custom-call(s32[2,8]{1,0:T(2,128)} %reduce_window_sum.11.seg_ref, s32[1]{0:T(128)} %bitcast.idx_ref, bf16[1,4,1280,256]{3,2,1,0:T(8,128)(2,1)} %get-tuple-element.64.ds_ref, bf16[1,4,512,192]{3,2,1,0:T(8,128)(2,1)} %get-tuple-element.65.d4_ref, bf16[4,6400,256]{2,1,0:T(8,128)(2,1)} %shard_map.390.w_ref), custom_call_target="tpu_custom_call" | custom-call | tf_op jit(solution)/shard_map/pallas_call | solution.py:260
  499.0 19.6 %psum.22 = f32[960]{0:T(1024)S(1)} all-reduce(f32[960]{0:T(1024)S(1)} %concatenate.102), channel_id=1, replica_groups=mesh['rows'=8,'seq'=4] {'rows'}, use_global_device_ids=true, to_apply=%region_15.16 | all-reduce | flops 960 | bytes 7680 | tf_op jit(solution)/shard_map/psum | solution.py:653
  522.6 6.0 collective-permute-done.27
  528.8 6.7 collective-permute-done.21
  538.6 4.7 add_convert_fusion.2
  549.6 8.0 %collective-permute-done.29 = bf16[96,768]{1,0:T(8,128)(2,1)S(1)} collective-permute-done((bf16[96,768]{1,0:T(8,128)(2,1)S(1)}, bf16[96,768]{1,0:T(8,128)(2,1)S(1)}, u32[]{:S(2)}, u32[]{:S(2)}) %collective-permute-start.29) | collective-permute-done | bytes 147488 | tf_op jit(solution)/shard_map/ppermute | solution.py:428
  557.6 7.3 %collective-permute-done.23 = bf16[96,768]{1,0:T(8,128)(2,1)S(1)} collective-permute-done((bf16[96,768]{1,0:T(8,128)(2,1)S(1)}, bf16[96,768]{1,0:T(8,128)(2,1)S(1)}, u32[]{:S(2)}, u32[]{:S(2)}) %collective-permute-start.23) | collective-permute-done | bytes 147488 | tf_op jit(solution)/shard_map/ppermute | solution.py:428
  565.0 6.6 collective-permute-done.30
  571.9 9.6 %collective-permute-done.24 = bf16[192,768]{1,0:T(8,128)(2,1)S(1)} collective-permute-done((bf16[192,768]{1,0:T(8,128)(2,1)S(1)}, bf16[192,768]{1,0:T(8,128)(2,1)S(1)}, u32[]{:S(2)}, u32[]{:S(2)}) %collective-permute-start.24) | collective-permute-done | bytes 294944 | tf_op jit(solution)/shard_map/ppermute | solution.py:428
  584.1 7.2 %collective-permute-done.31 = bf16[384,768]{1,0:T(8,128)(2,1)S(1)} collective-permute-done((bf16[384,768]{1,0:T(8,128)(2,1)S(1)}, bf16[384,768]{1,0:T(8,128)(2,1)S(1)}, u32[]{:S(2)}, u32[]{:S(2)}) %collective-permute-start.31) | collective-permute-done | bytes 589856 | tf_op jit(solution)/shard_map/ppermute | solution.py:428
  594.9 11.4 %reshape.282 = f32[128,48,192]{1,0,2:T(8,128)} reshape(f32[8,768,4,48]{1,0,3,2:T(8,128)} %bitcast.171) | data formatting | bytes 9437184 | tf_op jit(solution)/shard_map/convert_element_type | solution.py:639
  614.4 8.5 %fusion.1 = f32[128]{0:T(128)S(1)} fusion(f32[128,48,192]{1,0,2:T(8,128)} %reshape.282, bf16[128,48,192]{1,0,2:T(8,128)(2,1)} %copy.193), kind=kLoop, calls=%fused_computation.5 | loop fusion | flops 3538816 | bytes 7078400 | tf_op jit(solution)/shard_map/reduce_sum | solution.py:640
  622.9 5.7 psum.21
  633.5 7.9 %collective-permute-done.48 = bf16[224,768]{1,0:T(8,128)(2,1)S(1)} collective-permute-done((bf16[224,768]{1,0:T(8,128)(2,1)S(1)}, bf16[224,768]{1,0:T(8,128)(2,1)S(1)}, u32[]{:S(2)}, u32[]{:S(2)}) %collective-permute-start.48) | collective-permute-done | bytes 344096 | tf_op jit(solution)/shard_map/ppermute | solution.py:428
  644.9 10.2 %collective-permute-done.49 = bf16[112,768]{1,0:T(8,128)(2,1)S(1)} collective-permute-done((bf16[112,768]{1,0:T(8,128)(2,1)S(1)}, bf16[112,768]{1,0:T(8,128)(2,1)S(1)}, u32[]{:S(2)}, u32[]{:S(2)}) %collective-permute-start.49) | collective-permute-done | bytes 172064 | tf_op jit(solution)/shard_map/ppermute | solution.py:428
  655.2 7.2 %collective-permute-done.55 = bf16[112,768]{1,0:T(8,128)(2,1)S(1)} collective-permute-done((bf16[112,768]{1,0:T(8,128)(2,1)S(1)}, bf16[112,768]{1,0:T(8,128)(2,1)S(1)}, u32[]{:S(2)}, u32[]{:S(2)}) %collective-permute-start.55) | collective-permute-done | bytes 172064 | tf_op jit(solution)/shard_map/ppermute | solution.py:428
  662.6 7.2 %collective-permute-done.50 = bf16[112,768]{1,0:T(8,128)(2,1)S(1)} collective-permute-done((bf16[112,768]{1,0:T(8,128)(2,1)S(1)}, bf16[112,768]{1,0:T(8,128)(2,1)S(1)}, u32[]{:S(2)}, u32[]{:S(2)}) %collective-permute-start.50) | collective-permute-done | bytes 172064 | tf_op jit(solution)/shard_map/ppermute | solution.py:428
  673.5 6.3 collective-permute-done.51
  687.6 5.9 fusion.3
  693.5 9.7 %copy.189 = f32[128,48,192]{0,2,1:T(8,128)} copy(f32[128,48,192]{1,0,2:T(8,128)} %fusion.3) | data formatting | bytes 9437184
  (367 shorter events, 197.5 us)
Async XLA Ops:
  3.2 54.6 %collective-permute-start = (bf16[2,256,192]{2,1,0:T(8,128)(2,1)S(1)}, bf16[2,256,192]{2,1,0:T(8,128)(2,1)S(1)}, u32[]{:S(2)}, u32[]{:S(2)}) collective-permute-start(bf16[2,256,192]{2,1,0:T(8,128)(2,1)S(1)} %get-tuple-element.303), channel_id=1, source_target_pairs={{0,1},{1,0},{2,3},{3,2},{4,5},{5,4},{6,7},{7,6},{8,9},{9,8},{10,11... | collective-permute-start | bytes 589832 | tf_op jit(solution)/shard_map/ppermute | solution.py:428
  3.7 54.2 %collective-permute-start.1 = (bf16[2,256,192]{2,1,0:T(8,128)(2,1)S(1)}, bf16[2,256,192]{2,1,0:T(8,128)(2,1)S(1)}, u32[]{:S(2)}, u32[]{:S(2)}) collective-permute-start(bf16[2,256,192]{2,1,0:T(8,128)(2,1)S(1)} %get-tuple-element.305), channel_id=1, source_target_pairs={{0,2},{1,3},{2,0},{3,1},{4,6},{5,7},{6,4},{7,5},{8,10},{9,11},{10,... | collective-permute-start | bytes 589832 | tf_op jit(solution)/shard_map/ppermute | solution.py:428
  6.2 51.7 %collective-permute-start.2 = (bf16[2,256,192]{2,1,0:T(8,128)(2,1)S(1)}, bf16[2,256,192]{2,1,0:T(8,128)(2,1)S(1)}, u32[]{:S(2)}, u32[]{:S(2)}) collective-permute-start(bf16[2,256,192]{2,1,0:T(8,128)(2,1)S(1)} %get-tuple-element.302), channel_id=1, source_target_pairs={{0,3},{1,2},{2,1},{3,0},{4,7},{5,6},{6,5},{7,4},{8,11},{9,10},{10,... | collective-permute-start | bytes 589832 | tf_op jit(solution)/shard_map/ppermute | solution.py:428
  95.8 19.6 %collective-permute-start.3 = (bf16[2048,192]{0,1:T(8,128)(2,1)S(1)}, bf16[2048,192]{0,1:T(8,128)(2,1)S(1)}, u32[]{:S(2)}, u32[]{:S(2)}) collective-permute-start(bf16[2048,192]{0,1:T(8,128)(2,1)S(1)} %copy.161), channel_id=1, source_target_pairs={{0,2},{1,3},{2,0},{3,1},{4,6},{5,7},{6,4},{7,5},{8,10},{9,11},{10,... | collective-permute-start | bytes 2359304 | tf_op jit(solution)/shard_map/ppermute | solution.py:428
  103.1 16.1 %collective-permute-start.5 = (bf16[2048,192]{0,1:T(8,128)(2,1)S(1)}, bf16[2048,192]{0,1:T(8,128)(2,1)}, u32[]{:S(2)}, u32[]{:S(2)}) collective-permute-start(bf16[2048,192]{0,1:T(8,128)(2,1)S(1)} %copy.161), channel_id=1, source_target_pairs={{0,1},{1,0},{2,3},{3,2},{4,5},{5,4},{6,7},{7,6},{8,9},{9,8},{10,11... | collective-permute-start | bytes 2359304 | tf_op jit(solution)/shard_map/ppermute | solution.py:428
  152.3 8.3 %collective-permute-start.6 = (bf16[2,256,192]{2,1,0:T(8,128)(2,1)S(1)}, bf16[2,256,192]{2,1,0:T(8,128)(2,1)S(1)}, u32[]{:S(2)}, u32[]{:S(2)}) collective-permute-start(bf16[2,256,192]{2,1,0:T(8,128)(2,1)S(1)} %get-tuple-element.297), channel_id=1, source_target_pairs={{0,3},{1,2},{2,1},{3,0},{4,7},{5,6},{6,5},{7,4},{8,11},{9,10},{10,... | collective-permute-start | bytes 589832 | tf_op jit(solution)/shard_map/ppermute | solution.py:428
  153.9 12.6 %collective-permute-start.7 = (bf16[2,256,192]{2,1,0:T(8,128)(2,1)S(1)}, bf16[2,256,192]{2,1,0:T(8,128)(2,1)S(1)}, u32[]{:S(2)}, u32[]{:S(2)}) collective-permute-start(bf16[2,256,192]{2,1,0:T(8,128)(2,1)S(1)} %get-tuple-element.296), channel_id=1, source_target_pairs={{0,2},{1,3},{2,0},{3,1},{4,6},{5,7},{6,4},{7,5},{8,10},{9,11},{10,... | collective-permute-start | bytes 589832 | tf_op jit(solution)/shard_map/ppermute | solution.py:428
  154.5 12.1 %collective-permute-start.8 = (bf16[2,256,192]{2,1,0:T(8,128)(2,1)S(1)}, bf16[2,256,192]{2,1,0:T(8,128)(2,1)S(1)}, u32[]{:S(2)}, u32[]{:S(2)}) collective-permute-start(bf16[2,256,192]{2,1,0:T(8,128)(2,1)S(1)} %get-tuple-element.295), channel_id=1, source_target_pairs={{0,1},{1,0},{2,3},{3,2},{4,5},{5,4},{6,7},{7,6},{8,9},{9,8},{10,11... | collective-permute-start | bytes 589832 | tf_op jit(solution)/shard_map/ppermute | solution.py:428
  218.4 64.5 %collective-permute-start.11 = (bf16[2,256,192]{2,1,0:T(8,128)(2,1)}, bf16[2,256,192]{2,1,0:T(8,128)(2,1)}, u32[]{:S(2)}, u32[]{:S(2)}) collective-permute-start(bf16[2,256,192]{2,1,0:T(8,128)(2,1)} %get-tuple-element.299), channel_id=1, source_target_pairs={{0,3},{1,2},{2,1},{3,0},{4,7},{5,6},{6,5},{7,4},{8,11},{9,10},{10,... | collective-permute-start | bytes 589832 | tf_op jit(solution)/shard_map/ppermute | solution.py:428
  219.0 63.9 %collective-permute-start.10 = (bf16[2,256,192]{2,1,0:T(8,128)(2,1)}, bf16[2,256,192]{2,1,0:T(8,128)(2,1)}, u32[]{:S(2)}, u32[]{:S(2)}) collective-permute-start(bf16[2,256,192]{2,1,0:T(8,128)(2,1)} %get-tuple-element.300), channel_id=1, source_target_pairs={{0,2},{1,3},{2,0},{3,1},{4,6},{5,7},{6,4},{7,5},{8,10},{9,11},{10,... | collective-permute-start | bytes 589832 | tf_op jit(solution)/shard_map/ppermute | solution.py:428
  219.9 63.0 %collective-permute-start.9 = (bf16[2,256,192]{2,1,0:T(8,128)(2,1)}, bf16[2,256,192]{2,1,0:T(8,128)(2,1)}, u32[]{:S(2)}, u32[]{:S(2)}) collective-permute-start(bf16[2,256,192]{2,1,0:T(8,128)(2,1)} %get-tuple-element.301), channel_id=1, source_target_pairs={{0,1},{1,0},{2,3},{3,2},{4,5},{5,4},{6,7},{7,6},{8,9},{9,8},{10,11... | collective-permute-start | bytes 589832 | tf_op jit(solution)/shard_map/ppermute | solution.py:428
  229.2 306.4 %collective-permute-start.45 = (bf16[1728,768]{1,0:T(8,128)(2,1)}, bf16[1728,768]{1,0:T(8,128)(2,1)}, u32[]{:S(2)}, u32[]{:S(2)}) collective-permute-start(bf16[1728,768]{1,0:T(8,128)(2,1)} %get-tuple-element.273), channel_id=1, source_target_pairs={{0,1},{1,0},{2,3},{3,2},{4,5},{5,4},{6,7},{7,6},{8,9},{9,8},{10,11... | collective-permute-start | bytes 7962632 | tf_op jit(solution)/shard_map/ppermute | solution.py:428
  229.3 376.9 %collective-permute-start.44 = (bf16[1728,768]{1,0:T(8,128)(2,1)}, bf16[1728,768]{1,0:T(8,128)(2,1)}, u32[]{:S(2)}, u32[]{:S(2)}) collective-permute-start(bf16[1728,768]{1,0:T(8,128)(2,1)} %get-tuple-element.275), channel_id=1, source_target_pairs={{0,1},{1,0},{2,3},{3,2},{4,5},{5,4},{6,7},{7,6},{8,9},{9,8},{10,11... | collective-permute-start | bytes 7962632 | tf_op jit(solution)/shard_map/ppermute | solution.py:428
  329.2 101.1 %collective-permute-start.12 = (bf16[2048,192]{0,1:T(8,128)(2,1)}, bf16[2048,192]{0,1:T(8,128)(2,1)}, u32[]{:S(2)}, u32[]{:S(2)}) collective-permute-start(bf16[2048,192]{0,1:T(8,128)(2,1)} %copy.174), channel_id=1, source_target_pairs={{0,1},{1,0},{2,3},{3,2},{4,5},{5,4},{6,7},{7,6},{8,9},{9,8},{10,11... | collective-permute-start | bytes 2359304 | tf_op jit(solution)/shard_map/ppermute | solution.py:428
  329.2 13.1 %collective-permute-start.15 = (f32[8,8,256]{2,1,0:T(8,128)}, f32[8,8,256]{2,1,0:T(8,128)S(1)}, u32[]{:S(2)}, u32[]{:S(2)}) collective-permute-start(f32[8,8,256]{2,1,0:T(8,128)} %get-tuple-element.61), channel_id=1, source_target_pairs={{0,1},{1,0},{2,3},{3,2},{4,5},{5,4},{6,7},{7,6},{8,9},{9,8},{10,11... | collective-permute-start | bytes 196616 | tf_op jit(solution)/shard_map/ppermute | solution.py:428
  339.6 8.5 %collective-permute-start.32 = (bf16[576,192]{0,1:T(8,128)(2,1)S(1)}, bf16[576,192]{0,1:T(8,128)(2,1)S(1)}, u32[]{:S(2)}, u32[]{:S(2)}) collective-permute-start(bf16[576,192]{0,1:T(8,128)(2,1)S(1)} %broadcast_select_fusion.57), channel_id=1, source_target_pairs={{0,4},{4,0},{8,12},{12,8},{16,20},{20,16},{24,28},{28,24},{1,5},{5... | collective-permute-start | bytes 663560 | tf_op jit(solution)/shard_map/ppermute | solution.py:428
  346.7 72.9 %collective-permute-start.13 = (bf16[2048,192]{0,1:T(8,128)(2,1)}, bf16[2048,192]{0,1:T(8,128)(2,1)S(1)}, u32[]{:S(2)}, u32[]{:S(2)}) collective-permute-start(bf16[2048,192]{0,1:T(8,128)(2,1)} %copy.176), channel_id=1, source_target_pairs={{0,1},{1,0},{2,3},{3,2},{4,5},{5,4},{6,7},{7,6},{8,9},{9,8},{10,11... | collective-permute-start | bytes 2359304 | tf_op jit(solution)/shard_map/ppermute | solution.py:428
  348.0 7.7 %collective-permute-start.38 = (bf16[576,192]{0,1:T(8,128)(2,1)S(1)}, bf16[576,192]{0,1:T(8,128)(2,1)S(1)}, u32[]{:S(2)}, u32[]{:S(2)}) collective-permute-start(bf16[576,192]{0,1:T(8,128)(2,1)S(1)} %broadcast_select_fusion.54), channel_id=1, source_target_pairs={{0,8},{4,12},{8,0},{12,4},{16,24},{20,28},{24,16},{28,20},{1,9},{5... | collective-permute-start | bytes 663560 | tf_op jit(solution)/shard_map/ppermute | solution.py:428
  366.0 7.6 %collective-permute-start.34 = (bf16[144,192]{0,1:T(8,128)(2,1)S(1)}, bf16[144,192]{0,1:T(8,128)(2,1)S(1)}, u32[]{:S(2)}, u32[]{:S(2)}) collective-permute-start(bf16[144,192]{0,1:T(8,128)(2,1)S(1)} %broadcast_select_fusion.81), channel_id=1, source_target_pairs={{0,16},{4,20},{8,24},{12,28},{16,0},{20,4},{24,8},{28,12},{1,17},{... | collective-permute-start | bytes 165896 | tf_op jit(solution)/shard_map/ppermute | solution.py:428
  373.6 8.4 %collective-permute-start.40 = (bf16[144,192]{0,1:T(8,128)(2,1)S(1)}, bf16[144,192]{0,1:T(8,128)(2,1)S(1)}, u32[]{:S(2)}, u32[]{:S(2)}) collective-permute-start(bf16[144,192]{0,1:T(8,128)(2,1)S(1)} %broadcast_select_fusion.78), channel_id=1, source_target_pairs={{0,16},{4,20},{8,24},{12,28},{16,0},{20,4},{24,8},{28,12},{1,17},{... | collective-permute-start | bytes 165896 | tf_op jit(solution)/shard_map/ppermute | solution.py:428
  422.8 12.3 %collective-permute-start.14 = (bf16[2048,192]{0,1:T(8,128)(2,1)}, bf16[2048,192]{0,1:T(8,128)(2,1)}, u32[]{:S(2)}, u32[]{:S(2)}) collective-permute-start(bf16[2048,192]{0,1:T(8,128)(2,1)} %copy.178), channel_id=1, source_target_pairs={{0,2},{1,3},{2,0},{3,1},{4,6},{5,7},{6,4},{7,5},{8,10},{9,11},{10,... | collective-permute-start | bytes 2359304 | tf_op jit(solution)/shard_map/ppermute | solution.py:428
  464.2 54.5 %collective-permute-start.20 = (bf16[384,768]{1,0:T(8,128)(2,1)}, bf16[384,768]{1,0:T(8,128)(2,1)S(1)}, u32[]{:S(2)}, u32[]{:S(2)}) collective-permute-start(bf16[384,768]{1,0:T(8,128)(2,1)} %get-tuple-element.250), channel_id=1, source_target_pairs={{0,4},{4,0},{8,12},{12,8},{16,20},{20,16},{24,28},{28,24},{1,5},{5... | collective-permute-start | bytes 1769480 | tf_op jit(solution)/shard_map/ppermute | solution.py:428
  465.0 55.2 %collective-permute-start.26 = (bf16[384,768]{1,0:T(8,128)(2,1)S(1)}, bf16[384,768]{1,0:T(8,128)(2,1)}, u32[]{:S(2)}, u32[]{:S(2)}) collective-permute-start(bf16[384,768]{1,0:T(8,128)(2,1)S(1)} %get-tuple-element.251), channel_id=1, source_target_pairs={{0,8},{4,12},{8,0},{12,4},{16,24},{20,28},{24,16},{28,20},{1,9},{5... | collective-permute-start | bytes 1769480 | tf_op jit(solution)/shard_map/ppermute | solution.py:428
  496.7 75.1 %collective-permute-start.17 = (bf16[2,256,192]{2,1,0:T(8,128)(2,1)}, bf16[2,256,192]{2,1,0:T(8,128)(2,1)}, u32[]{:S(2)}, u32[]{:S(2)}) collective-permute-start(bf16[2,256,192]{2,1,0:T(8,128)(2,1)} %get-tuple-element.294), channel_id=1, source_target_pairs={{0,3},{1,2},{2,1},{3,0},{4,7},{5,6},{6,5},{7,4},{8,11},{9,10},{10,... | collective-permute-start | bytes 589832 | tf_op jit(solution)/shard_map/ppermute | solution.py:428
  518.6 62.9 %collective-permute-start.18 = (bf16[2,256,192]{2,1,0:T(8,128)(2,1)}, bf16[2,256,192]{2,1,0:T(8,128)(2,1)S(1)}, u32[]{:S(2)}, u32[]{:S(2)}) collective-permute-start(bf16[2,256,192]{2,1,0:T(8,128)(2,1)} %get-tuple-element.293), channel_id=1, source_target_pairs={{0,2},{1,3},{2,0},{3,1},{4,6},{5,7},{6,4},{7,5},{8,10},{9,11},{10,... | collective-permute-start | bytes 589832 | tf_op jit(solution)/shard_map/ppermute | solution.py:428
  521.9 6.8 collective-permute-start.27
  528.7 6.8 collective-permute-start.21
  535.5 10.9 %collective-permute-start.28 = (bf16[96,768]{1,0:T(8,128)(2,1)S(1)}, bf16[96,768]{1,0:T(8,128)(2,1)S(1)}, u32[]{:S(2)}, u32[]{:S(2)}) collective-permute-start(bf16[96,768]{1,0:T(8,128)(2,1)S(1)} %broadcast_select_fusion.72), channel_id=1, source_target_pairs={{0,16},{4,20},{8,24},{12,28},{16,0},{20,4},{24,8},{28,12},{1,17},{... | collective-permute-start | bytes 442376 | tf_op jit(solution)/shard_map/ppermute | solution.py:428
  535.7 13.8 %collective-permute-start.22 = (bf16[96,768]{1,0:T(8,128)(2,1)S(1)}, bf16[96,768]{1,0:T(8,128)(2,1)S(1)}, u32[]{:S(2)}, u32[]{:S(2)}) collective-permute-start(bf16[96,768]{1,0:T(8,128)(2,1)S(1)} %broadcast_select_fusion.75), channel_id=1, source_target_pairs={{0,16},{4,20},{8,24},{12,28},{16,0},{20,4},{24,8},{28,12},{1,17},{... | collective-permute-start | bytes 442376 | tf_op jit(solution)/shard_map/ppermute | solution.py:428
  546.4 59.9 %collective-permute-start.46 = (bf16[1728,768]{1,0:T(8,128)(2,1)}, bf16[1728,768]{1,0:T(8,128)(2,1)}, u32[]{:S(2)}, u32[]{:S(2)}) collective-permute-start(bf16[1728,768]{1,0:T(8,128)(2,1)} %add_convert_fusion.2), channel_id=1, source_target_pairs={{0,2},{1,3},{2,0},{3,1},{4,6},{5,7},{6,4},{7,5},{8,10},{9,11},{10,... | collective-permute-start | bytes 7962632 | tf_op jit(solution)/shard_map/ppermute | solution.py:428
  549.5 8.1 %collective-permute-start.29 = (bf16[96,768]{1,0:T(8,128)(2,1)S(1)}, bf16[96,768]{1,0:T(8,128)(2,1)S(1)}, u32[]{:S(2)}, u32[]{:S(2)}) collective-permute-start(bf16[96,768]{1,0:T(8,128)(2,1)S(1)} %add_convert_fusion.18), channel_id=1, source_target_pairs={{0,16},{4,20},{8,24},{12,28},{16,0},{20,4},{24,8},{28,12},{1,17},{... | collective-permute-start | bytes 442376 | tf_op jit(solution)/shard_map/ppermute | solution.py:428
  557.5 7.3 %collective-permute-start.23 = (bf16[96,768]{1,0:T(8,128)(2,1)S(1)}, bf16[96,768]{1,0:T(8,128)(2,1)S(1)}, u32[]{:S(2)}, u32[]{:S(2)}) collective-permute-start(bf16[96,768]{1,0:T(8,128)(2,1)S(1)} %add_convert_fusion.19), channel_id=1, source_target_pairs={{0,16},{4,20},{8,24},{12,28},{16,0},{20,4},{24,8},{28,12},{1,17},{... | collective-permute-start | bytes 442376 | tf_op jit(solution)/shard_map/ppermute | solution.py:428
  571.6 9.8 %collective-permute-start.24 = (bf16[192,768]{1,0:T(8,128)(2,1)S(1)}, bf16[192,768]{1,0:T(8,128)(2,1)S(1)}, u32[]{:S(2)}, u32[]{:S(2)}) collective-permute-start(bf16[192,768]{1,0:T(8,128)(2,1)S(1)} %pad_maximum_fusion.14), channel_id=1, source_target_pairs={{0,8},{4,12},{8,0},{12,4},{16,24},{20,28},{24,16},{28,20},{1,9},{5... | collective-permute-start | bytes 884744 | tf_op jit(solution)/shard_map/ppermute | solution.py:428
  571.8 10.0 %collective-permute-start.19 = (bf16[2,256,192]{2,1,0:T(8,128)(2,1)S(1)}, bf16[2,256,192]{2,1,0:T(8,128)(2,1)S(1)}, u32[]{:S(2)}, u32[]{:S(2)}) collective-permute-start(bf16[2,256,192]{2,1,0:T(8,128)(2,1)S(1)} %copy-done.12), channel_id=1, source_target_pairs={{0,1},{1,0},{2,3},{3,2},{4,5},{5,4},{6,7},{7,6},{8,9},{9,8},{10,11... | collective-permute-start | bytes 589832 | tf_op jit(solution)/shard_map/ppermute | solution.py:428
  581.4 9.9 %collective-permute-start.31 = (bf16[384,768]{1,0:T(8,128)(2,1)S(1)}, bf16[384,768]{1,0:T(8,128)(2,1)S(1)}, u32[]{:S(2)}, u32[]{:S(2)}) collective-permute-start(bf16[384,768]{1,0:T(8,128)(2,1)S(1)} %pad_maximum_fusion.10), channel_id=1, source_target_pairs={{0,8},{4,12},{8,0},{12,4},{16,24},{20,28},{24,16},{28,20},{1,9},{5... | collective-permute-start | bytes 1769480 | tf_op jit(solution)/shard_map/ppermute | solution.py:428
  581.6 9.9 %collective-permute-start.25 = (bf16[384,768]{1,0:T(8,128)(2,1)S(1)}, bf16[384,768]{1,0:T(8,128)(2,1)S(1)}, u32[]{:S(2)}, u32[]{:S(2)}) collective-permute-start(bf16[384,768]{1,0:T(8,128)(2,1)S(1)} %pad_maximum_fusion.9), channel_id=1, source_target_pairs={{0,4},{4,0},{8,12},{12,8},{16,20},{20,16},{24,28},{28,24},{1,5},{5... | collective-permute-start | bytes 1769480 | tf_op jit(solution)/shard_map/ppermute | solution.py:428
  612.3 16.2 %collective-permute-start.53 = (bf16[448,768]{1,0:T(8,128)(2,1)}, bf16[448,768]{1,0:T(8,128)(2,1)}, u32[]{:S(2)}, u32[]{:S(2)}) collective-permute-start(bf16[448,768]{1,0:T(8,128)(2,1)} %get-tuple-element.246), channel_id=1, source_target_pairs={{0,4},{4,0},{8,12},{12,8},{16,20},{20,16},{24,28},{28,24},{1,5},{5... | collective-permute-start | bytes 2064392 | tf_op jit(solution)/shard_map/ppermute | solution.py:428
  612.4 16.2 %collective-permute-start.47 = (bf16[448,768]{1,0:T(8,128)(2,1)S(1)}, bf16[448,768]{1,0:T(8,128)(2,1)}, u32[]{:S(2)}, u32[]{:S(2)}) collective-permute-start(bf16[448,768]{1,0:T(8,128)(2,1)S(1)} %get-tuple-element.247), channel_id=1, source_target_pairs={{0,8},{4,12},{8,0},{12,4},{16,24},{20,28},{24,16},{28,20},{1,9},{5... | collective-permute-start | bytes 2064392 | tf_op jit(solution)/shard_map/ppermute | solution.py:428
  631.4 10.1 %collective-permute-start.48 = (bf16[224,768]{1,0:T(8,128)(2,1)S(1)}, bf16[224,768]{1,0:T(8,128)(2,1)S(1)}, u32[]{:S(2)}, u32[]{:S(2)}) collective-permute-start(bf16[224,768]{1,0:T(8,128)(2,1)S(1)} %broadcast_select_fusion.23), channel_id=1, source_target_pairs={{0,4},{4,0},{8,12},{12,8},{16,20},{20,16},{24,28},{28,24},{1,5},{5... | collective-permute-start | bytes 1032200 | tf_op jit(solution)/shard_map/ppermute | solution.py:428
  633.5 9.6 %collective-permute-start.54 = (bf16[224,768]{1,0:T(8,128)(2,1)S(1)}, bf16[224,768]{1,0:T(8,128)(2,1)S(1)}, u32[]{:S(2)}, u32[]{:S(2)}) collective-permute-start(bf16[224,768]{1,0:T(8,128)(2,1)S(1)} %broadcast_select_fusion.20), channel_id=1, source_target_pairs={{0,8},{4,12},{8,0},{12,4},{16,24},{20,28},{24,16},{28,20},{1,9},{5... | collective-permute-start | bytes 1032200 | tf_op jit(solution)/shard_map/ppermute | solution.py:428
  641.7 13.4 %collective-permute-start.49 = (bf16[112,768]{1,0:T(8,128)(2,1)S(1)}, bf16[112,768]{1,0:T(8,128)(2,1)S(1)}, u32[]{:S(2)}, u32[]{:S(2)}) collective-permute-start(bf16[112,768]{1,0:T(8,128)(2,1)S(1)} %broadcast_select_fusion.63), channel_id=1, source_target_pairs={{0,16},{4,20},{8,24},{12,28},{16,0},{20,4},{24,8},{28,12},{1,17},{... | collective-permute-start | bytes 516104 | tf_op jit(solution)/shard_map/ppermute | solution.py:428
  643.2 19.2 %collective-permute-start.55 = (bf16[112,768]{1,0:T(8,128)(2,1)S(1)}, bf16[112,768]{1,0:T(8,128)(2,1)S(1)}, u32[]{:S(2)}, u32[]{:S(2)}) collective-permute-start(bf16[112,768]{1,0:T(8,128)(2,1)S(1)} %broadcast_select_fusion.60), channel_id=1, source_target_pairs={{0,16},{4,20},{8,24},{12,28},{16,0},{20,4},{24,8},{28,12},{1,17},{... | collective-permute-start | bytes 516104 | tf_op jit(solution)/shard_map/ppermute | solution.py:428
  655.1 14.7 %collective-permute-start.50 = (bf16[112,768]{1,0:T(8,128)(2,1)S(1)}, bf16[112,768]{1,0:T(8,128)(2,1)S(1)}, u32[]{:S(2)}, u32[]{:S(2)}) collective-permute-start(bf16[112,768]{1,0:T(8,128)(2,1)S(1)} %add_convert_fusion.15), channel_id=1, source_target_pairs={{0,16},{4,20},{8,24},{12,28},{16,0},{20,4},{24,8},{28,12},{1,17},{... | collective-permute-start | bytes 516104 | tf_op jit(solution)/shard_map/ppermute | solution.py:428
  662.5 10.9 %collective-permute-start.56 = (bf16[112,768]{1,0:T(8,128)(2,1)S(1)}, bf16[112,768]{1,0:T(8,128)(2,1)S(1)}, u32[]{:S(2)}, u32[]{:S(2)}) collective-permute-start(bf16[112,768]{1,0:T(8,128)(2,1)S(1)} %add_convert_fusion.14), channel_id=1, source_target_pairs={{0,16},{4,20},{8,24},{12,28},{16,0},{20,4},{24,8},{28,12},{1,17},{... | collective-permute-start | bytes 516104 | tf_op jit(solution)/shard_map/ppermute | solution.py:428
  669.9 10.0 %collective-permute-start.51 = (bf16[224,768]{1,0:T(8,128)(2,1)S(1)}, bf16[224,768]{1,0:T(8,128)(2,1)S(1)}, u32[]{:S(2)}, u32[]{:S(2)}) collective-permute-start(bf16[224,768]{1,0:T(8,128)(2,1)S(1)} %pad_maximum_fusion.11), channel_id=1, source_target_pairs={{0,4},{4,0},{8,12},{12,8},{16,20},{20,16},{24,28},{28,24},{1,5},{5... | collective-permute-start | bytes 1032200 | tf_op jit(solution)/shard_map/ppermute | solution.py:428
  673.5 10.8 %collective-permute-start.57 = (bf16[224,768]{1,0:T(8,128)(2,1)S(1)}, bf16[224,768]{1,0:T(8,128)(2,1)S(1)}, u32[]{:S(2)}, u32[]{:S(2)}) collective-permute-start(bf16[224,768]{1,0:T(8,128)(2,1)S(1)} %pad_maximum_fusion.12), channel_id=1, source_target_pairs={{0,8},{4,12},{8,0},{12,4},{16,24},{20,28},{24,16},{28,20},{1,9},{5... | collective-permute-start | bytes 1032200 | tf_op jit(solution)/shard_map/ppermute | solution.py:428
  680.8 22.9 %collective-permute-start.52 = (bf16[448,768]{1,0:T(8,128)(2,1)}, bf16[448,768]{1,0:T(8,128)(2,1)}, u32[]{:S(2)}, u32[]{:S(2)}) collective-permute-start(bf16[448,768]{1,0:T(8,128)(2,1)} %pad_maximum_fusion.7), channel_id=1, source_target_pairs={{0,8},{4,12},{8,0},{12,4},{16,24},{20,28},{24,16},{28,20},{1,9},{5... | collective-permute-start | bytes 2064392 | tf_op jit(solution)/shard_map/ppermute | solution.py:428
  686.0 19.9 %collective-permute-start.58 = (bf16[448,768]{1,0:T(8,128)(2,1)}, bf16[448,768]{1,0:T(8,128)(2,1)}, u32[]{:S(2)}, u32[]{:S(2)}) collective-permute-start(bf16[448,768]{1,0:T(8,128)(2,1)} %pad_maximum_fusion.8), channel_id=1, source_target_pairs={{0,4},{4,0},{8,12},{12,8},{16,20},{20,16},{24,28},{28,24},{1,5},{5... | collective-permute-start | bytes 2064392 | tf_op jit(solution)/shard_map/ppermute | solution.py:428
  (54 other events, 893.6 us)

commit v2 on v1

v2 whole, which is shorter than its diff:
```python
import jax, jax.numpy as jnp
from jax import lax
from jax.sharding import PartitionSpec as P
from jax.experimental import pallas as pl
from jax.experimental.pallas import tpu as pltpu
F32=jnp.float32; BF=jnp.bfloat16
CH=48; PH=4; LW=PH*CH
NJ=33; SEGL=48; XROWS=(SEGL+NJ-1)*16; MROWS=SEGL*16
VM=60*1024*1024

def cost(us):
    return pl.CostEstimate(flops=int(us*1.0e9),bytes_accessed=int(us*3.0e6),transcendentals=0)

ANY=pl.BlockSpec(memory_space=pl.ANY)
PW=2*LW

def skip(kernel,at,count):
    if not count:
        return kernel
    return lambda *refs: kernel(*refs[:at],*refs[at+count:])

def dot(a,b): return jnp.dot(a,b,preferred_element_type=F32)
def dot_nt(a,b): return lax.dot_general(a,b,(((1,),(1,)),((),())),preferred_element_type=F32)
def dot_tn(a,b): return lax.dot_general(a,b,(((0,),(0,)),((),())),preferred_element_type=F32)

def erf_gelu_parts(v):
    phi=0.5*(1.0+lax.erf(v*0.7071067811865476))
    return phi

WROWS=6400
def build_w_kernel(t_ref, w_ref, tp, rs):
    g=pl.program_id(0)
    rows=t_ref.shape[0]
    @pl.when(g==0)
    def _():
        tp[0:144,:]=jnp.zeros((144,LW),BF)
        tp[144:144+rows,:]=t_ref[...]
        tp[144+rows:,:]=jnp.zeros((256,LW),BF)
    src=lax.broadcasted_iota(jnp.int32,(LW,256),0); l=lax.broadcasted_iota(jnp.int32,(LW,256),1)
    pick=((src==48*g+lax.rem(l,48))&(l<LW)).astype(F32).astype(BF)
    n=640
    lane=lax.broadcasted_iota(jnp.int32,(n,256),1)
    for i in range(WROWS//n):
        r0=i*n
        R=dot(tp[r0:r0+n+144,:],pick).astype(BF)
        lo=jnp.where(lane[:,:128]<96,jnp.where(lane[:,:128]<48,R[144:144+n,:128],R[96:96+n,:128]),R[48:48+n,:128])
        hi=jnp.where(lane[:,128:]<144,R[48:48+n,128:],R[0:n,128:])
        w_ref[0,r0:r0+n,:128]=lo
        w_ref[0,r0:r0+n,128:]=hi

def build_w(taps2):
    rows=taps2.shape[0]
    return pl.pallas_call(build_w_kernel,grid=(4,),
        in_specs=[pl.BlockSpec((rows,LW),lambda g:(0,0))],
        out_specs=pl.BlockSpec((1,WROWS,256),lambda g:(g,0,0)),
        out_shape=jax.ShapeDtypeStruct((4,WROWS,256),BF),
        scratch_shapes=[pltpu.VMEM((rows+144+256,LW),BF),pltpu.VMEM((640+144,256),BF)],
        cost_estimate=cost(10),
        compiler_params=pltpu.CompilerParams(vmem_limit_bytes=VM))(taps2)

def sload(ref,start,n,stride):
    return jnp.concatenate([ref[0,pl.ds(start,n,stride=stride),:],ref[1,pl.ds(start,n,stride=stride),:]],axis=1)[:,:LW]
def sstore(ref,start,n,stride,v):
    ref[0,pl.ds(start,n,stride=stride),:]=v[:,:128]
    ref[1,pl.ds(start,n,stride=stride),:]=jnp.concatenate([v[:,128:],jnp.zeros((n,64),v.dtype)],axis=1)
def fload(ref,start,n):
    return jnp.concatenate([ref[0,pl.ds(start,n),:],ref[1,pl.ds(start,n),:]],axis=1)[:,:LW]
def fstore(ref,start,n,v):
    ref[0,pl.ds(start,n),:]=v[:,:128]
    ref[1,pl.ds(start,n),:]=jnp.concatenate([v[:,128:],jnp.zeros((n,64),v.dtype)],axis=1)

def pick_matrix(g,a):
    ch=lax.broadcasted_iota(jnp.int32,(LW,LW),0); l=lax.broadcasted_iota(jnp.int32,(LW,LW),1)
    return ((ch==48*g+(l-48*a))&(l>=48*a)&(l<48*a+48)).astype(F32).astype(BF)

def lane_times():
    sub=lax.broadcasted_iota(jnp.int32,(16,LW),0); l=lax.broadcasted_iota(jnp.int32,(16,LW),1)
    a=(l>=48).astype(jnp.int32)+(l>=96).astype(jnp.int32)+(l>=144).astype(jnp.int32)
    return 4*sub+a

def bounds(seg_ref,r,q):
    lo=seg_ref[r,q-1] if q>0 else 0
    return lo,seg_ref[r,q]

def respace(seg_ref,pair,src,xr,xsf):
    xsf[0,1280:1296,:]=jnp.zeros((16,128),F32); xsf[1,1280:1296,:]=jnp.zeros((16,128),F32)
    tin=lane_times()
    for r in range(2):
        bl=[bounds(seg_ref,pair*2+r,q) for q in range(8)]
        for B in range(26):
            v=jnp.zeros((16,LW),F32)
            for q in range(8):
                bb=B-1-q
                if 0<=bb<16:
                    t=tin+64*bb
                    v=jnp.where((t>=bl[q][0])&(t<bl[q][1]),src[pl.ds(r*256+16*bb,16),:],v)
            xr[r,pl.ds(16*B,16),:]=v
        for sp in range(8):
            sstore(xsf,r*8+sp,80,16,xr[r,pl.ds(48*sp,80),:])

def unspace(seg_ref,pair,acc,yr,emit):
    tin=lane_times()
    for r in range(2):
        bl=[bounds(seg_ref,pair*2+r,q) for q in range(8)]
        for sp in range(8):
            yr[r,pl.ds(48*sp,48),:]=sload(acc,r*8+sp,48,16)
        for bb in range(16):
            v=jnp.zeros((16,LW),F32)
            t=tin+64*bb
            for q in range(8):
                v=jnp.where((t>=bl[q][0])&(t<bl[q][1]),yr[r,pl.ds(16*(bb+q),16),:],v)
            emit(r*256+16*bb,v)

def conv_fwd_kernel(seg_ref,idx_ref,x0_ref,x1_ref,x2_ref,x3_ref,w_ref,bias_ref,first_ref,pre_ref,xs_ref,xt,xa,x4,xr,xsf,acc,yr,facc,accv,pk):
    pair=pl.program_id(0); g=pl.program_id(1)
    @pl.when(g==0)
    def _():
        for m,x_ref in enumerate((x0_ref,x1_ref,x2_ref,x3_ref)):
            k=pl.multiple_of((idx_ref[0]^m)*256,256)
            for r in range(2):
                fstore(xt,r*1024+k,256,x_ref[...].astype(F32)[:,LW*r:LW*r+LW])
        for a in range(4):
            xa[a]=sload(xt,a,512,4).astype(BF)
    v=dot(xa[0],pick_matrix(g,0))
    for a in range(1,4):
        v=v+dot(xa[a],pick_matrix(g,a))
    x4[...]=v
    respace(seg_ref,pair,x4,xr,xsf)
    n=XROWS
    zt=jnp.zeros((n+16,64),F32)
    va=xsf[0,0:n+16,:]; vb=xsf[1,0:n+16,:]
    z0=jnp.concatenate([zt,va[:,:64]],axis=1); z1=jnp.concatenate([va[:,64:],vb[:,:64]],axis=1)
    pk[n:n+32,:]=jnp.zeros((32,384),BF)
    pk[0:n,0:128]=va[0:n].astype(BF)
    pk[0:n,128:256]=(vb[0:n]+z0[16:]).astype(BF)
    pk[0:n,256:384]=z1[16:].astype(BF)
    xs_ref[0,0,:,0:384]=pk[0:n]
    xs_ref[0,0,:,384:768]=pk[32:32+n]
    s=dot(xs_ref[0,0,512:512+MROWS,0:256],w_ref[0,6144:6400,:])
    for J in range(8):
        s=s+dot(xs_ref[0,0,64*J:64*J+MROWS,:],w_ref[0,768*J:768*J+768,:])
    accv[...]=s
    bias=bias_ref[0]
    def emit(row,v):
        pre_ref[0,0,pl.ds(row,16),:]=v+bias
    acc[0]=accv[:,:128]; acc[1]=accv[:,128:]
    unspace(seg_ref,pair,acc,yr,emit)
    pre=pre_ref[0,0]
    fs=(x4[...]+pre*erf_gelu_parts(pre)).astype(BF)
    for a in range(4):
        f=dot_nt(fs,pick_matrix(g,a))
        @pl.when(g==0)
        def _(): facc[a]=f
        @pl.when(g>0)
        def _(): facc[a]=facc[a]+f
    @pl.when(g==3)
    def _():
        for a in range(4):
            sstore(xt,a,512,4,facc[a])
        first_ref[...]=jnp.concatenate([fload(xt,0,1024),fload(xt,1024,1024)],axis=1).astype(BF)

def conv_fwd(ends,idx,xs4,w,bias4):
    pairs=xs4[0].shape[0]//256
    return pl.pallas_call(conv_fwd_kernel,grid=(pairs,4),
        in_specs=[pl.BlockSpec(memory_space=pltpu.SMEM)]*2+[pl.BlockSpec((256,PW),lambda p,g:(p,0))]*4+[
                  pl.BlockSpec((1,WROWS,256),lambda p,g:(g,0,0)),
                  pl.BlockSpec((1,1,LW),lambda p,g:(g,0,0))],
        out_specs=[pl.BlockSpec((1024,PW),lambda p,g:(p,0)),
                   pl.BlockSpec((1,1,512,LW),lambda p,g:(p,g,0,0)),
                   pl.BlockSpec((1,1,XROWS,768),lambda p,g:(p,g,0,0))],
        out_shape=[jax.ShapeDtypeStruct((pairs*1024,PW),BF),
                   jax.ShapeDtypeStruct((pairs,4,512,LW),F32),
                   jax.ShapeDtypeStruct((pairs,4,XROWS,768),BF)],
        scratch_shapes=[pltpu.VMEM((2,2048,128),F32),pltpu.VMEM((4,512,LW),BF),pltpu.VMEM((512,LW),F32),
            pltpu.VMEM((2,416,LW),F32),pltpu.VMEM((2,XROWS+16,128),F32),pltpu.VMEM((2,MROWS,128),F32),pltpu.VMEM((2,384,LW),F32),
            pltpu.VMEM((4,512,LW),F32),pltpu.VMEM((MROWS,256),F32),pltpu.VMEM((XROWS+32,384),BF)],
        cost_estimate=cost(35),
        compiler_params=pltpu.CompilerParams(vmem_limit_bytes=VM))(ends,idx,*xs4,w,bias4)

def tap_kernel(seg_ref,e0_ref,e1_ref,first_ref,stat_ref,mom_ref,gain_ref,pre_ref,xs_ref,qkv_ref,tap_ref,ds_ref,d4_ref,bias_ref,vec_ref,xt,xa,dc,xr,xsf,A):
    pair=pl.program_id(0); g=pl.program_id(1)
    @pl.when(g==0)
    def _():
        gain=gain_ref[...]
        sg=jnp.zeros((1,LW),F32); sh=jnp.zeros((1,LW),F32)
        for t in range(8):
            r,k=t//4,t%4
            rows=slice(256*k,256*k+256); cols=slice(LW*r,LW*r+LW)
            e=(e0_ref[rows]+e1_ref[rows].astype(F32))[:,cols]
            st=stat_ref[256*t:256*t+256]
            mean=st[:,0:1]; rstd=st[:,1:2]
            mom=jnp.concatenate([mom_ref[t],jnp.zeros((120,256),F32)],axis=0).T*(1.0/768)
            xhat=(first_ref[rows].astype(F32)[:,cols]-mean)*rstd
            sg=sg+jnp.sum(e*xhat,axis=0,keepdims=True); sh=sh+jnp.sum(e,axis=0,keepdims=True)
            fstore(xt,256*t,256,rstd*(e*gain-mom[:,0:1]-xhat*mom[:,1:2]))
        vec_ref[0,0:1]=sg; vec_ref[0,1:2]=sh; vec_ref[0,2:8]=jnp.zeros((6,LW),F32)
        for a in range(4):
            xa[a]=sload(xt,a,512,4).astype(BF)
    v=dot(xa[0],pick_matrix(g,0))
    for a in range(1,4):
        v=v+dot(xa[a],pick_matrix(g,a))
    d4_ref[0,0]=v.astype(BF)
    pre=pre_ref[0,0]
    cdf=erf_gelu_parts(pre)
    slope=cdf+pre*(jnp.exp(-0.5*pre*pre)*0.3989422804014327)
    d=v*slope
    dc[...]=d
    bias_ref[0,0]=jnp.sum(d,axis=0,keepdims=True)
    respace(seg_ref,pair,dc,xr,xsf)
    ds_ref[0,0,:,0:128]=xsf[0,0:XROWS].astype(BF); ds_ref[0,0,:,128:256]=xsf[1,0:XROWS].astype(BF)
    DT=fload(xsf,256,MROWS).astype(BF).T
    for J in range(8):
        A[:,768*J:768*J+768]=dot(DT,xs_ref[0,0,64*J:64*J+MROWS,:])
    A[:,6144:6400]=dot(DT,xs_ref[0,0,512:512+MROWS,0:256])
    n=6144
    o=A[0:48,0:n]
    for b in range(1,4):
        o=o+A[48*b:48*b+48,48*b:48*b+n]
    for J in range(8):
        tap_ref[0,J]=o[:,768*J:768*J+768].astype(BF)
    tap_ref[0,8:11]=jnp.where(pair==0,qkv_ref[...],jnp.zeros((3,48,768),BF))

def tap_grads(ends,e0,e1,first,stat,mom,gain,pre,xs,g_qkv,deps=()):
    pairs=e0.shape[0]//1024
    return pl.pallas_call(skip(tap_kernel,10,len(deps)),grid=(pairs,4),
        in_specs=[pl.BlockSpec(memory_space=pltpu.SMEM),
                  pl.BlockSpec((1024,PW),lambda p,g:(p,0)),
                  pl.BlockSpec((1024,PW),lambda p,g:(p,0)),
                  pl.BlockSpec((1024,PW),lambda p,g:(p,0)),
                  pl.BlockSpec((2048,128),lambda p,g:(p,0)),
                  pl.BlockSpec((8,8,256),lambda p,g:(p,0,0)),
                  pl.BlockSpec((1,LW),lambda p,g:(0,0)),
                  pl.BlockSpec((1,1,512,LW),lambda p,g:(p,g,0,0)),
                  pl.BlockSpec((1,1,XROWS,768),lambda p,g:(p,g,0,0)),
                  pl.BlockSpec((3,48,768),lambda p,g:(0,g,0))]+[ANY]*len(deps),
        out_specs=[pl.BlockSpec((1,11,48,768),lambda p,g:(p,0,g,0)),
                   pl.BlockSpec((1,1,XROWS,256),lambda p,g:(p,g,0,0)),
                   pl.BlockSpec((1,1,512,LW),lambda p,g:(p,g,0,0)),
                   pl.BlockSpec((1,1,1,LW),lambda p,g:(p,g,0,0)),
                   pl.BlockSpec((1,8,LW),lambda p,g:(p,0,0))],
        out_shape=[jax.ShapeDtypeStruct((pairs,11,LW,768),BF),
                   jax.ShapeDtypeStruct((pairs,4,XROWS,256),BF),
                   jax.ShapeDtypeStruct((pairs,4,512,LW),BF),
                   jax.ShapeDtypeStruct((pairs,4,1,LW),F32),jax.ShapeDtypeStruct((pairs,8,LW),F32)],
        scratch_shapes=[pltpu.VMEM((2,2048,128),F32),pltpu.VMEM((4,512,LW),BF),pltpu.VMEM((512,LW),F32),
            pltpu.VMEM((2,416,LW),F32),pltpu.VMEM((2,XROWS+16,128),F32),pltpu.VMEM((LW,6400),F32)],
        cost_estimate=cost(24),
        compiler_params=pltpu.CompilerParams(vmem_limit_bytes=VM))(ends,e0,e1,first,stat,mom,gain,pre,xs,g_qkv,*deps)

def back_kernel(at,seg_ref,idx_ref,ds_ref,d4_ref,w_ref,*rest):
    if at:
        part_ref,out_ref,xt,acc,yr,fs,accv=rest
    else:
        facc,acc,yr,fs,accv=rest
    pair=pl.program_id(0); i=pl.program_id(1); g=i+at
    s=None
    for j in range(NJ):
        p=dot_nt(ds_ref[0,0,16*(NJ-1-j):16*(NJ-1-j)+MROWS,:],w_ref[0,LW*j:LW*j+256,:])
        s=p if s is None else s+p
    accv[...]=s
    def emit(row,v):
        fs[pl.ds(row,16),:]=(v+d4_ref[0,0,pl.ds(row,16),:].astype(F32)).astype(BF)
    acc[0]=accv[:,:128]; acc[1]=accv[:,128:]
    unspace(seg_ref,pair,acc,yr,emit)
    if at:
        for a in range(4):
            f=dot_nt(fs[...],pick_matrix(g,a))
            @pl.when(i==0)
            def _(): sstore(xt,a,512,4,f+part_ref[0,a])
            @pl.when(i>0)
            def _(): sstore(xt,a,512,4,f+sload(xt,a,512,4))
        @pl.when(i==1)
        def _():
            for k in range(4):
                out_ref[idx_ref[0]^k]=jnp.concatenate([fload(xt,k*256,256),fload(xt,1024+k*256,256)],axis=1).astype(BF)
    else:
        for a in range(4):
            f=dot_nt(fs[...],pick_matrix(g,a))
            @pl.when(i==0)
            def _(): facc[0,a]=f
            @pl.when(i>0)
            def _(): facc[0,a]=facc[0,a]+f

def conv_back(at,ends,idx,ds,d4,w,part=None,deps=()):
    pairs=ds.shape[0]
    parts=() if part is None else (part,)
    facc=pl.BlockSpec((1,4,512,LW),lambda p,g:(p,0,0,0))
    scratch=[pltpu.VMEM((2,2048,128),F32)] if at else []
    return pl.pallas_call(skip(lambda *refs: back_kernel(at,*refs),5+len(parts),len(deps)),grid=(pairs,2),
        in_specs=[pl.BlockSpec(memory_space=pltpu.SMEM),pl.BlockSpec(memory_space=pltpu.SMEM),
                  pl.BlockSpec((1,1,XROWS,256),lambda p,g:(p,g+at,0,0)),
                  pl.BlockSpec((1,1,512,LW),lambda p,g:(p,g+at,0,0)),
                  pl.BlockSpec((1,WROWS,256),lambda p,g:(g+at,0,0))]+[facc]*len(parts)+[ANY]*len(deps),
        out_specs=pl.BlockSpec((4,256,PW),lambda p,g:(0,p,0)) if at else facc,
        out_shape=jax.ShapeDtypeStruct((4,pairs*256,PW),BF) if at else jax.ShapeDtypeStruct((pairs,4,512,LW),F32),
        scratch_shapes=scratch+[pltpu.VMEM((2,MROWS,128),F32),pltpu.VMEM((2,384,LW),F32),
            pltpu.VMEM((512,LW),BF),pltpu.VMEM((MROWS,256),F32)],
        cost_estimate=cost(15),
        compiler_params=pltpu.CompilerParams(vmem_limit_bytes=VM))(ends,idx,ds,d4,w,*parts,*deps)


def qkv_kernel(f0,f1,f2,f3,w_ref,bias_ref,gain_ref,shift_ref,q_ref,k_ref,v_ref,ml_ref,stat_ref):
    fs=[f[...].astype(F32) for f in (f0,f1,f2,f3)]
    fs=[jnp.concatenate([f[:,:LW],f[:,LW:]],axis=0) for f in fs]
    mean=sum(jnp.sum(f,axis=1,keepdims=True) for f in fs)*(1.0/768)
    cs=[f-mean for f in fs]
    var=sum(jnp.sum(c*c,axis=1,keepdims=True) for c in cs)*(1.0/768)
    rstd=lax.rsqrt(var+1e-5)
    n=mean.shape[0]
    pad=jnp.zeros((n,64),BF)
    out=None
    for m in range(4):
        ml=(cs[m]*rstd*gain_ref[m]+shift_ref[m]).astype(BF)
        ml_ref[m]=ml.reshape(2,256,LW)
        p=dot(jnp.concatenate([ml,pad],axis=1),w_ref[m])
        out=p if out is None else out+p
    out=(out+bias_ref[...]).astype(BF)
    out=out.reshape(2,256,768)
    q_ref[...]=out[:,:,0:192]; k_ref[...]=out[:,:,256:448]; v_ref[...]=out[:,:,512:704]
    lane=lax.broadcasted_iota(jnp.int32,(n,128),1)
    stat_ref[...]=jnp.where(lane==0,mean,jnp.where(lane==1,rstd,0.0)).reshape(2,256,128)

def qkv(fs,w,bias,gain,shift):
    pairs=fs[0].shape[0]//1024; R=2*pairs
    row=pl.BlockSpec((2,256,LW),lambda p,k:(p,k,0))
    full=lambda a: pl.BlockSpec(a.shape,lambda p,k:(0,)*a.ndim)
    return pl.pallas_call(qkv_kernel,grid=(pairs,4),
        in_specs=[pl.BlockSpec((256,PW),lambda p,k:(4*p+k,0))]*4+[full(w),full(bias),full(gain),full(shift)],
        out_specs=[row]*3+[pl.BlockSpec((4,2,256,LW),lambda p,k:(0,p,k,0)),pl.BlockSpec((2,256,128),lambda p,k:(p,k,0))],
        out_shape=[jax.ShapeDtypeStruct((R,1024,LW),BF)]*3+[jax.ShapeDtypeStruct((4,R,1024,LW),BF),jax.ShapeDtypeStruct((R,1024,128),F32)],
        cost_estimate=cost(10),
        compiler_params=pltpu.CompilerParams(vmem_limit_bytes=VM))(*fs,w,bias,gain,shift)

def seg_vec(seg_ref,r,shape,axis,start):
    t=lax.broadcasted_iota(jnp.int32,shape,axis)+start
    v=jnp.zeros(shape,jnp.int32)
    for i in range(8):
        v=v+(t>=seg_ref[r,i]).astype(jnp.int32)
    return v

def attn_kernel(idx_ref,seg_ref,q_ref,k_ref,v_ref,o_ref,of_ref,lse_ref):
    pair=pl.program_id(0); kb=pl.program_id(1)
    for r in range(2):
        sq=seg_vec(seg_ref,2*pair+r,(256,1),0,kb*256); sk=seg_vec(seg_ref,2*pair+r,(1,1024),1,0)
        same=sq==sk
        outs=[]; rows=[]
        for h in range(3):
            c=slice(64*h,64*h+64)
            s=jnp.where(same,dot_nt(q_ref[r,:,c],k_ref[r,:,c]),-1e30)
            mx=jnp.max(s,axis=1,keepdims=True)
            p=jnp.exp(s-mx)
            tot=jnp.sum(p,axis=1,keepdims=True)
            outs.append(dot(p.astype(BF),v_ref[r,:,c])/tot)
            rows.append(jnp.broadcast_to(mx+jnp.log(tot),(256,128)).T[0:1,:])
        o=jnp.concatenate(outs,axis=1)
        of_ref[r]=o
        o_ref[0,:,LW*r:LW*r+LW]=o.astype(BF)
        lse_ref[r,0]=jnp.concatenate(rows+[jnp.zeros((5,256),F32)],axis=0)

def attn(idx,ends,q,k,v):
    R=ends.shape[0]; pairs=R//2
    blk=pl.BlockSpec((2,256,LW),lambda p,b,i,s:(p,b,0)); full=pl.BlockSpec((2,1024,LW),lambda p,b,i,s:(p,0,0))
    return pl.pallas_call(attn_kernel,
        grid_spec=pltpu.PrefetchScalarGridSpec(num_scalar_prefetch=2,grid=(pairs,4),
        in_specs=[blk,full,full],
        out_specs=[pl.BlockSpec((1,256,PW),lambda p,b,i,s:(b^i[0],p,0)),blk,pl.BlockSpec((2,1,8,256),lambda p,b,i,s:(p,b,0,0))]),
        out_shape=[jax.ShapeDtypeStruct((4,pairs*256,PW),BF),jax.ShapeDtypeStruct((R,1024,LW),F32),jax.ShapeDtypeStruct((R,4,8,256),F32)],
        cost_estimate=cost(18),
        compiler_params=pltpu.CompilerParams(vmem_limit_bytes=VM))(idx,ends,q,k,v)

def attn_bwd_kernel(r,idx_ref,seg_ref,q_ref,k_ref,v_ref,o_ref,d0,d1,d2,d3,lse_ref,dq_ref,dk_ref,dv_ref,dks,dvs):
    pair=pl.program_id(0); kb=pl.program_id(1)
    m=kb^idx_ref[0]
    mine=slice(LW*r,LW*r+LW)
    dod=jnp.where(m<2,jnp.where(m==0,d0[...],d1[...]),jnp.where(m==2,d2[...],d3[...])).astype(F32)[:,mine].astype(BF)
    @pl.when(kb==0)
    def _():
        dks[...]=jnp.zeros_like(dks); dvs[...]=jnp.zeros_like(dvs)
    sq=seg_vec(seg_ref,2*pair+r,(1,256),1,kb*256); sk=seg_vec(seg_ref,2*pair+r,(1024,1),0,0)
    same=sk==sq
    dqs=[]; ks=[]; vs=[]
    for h in range(3):
        c=slice(64*h,64*h+64)
        q=q_ref[0,:,c]; k=k_ref[0,:,c]; do=dod[:,c]
        delta=jnp.sum(do.astype(F32)*o_ref[0,:,c],axis=1,keepdims=True)
        delta=jnp.broadcast_to(delta,(256,128)).T[0:1,:]
        st=jnp.where(same,dot_nt(k,q)-lse_ref[0,0,h:h+1,:],-1e30)
        p=jnp.exp(st)
        dp=dot_nt(v_ref[0,:,c],do)
        ds=(p*(dp-delta)).astype(BF)
        vs.append(dot(p.astype(BF),do)); ks.append(dot(ds,q)); dqs.append(dot_tn(ds,k))
    dks[...]+=jnp.concatenate(ks,axis=1); dvs[...]+=jnp.concatenate(vs,axis=1)
    dq_ref[0]=jnp.concatenate(dqs,axis=1).astype(BF)
    @pl.when(kb==3)
    def _():
        dk_ref[0]=dks[...].astype(BF); dv_ref[0]=dvs[...].astype(BF)

def attn_bwd(r,idx,ends,q,k,v,o,dos,lse,deps=()):
    pairs=ends.shape[0]//2
    blk=pl.BlockSpec((1,256,LW),lambda p,b,i,s:(2*p+r,b,0)); full=pl.BlockSpec((1,1024,LW),lambda p,b,i,s:(2*p+r,0,0))
    out=pl.BlockSpec((1,256,LW),lambda p,b,i,s:(p,b,0)); outs=pl.BlockSpec((1,1024,LW),lambda p,b,i,s:(p,0,0))
    return pl.pallas_call(skip(lambda *refs: attn_bwd_kernel(r,*refs),11,len(deps)),
        grid_spec=pltpu.PrefetchScalarGridSpec(num_scalar_prefetch=2,grid=(pairs,4),
        in_specs=[blk,full,full,blk]+[pl.BlockSpec((256,PW),lambda p,b,i,s:(p,0))]*4+[pl.BlockSpec((1,1,8,256),lambda p,b,i,s:(2*p+r,b,0,0))]+[ANY]*len(deps),
        out_specs=[out,outs,outs],scratch_shapes=[pltpu.VMEM((1024,LW),F32)]*2),
        out_shape=[jax.ShapeDtypeStruct((pairs,1024,LW),BF)]*3,
        cost_estimate=cost(60),
        compiler_params=pltpu.CompilerParams(vmem_limit_bytes=VM))(idx,ends,q,k,v,o,*dos,lse,*deps)

def pad3(a,b,c):
    z=jnp.zeros((a.shape[0],64),BF)
    return jnp.concatenate([a,z,b,z,c,z],axis=1)

def dmix_kernel(idx_ref,q0,k0,v0,q1,k1,v1,w_ref,sec_ref,f0,f1,f2,f3,stat_ref,gain_ref,keep_ref,send_ref,mom_ref):
    kb=pl.program_id(1)
    flat=lambda x: x[...].reshape(512,x.shape[-1])
    d=jnp.concatenate([pad3(q0[0],k0[0],v0[0]),pad3(q1[0],k1[0],v1[0])],axis=0)
    st=flat(stat_ref); mean=st[:,0:1]; rstd=st[:,1:2]
    mine=(kb==idx_ref[0]).astype(F32)
    m1=None
    for m,f in enumerate((f0,f1,f2,f3)):
        part=dot_nt(d,w_ref[m])[:,:LW]
        part=part+mine*sec_ref[m].reshape(512,LW)
        both=jnp.concatenate([part[:256],part[256:]],axis=1)
        if m%2: send_ref[m//2]=both.astype(BF)
        else: keep_ref[m//2]=both
        eg=part*gain_ref[m]
        f=f[...].astype(F32)
        xh=(jnp.concatenate([f[:,:LW],f[:,LW:]],axis=0)-mean)*rstd
        a=jnp.sum(eg,axis=1,keepdims=True); b=jnp.sum(eg*xh,axis=1,keepdims=True)
        m1=(a,b) if m1 is None else (m1[0]+a,m1[1]+b)
    lane=lax.broadcasted_iota(jnp.int32,(512,128),1)
    t=jnp.where(lane==0,m1[0],jnp.where(lane==1,m1[1],0.0)).T[0:8,:]
    mom_ref[0,0]=t[:,:256]; mom_ref[1,0]=t[:,256:]

def dmix(idx,heads,w,sec,fs,stat,gain,deps=()):
    pairs=heads[0].shape[0]; R=2*pairs
    blk=pl.BlockSpec((1,256,LW),lambda p,b,i:(p,b,0))
    full=lambda a: pl.BlockSpec(a.shape,lambda p,b,i:(0,)*a.ndim)
    pack=pl.BlockSpec((2,256,PW),lambda p,b,i:(0,4*p+b,0))
    return pl.pallas_call(skip(dmix_kernel,15,len(deps)),
        grid_spec=pltpu.PrefetchScalarGridSpec(num_scalar_prefetch=1,grid=(pairs,4),
        in_specs=[blk]*6+[full(w),pl.BlockSpec((4,2,256,LW),lambda p,b,i:(0,p,0,0))]+[pl.BlockSpec((256,PW),lambda p,b,i:(4*p+b,0))]*4
            +[pl.BlockSpec((2,256,128),lambda p,b,i:(p,b,0)),full(gain)]+[ANY]*len(deps),
        out_specs=[pack,pack,pl.BlockSpec((2,1,8,256),lambda p,b,i:(p,b,0,0))]),
        out_shape=[jax.ShapeDtypeStruct((2,pairs*1024,PW),F32),jax.ShapeDtypeStruct((2,pairs*1024,PW),BF),jax.ShapeDtypeStruct((R,4,8,256),F32)],
        cost_estimate=cost(12),
        compiler_params=pltpu.CompilerParams(vmem_limit_bytes=VM))(idx,*heads,w,sec,*fs,stat,gain,*deps)

def qkvw_kernel(q0,k0,v0,q1,k1,v1,ml_ref,out_ref,bias_ref,acc):
    i=pl.program_id(0)*2+pl.program_id(1)
    @pl.when(i==0)
    def _(): acc[...]=jnp.zeros_like(acc); bias_ref[...]=jnp.zeros_like(bias_ref)
    d=jnp.concatenate([pad3(q0[0],k0[0],v0[0]),pad3(q1[0],k1[0],v1[0])],axis=0)
    dt=d.T
    bias_ref[...]+=jnp.broadcast_to(jnp.sum(d.astype(F32),axis=0,keepdims=True),bias_ref.shape)
    pad=jnp.zeros((d.shape[0],64),BF)
    for m in range(4):
        acc[m]+=dot(dt,jnp.concatenate([ml_ref[m].reshape(d.shape[0],LW),pad],axis=1))
    @pl.when(i==2*pl.num_programs(0)-1)
    def _():
        for t in range(3):
            out_ref[t]=jnp.concatenate([acc[m,256*t:256*t+192,:LW] for m in range(4)],axis=1).astype(BF)

def qkvw(heads,ml,deps=()):
    pairs=heads[0].shape[0]
    row=pl.BlockSpec((1,512,LW),lambda p,i:(p,i,0))
    return pl.pallas_call(skip(qkvw_kernel,7,len(deps)),grid=(pairs,2),
        in_specs=[row]*6+[pl.BlockSpec((4,2,512,LW),lambda p,i:(0,p,i,0))]+[ANY]*len(deps),
        out_specs=[pl.BlockSpec((3,LW,768),lambda p,i:(0,0,0)),pl.BlockSpec((8,768),lambda p,i:(0,0))],
        out_shape=[jax.ShapeDtypeStruct((3,LW,768),BF),jax.ShapeDtypeStruct((8,768),F32)],
        scratch_shapes=[pltpu.VMEM((4,768,256),F32)],
        cost_estimate=cost(8),
        compiler_params=pltpu.CompilerParams(vmem_limit_bytes=VM))(*heads,ml,*deps)


def row_sum(x):
    return jnp.sum(x, axis=0, keepdims=True)


def norm_parts(x):
    c = x - jnp.mean(x, axis=1, keepdims=True)
    rstd = lax.rsqrt(jnp.mean(c * c, axis=1, keepdims=True) + 1e-5)
    return c * rstd, rstd


def norm_back(e, xhat, rstd, gain):
    eg = e * gain
    return rstd * (eg - jnp.mean(eg, axis=1, keepdims=True) - xhat * jnp.mean(eg * xhat, axis=1, keepdims=True))


def in_order(blocks, index):
    low = (index & 1) != 0
    high = (index & 2) != 0
    b = [jnp.where(low, blocks[m ^ 1], blocks[m]) for m in range(4)]
    return jnp.concatenate([jnp.where(high, b[m ^ 2], b[m]) for m in range(4)], axis=1)


def half(r):
    return slice(LW * (r % 2), LW * (r % 2) + LW)


def ff_kernel(
    idx_ref, f0, f1, f2, f3, a0, a1, a2, a3, og_ref, pw_ref, iw_ref, ow_ref, ib_ref, vec_ref,
    out_ref, act_ref, din_ref, ml_ref, do_ref, dp_ref, att_ref, datt_ref, sec_ref, sums_ref, ibg_ref,
    mid, xh2, rs2, acc, slopes,
):
    i = pl.program_id(0)
    index = idx_ref[0]
    R = 2 * f0.shape[0]
    M = R * 256
    pos_gain, pos_shift, proj_bias, gain2, shift2, outer_bias, gain3, shift3 = [vec_ref[j : j + 1, :] for j in range(8)]

    @pl.when(i == 0)
    def _():
        for r in range(R):
            rows = pl.ds(256 * r, 256)
            xhat, _ = norm_parts(in_order([f[r // 2, 0].astype(F32)[:, half(r)] for f in (f0, f1, f2, f3)], index))
            att_ref[rows] = in_order([a[pl.ds(256 * (r // 2), 256)].astype(F32)[:, half(r)] for a in (a0, a1, a2, a3)], index).astype(BF)
            second = xhat * pos_gain + pos_shift + dot(att_ref[rows], pw_ref[...]) + proj_bias
            xhat, rstd = norm_parts(second)
            xh2[rows] = xhat
            rs2[rows] = jnp.broadcast_to(rstd, (256, 128))
            middle = xhat * gain2 + shift2
            mid[rows] = middle
            ml_ref[rows] = middle.astype(BF)
        acc[...] = jnp.zeros_like(acc)

    @pl.when(i < 4)
    def _():
        for r in range(R):
            rows = pl.ds(256 * r, 256)
            inner = dot(ml_ref[rows], iw_ref[...]) + ib_ref[0]
            phi = erf_gelu_parts(inner)
            slopes[i, rows] = (phi + inner * (jnp.exp(-0.5 * inner * inner) * 0.3989422804014327)).astype(BF)
            act_ref[rows] = (inner * phi).astype(BF)
            acc[rows] += dot(act_ref[rows], ow_ref[...])

    @pl.when(i == 3)
    def _():
        g1 = g2 = g3 = jnp.zeros((1, 768), F32)
        for r in range(R):
            rows = pl.ds(256 * r, 256)
            xhat, rstd = norm_parts(mid[rows] + acc[rows] + outer_bias)
            out_ref[rows] = (xhat * gain3 + shift3).astype(BF)
            e = og_ref[rows].astype(F32)
            d = norm_back(e, xhat, rstd, gain3)
            low = d.astype(BF)
            do_ref[rows] = low
            mid[rows] = d
            g1, g2, g3 = g1 + row_sum(e * xhat), g2 + row_sum(e), g3 + row_sum(low.astype(F32))
        sums_ref[0:1] = g1
        sums_ref[1:2] = g2
        sums_ref[2:3] = g3
        sums_ref[3:8] = jnp.zeros((5, 768), F32)

    @pl.when(i >= 4)
    def _():
        g = jnp.zeros((1, 768), F32)
        for r in range(R):
            rows = pl.ds(256 * r, 256)
            d = dot_nt(do_ref[rows], ow_ref[...]) * slopes[7 - i, rows].astype(F32)
            low = d.astype(BF)
            din_ref[rows] = low
            g = g + row_sum(low.astype(F32))
            mid[rows] += dot_nt(low, iw_ref[...])
        ibg_ref[0] = g

    @pl.when(i == 7)
    def _():
        g1 = g2 = g3 = jnp.zeros((1, 768), F32)
        for r in range(R):
            rows = pl.ds(256 * r, 256)
            e = mid[rows]
            xhat = xh2[rows]
            d = norm_back(e, xhat, rs2[rows, 0:1], gain2)
            low = d.astype(BF)
            dp_ref[rows] = low
            datt = dot_nt(low, pw_ref[...]).astype(BF)
            for b in range(4):
                datt_ref[index ^ b, pl.ds(256 * (r // 2), 256), half(r)] = datt[:, LW * b : LW * b + LW]
                sec_ref[index ^ b, r] = d[:, LW * b : LW * b + LW]
            g1, g2, g3 = g1 + row_sum(e * xhat), g2 + row_sum(e), g3 + row_sum(low.astype(F32))
        sums_ref[3:4] = g1
        sums_ref[4:5] = g2
        sums_ref[5:6] = g3


def ff(idx, firsts, atts, out_grad, pw, iw, ow, ib, vec):
    pairs = atts[0].shape[0] // 256
    R = 2 * pairs
    M = R * 256
    chunk = lambda i: jnp.where(i < 4, i, 7 - i)
    whole = lambda *s: pl.BlockSpec(s, lambda i, x: (0,) * len(s))
    return pl.pallas_call(
        ff_kernel,
        grid_spec=pltpu.PrefetchScalarGridSpec(
            num_scalar_prefetch=1,
            grid=(8,),
            in_specs=[pl.BlockSpec((pairs, 1, 256, PW), lambda i, x: (0, x[0], 0, 0))] * 4
            + [whole(pairs * 256, PW)] * 4
            + [
                whole(M, 768),
                whole(768, 768),
                pl.BlockSpec((768, 768), lambda i, x: (0, chunk(i))),
                pl.BlockSpec((768, 768), lambda i, x: (chunk(i), 0)),
                pl.BlockSpec((1, 1, 768), lambda i, x: (chunk(i), 0, 0)),
                whole(8, 768),
            ],
            out_specs=[
                whole(M, 768),
                pl.BlockSpec((M, 768), lambda i, x: (0, jnp.minimum(i, 3))),
                pl.BlockSpec((M, 768), lambda i, x: (0, jnp.minimum(7 - i, 3))),
            ]
            + [whole(M, 768)] * 4
            + [
                whole(4, pairs * 256, PW),
                whole(4, R, 256, LW),
                whole(8, 768),
                pl.BlockSpec((1, 1, 768), lambda i, x: (jnp.minimum(7 - i, 3), 0, 0)),
            ],
            scratch_shapes=[
                pltpu.VMEM((M, 768), F32),
                pltpu.VMEM((M, 768), F32),
                pltpu.VMEM((M, 128), F32),
                pltpu.VMEM((M, 768), F32),
                pltpu.VMEM((4, M, 768), BF),
            ],
        ),
        out_shape=[
            jax.ShapeDtypeStruct((M, 768), BF),
            jax.ShapeDtypeStruct((M, 3072), BF),
            jax.ShapeDtypeStruct((M, 3072), BF),
        ]
        + [jax.ShapeDtypeStruct((M, 768), BF)] * 4
        + [
            jax.ShapeDtypeStruct((4, pairs * 256, PW), BF),
            jax.ShapeDtypeStruct((4, R, 256, LW), F32),
            jax.ShapeDtypeStruct((8, 768), F32),
            jax.ShapeDtypeStruct((4, 1, 768), F32),
        ],
        cost_estimate=cost(40),
        compiler_params=pltpu.CompilerParams(vmem_limit_bytes=VM),
    )(idx, *[f.reshape(pairs, 4, 256, PW) for f in firsts], *atts, out_grad, pw, iw, ow, ib, vec)


BULK = 1792


def ffw_kernel(idx_ref, act_ref, din_ref, ml_ref, do_ref, dp_ref, att_ref, sums_ref, ibg_ref, keep_ref, send_ref):
    c = pl.program_id(0)
    index = idx_ref[0]

    def put(b, rows, value):
        m = index ^ b

        @pl.when((m & 1) == 0)
        def _():
            keep_ref[m >> 1, rows] = value

        @pl.when((m & 1) == 1)
        def _():
            send_ref[m >> 1, rows] = value

    put(c, pl.ds(0, 768), dot_tn(ml_ref[...], din_ref[...]).astype(BF))
    outer = dot_tn(do_ref[...], act_ref[...]).astype(BF)
    for b in range(4):
        put(b, pl.ds(pl.multiple_of(768 + LW * c, LW), LW), outer[LW * b : LW * b + LW])

    @pl.when(c == 0)
    def _():
        proj = dot_tn(dp_ref[...], att_ref[...]).astype(BF)
        for b in range(4):
            put(b, pl.ds(1536, LW), proj[LW * b : LW * b + LW])
            small = jnp.concatenate([sums_ref[:, LW * b : LW * b + LW], jnp.zeros((8, 576), F32)], axis=1)
            small = jnp.concatenate([small, ibg_ref[b], jnp.zeros((7, 768), F32)], axis=0)
            put(b, pl.ds(1728, 16), small.astype(BF))
            put(b, pl.ds(1744, 48), jnp.zeros((48, 768), BF))


def ffw(idx, act, din, ml, do, dp, att, sums, ibg):
    M = ml.shape[0]
    col = pl.BlockSpec((M, 768), lambda i, x: (0, i))
    whole = lambda *s: pl.BlockSpec(s, lambda i, x: (0,) * len(s))
    return pl.pallas_call(
        ffw_kernel,
        grid_spec=pltpu.PrefetchScalarGridSpec(
            num_scalar_prefetch=1,
            grid=(4,),
            in_specs=[col, col] + [whole(M, 768)] * 4 + [whole(8, 768), whole(4, 1, 768)],
            out_specs=[whole(2, BULK, 768)] * 2,
        ),
        out_shape=[jax.ShapeDtypeStruct((2, BULK, 768), BF)] * 2,
        cost_estimate=cost(15),
        compiler_params=pltpu.CompilerParams(vmem_limit_bytes=VM),
    )(idx, act, din, ml, do, dp, att, sums, ibg)


def taps_kernel(own_ref, coef_ref, dir_ref, out_ref, tmp):
    n = dir_ref.shape[0]
    for k in range(n):
        tmp[48 * k : 48 * k + 48] = (dir_ref[k].astype(F32) * coef_ref[pl.program_id(0) * n + k]).astype(BF)
    row = lax.broadcasted_iota(jnp.int32, (PW, 256), 0)
    lane = lax.broadcasted_iota(jnp.int32, (PW, 256), 1)
    pick = ((row == lane + LW * (own_ref[0] & 1)) & (lane < LW)).astype(F32).astype(BF)
    out_ref[...] = dot(tmp[...], pick)[:, :LW].astype(BF)


def own_taps(idx, coef, tap_dir, deps=()):
    return pl.pallas_call(
        skip(taps_kernel, 3, len(deps)),
        grid_spec=pltpu.PrefetchScalarGridSpec(
            num_scalar_prefetch=2,
            grid=(8,),
            in_specs=[pl.BlockSpec((16, 48, PW), lambda i, x, c: (i, 0, x[0] // 2))] + [ANY] * len(deps),
            out_specs=pl.BlockSpec((768, LW), lambda i, x, c: (i, 0)),
            scratch_shapes=[pltpu.VMEM((768, PW), BF)],
        ),
        out_shape=jax.ShapeDtypeStruct((6144, LW), BF),
        cost_estimate=cost(5),
        compiler_params=pltpu.CompilerParams(vmem_limit_bytes=VM),
    )(idx, coef, tap_dir, *deps)


def dots_kernel(tap_ref, dir_ref, out_ref):
    g = tap_ref[0].astype(F32).T
    p = g * dir_ref[...].astype(F32)
    rows = [jnp.sum(p[48 * t : 48 * t + 48], axis=0, keepdims=True) for t in range(16)]
    s = jnp.sum(jnp.concatenate(rows, axis=0), axis=1, keepdims=True)
    out_ref[0] = jnp.broadcast_to(s, (16, 128))


def tap_dots(tap, dirs, deps=()):
    return pl.pallas_call(
        skip(dots_kernel, 2, len(deps)),
        grid=(8,),
        in_specs=[pl.BlockSpec((1, LW, 768), lambda i: (i, 0, 0)), pl.BlockSpec((768, LW), lambda i: (i, 0))] + [ANY] * len(deps),
        out_specs=pl.BlockSpec((1, 16, 128), lambda i: (i, 0, 0)),
        out_shape=jax.ShapeDtypeStruct((8, 16, 128), F32),
        cost_estimate=cost(6),
        compiler_params=pltpu.CompilerParams(vmem_limit_bytes=VM),
    )(tap, dirs, *deps)


def last_kernel(tap_ref, dir_ref, coef_ref, beta_ref, out_ref, turned):
    i = pl.program_id(0)

    @pl.when(i == 0)
    def _():
        for J in range(8):
            t = tap_ref[J].astype(F32).T
            turned[0, 768 * J : 768 * J + 768] = t[:, :128]
            turned[1, 768 * J : 768 * J + 768, :64] = t[:, 128:]

    for c in range(8):
        at = pl.ds(8 * i + c, 128, stride=48)
        g = jnp.concatenate([turned[0, at].T, turned[1, at].T[:64]], axis=0)
        out_ref[c] = g * coef_ref[...] - dir_ref[c].astype(F32) * beta_ref[...]


def last_taps(coef, beta, taps, dirs):
    row = pl.BlockSpec((1, 128), lambda i: (0, 0))
    block = pl.BlockSpec((8, LW, 128), lambda i: (i, 0, 0))
    return pl.pallas_call(
        last_kernel,
        grid=(6,),
        in_specs=[pl.BlockSpec((8, LW, 768), lambda i: (0, 0, 0)), block, row, row],
        out_specs=block,
        out_shape=jax.ShapeDtypeStruct((48, LW, 128), F32),
        scratch_shapes=[pltpu.VMEM((2, 6144, 128), F32)],
        cost_estimate=cost(8),
        compiler_params=pltpu.CompilerParams(vmem_limit_bytes=VM),
    )(taps, dirs, coef[None], beta[None])


def swap(x, axis, bit):
    return lax.ppermute(x, axis, [(i, i ^ bit) for i in range(lax.axis_size(axis))])


def pick_half(x, axis, bit, dim):
    on = (lax.axis_index(axis) & bit) != 0
    lo, hi = jnp.split(x, 2, axis=dim)
    return jnp.where(on, lo, hi), jnp.where(on, hi, lo)


def double(x, axis, bit):
    on = (lax.axis_index(axis) & bit) != 0
    got = swap(x, axis, bit)
    return jnp.concatenate([jnp.where(on, got, x), jnp.where(on, x, got)], axis=0)


class RowSum:
    def __init__(self, x, dim=0):
        n = lax.axis_size("rows")
        bits = [1 << i for i in range(n.bit_length() - 1)]
        self.orders = (bits, bits[1::-1] + bits[2:])
        self.dim = dim
        self.count = x.shape[dim]
        full = -(-self.count // (8 * n)) * (8 * n)
        if full != self.count:
            widths = [(0, 0)] * x.ndim
            widths[dim] = (0, full - self.count)
            x = jnp.pad(x, widths)
        cut_at = -(-full // (16 * n)) * (8 * n)
        self.parts = [lax.slice_in_dim(x, 0, cut_at, axis=dim), lax.slice_in_dim(x, cut_at, full, axis=dim)]
        self.stage = 0
        self.cut()

    def cut(self):
        pairs = [pick_half(p, "rows", o[self.stage], self.dim) for p, o in zip(self.parts, self.orders)]
        self.sends = [p[0] for p in pairs]
        self.keeps = [p[1] for p in pairs]

    def done(self):
        return self.stage == len(self.orders[0])

    def step(self, after=None):
        if after is not None:
            self.keeps = [late(k, after) for k in self.keeps]
        self.parts = [
            (k.astype(F32) + swap(s, "rows", o[self.stage]).astype(F32)).astype(BF)
            for k, s, o in zip(self.keeps, self.sends, self.orders)
        ]
        self.stage += 1
        if not self.done():
            self.cut()

    def finish(self):
        while not self.done():
            self.step()
        parts = self.parts
        if self.dim:
            parts = [(p[0].astype(F32) + swap(p[1], "seq", 2).astype(F32)).astype(BF) for p in parts]
        for s in reversed(range(len(self.orders[0]))):
            parts = [double(p, "rows", o[s]) for p, o in zip(parts, self.orders)]
        return jnp.concatenate(parts, axis=0)[: self.count]


def late(x, after):
    return x + (after[(0,) * after.ndim].astype(F32) * 0.0).astype(x.dtype)


def gather_seq(x):
    far = swap(x, "seq", 2)
    near = swap(x, "seq", 1)
    return [x, near, far, swap(far, "seq", 1)]


def trade(blocks):
    return [blocks[0], swap(blocks[1], "seq", 1), swap(blocks[2], "seq", 2), swap(blocks[3], "seq", 3)]


def scatter_pair(keep, send):
    got = swap(send, "seq", 1).astype(F32)
    far = (keep[1].astype(F32) + got[1]).astype(BF)
    return keep[0].astype(F32) + got[0], far


def all_sum(x, axis):
    for i in range(lax.axis_size(axis).bit_length() - 1):
        x = x + swap(x, axis, 1 << i)
    return x


def assemble(blocks, index):
    low = (index & 1) != 0
    high = (index & 2) != 0
    b = [jnp.where(low, blocks[m ^ 1], blocks[m]) for m in range(4)]
    return [jnp.where(high, b[m ^ 2], b[m]) for m in range(4)]


def cut(x, start, size, axis):
    return lax.dynamic_slice_in_dim(x, start, size, axis)


def local(
    frames,
    utterance_lengths,
    tap_dir,
    tap_scale,
    conv_bias,
    pos_gain,
    pos_shift,
    query_weight,
    query_bias,
    key_weight,
    value_weight,
    value_bias,
    proj_weight,
    proj_bias,
    attend_gain,
    attend_shift,
    inner_weight,
    inner_bias,
    outer_weight,
    outer_bias,
    final_gain,
    final_shift,
    out_grad,
):
    R = frames.shape[0]
    index = lax.axis_index("seq")
    idx = jnp.full((1,), index, jnp.int32)
    ends = jnp.cumsum(utterance_lengths, axis=1, dtype=jnp.int32)
    order = [index ^ m for m in range(4)]
    own = index * LW

    def packed(x):
        return jnp.concatenate([x[0::2], x[1::2]], axis=2).reshape(R * 128, PW)

    sent = trade([packed(cut(frames, b * LW, LW, 2)) for b in order])
    squares = jnp.sum(jnp.square(tap_dir.astype(F32)), axis=(1, 2))
    coef = tap_scale * lax.rsqrt(squares)
    w = build_w(own_taps(idx, coef, tap_dir))
    bias4 = jnp.tile(cut(conv_bias, own, LW, 0).reshape(4, 1, 48), (1, 4, 1)).reshape(4, 1, LW)
    first, pre, xs = conv_fwd(ends, idx, sent, w, bias4)
    firsts = gather_seq(first)

    def xor_rows(a):
        return jnp.stack([cut(a, b * LW, LW, 0) for b in order])

    def pad_to(a, axis, size):
        widths = [(0, 0)] * a.ndim
        widths[axis] = (0, size - a.shape[axis])
        return jnp.pad(a, widths)

    own_cols = [
        pad_to(cut(a, own, LW, 1), 1, 256)
        for a in (query_weight * jnp.asarray(0.125, BF), key_weight, value_weight)
    ]
    w_qkv = pad_to(xor_rows(jnp.concatenate(own_cols, axis=1)), 1, 256)
    b_qkv = jnp.concatenate(
        [
            pad_to(cut(query_bias, own, LW, 0) * 0.125, 0, 512),
            pad_to(cut(value_bias, own, LW, 0), 0, 256),
        ]
    )[None]
    gain_x = xor_rows(pos_gain)[:, None]
    shift_x = xor_rows(pos_shift)[:, None]
    q, k, v, mixed_low, stat = qkv(firsts, w_qkv, b_qkv, gain_x, shift_x)
    att, att_full, lse = attn(idx, ends, q, k, v)
    att_blocks = trade([att[m] for m in range(4)])

    vecs = jnp.stack([pos_gain, pos_shift, proj_bias, attend_gain, attend_shift, outer_bias, final_gain, final_shift])
    layer_out, act, d_inner, middle_low, d_outer, d_proj, attended, d_att, second_x, sums, inner_sums = ff(
        idx, firsts, att_blocks, out_grad.reshape(R * 256, 768), proj_weight, inner_weight, outer_weight,
        inner_bias.reshape(4, 1, 768), vecs,
    )
    dos = trade_out(d_att)
    keep, send = ffw(idx, act, d_inner, middle_low, d_outer, d_proj, attended, sums, inner_sums)

    heads = attn_bwd(0, idx, ends, q, k, v, att_full, dos, lse)
    bulk = RowSum((late(keep, heads[0]).astype(F32) + swap(send, "seq", 1).astype(F32)).astype(BF), 1)
    heads += attn_bwd(1, idx, ends, q, k, v, att_full, dos, lse, tuple(bulk.sends))
    keep, send, moments = dmix(idx, heads, w_qkv, second_x, firsts, stat, gain_x)
    e_near, e_far = scatter_pair(keep, send)
    bulk.step(send)
    g_qkv, b_grads = qkvw(heads, mixed_low, (e_far, *bulk.sends))
    e_far = swap(e_far, "seq", 2)
    m1 = moments + swap(moments, "seq", 1)
    moments = (m1 + swap(m1, "seq", 2)).reshape(R * 4, 8, 256)

    tap_part, ds, d4, conv_b, vec = tap_grads(
        ends, e_near, e_far, first, stat.reshape(R * 1024, 128), moments, cut(pos_gain, own, LW, 0)[None], pre, xs, g_qkv,
    )
    if R > 2:
        tap_part = jnp.sum(tap_part.astype(F32), axis=0, keepdims=True).astype(BF)
    tap_part = tap_part[0]
    tap_sum = RowSum(tap_part.reshape(11 * LW, 768))
    bulk.step(tap_part)
    part = conv_back(0, ends, idx, ds, d4, w, None, tuple(tap_sum.sends + bulk.sends))
    tap_sum.step(part)
    back = conv_back(2, ends, idx, ds, d4, w, part, tuple(tap_sum.sends))
    tap_sum.step(back)
    bulk.step(back)
    dir_own = own_taps(idx, jnp.ones((128,), F32), tap_dir, tuple(tap_sum.sends + bulk.parts))
    dir_turned = jnp.transpose(dir_own.reshape(128, 48, LW), (1, 2, 0))
    dots = all_sum(tap_dots(tap_part, dir_own)[:, :, 0], "seq")
    back = trade_out(back)
    back = jnp.concatenate([b.reshape(R // 2, 1, 256, PW) for b in assemble(back, index)], axis=1)
    back = back.reshape(R // 2, 4, 256, 2, LW)
    frames_grad = jnp.transpose(back, (0, 3, 2, 1, 4)).reshape(R, 256, 768)
    bulk_sum = bulk.finish()
    t_inner = bulk_sum[:768].astype(F32)
    t_outer = jnp.concatenate([bulk_sum[768 + LW * i : 768 + LW * i + LW] for i in range(4)], axis=1).astype(F32).T
    t_proj = bulk_sum[1536:1728].astype(F32).T
    small = bulk_sum[1728:1744].astype(F32)
    tap_total = tap_sum.finish().reshape(11, LW, 768)
    qkv_std = assemble([tap_total[8:, :, LW * m : LW * m + LW] for m in range(4)], index)
    t_qkv = jnp.concatenate(qkv_std, axis=2).astype(F32)
    lates = jnp.concatenate(
        [
            jnp.sum(conv_b, axis=(0, 2)).reshape(4, 4, 48).sum(1).reshape(LW),
            jnp.sum(vec[:, 0], axis=0),
            jnp.sum(vec[:, 1], axis=0),
            b_grads[0, 0:LW] * 0.125,
            b_grads[0, 512 : 512 + LW],
            dots.reshape(128),
            jnp.zeros((2048 - 1088,), F32),
        ]
    )
    lates = all_sum(lates.reshape(16, 128), "rows").reshape(2048)
    dots = lates[5 * LW : 5 * LW + 128]
    inverse = lax.rsqrt(squares)
    g_tap_dir = jnp.transpose(last_taps(coef, coef * dots * inverse * inverse, tap_total, dir_turned), (2, 0, 1))
    g_tap_scale = cut(dots * inverse, index * 32, 32, 0)

    return (
        layer_out.reshape(R, 256, 768),
        frames_grad,
        g_tap_dir,
        g_tap_scale,
        lates[0:LW],
        lates[LW : 2 * LW],
        lates[2 * LW : 3 * LW],
        t_qkv[0].T * 0.125,
        lates[3 * LW : 4 * LW],
        t_qkv[1].T,
        t_qkv[2].T,
        lates[4 * LW : 5 * LW],
        t_proj,
        small[5, :LW],
        small[3, :LW],
        small[4, :LW],
        t_inner,
        small[8],
        t_outer,
        small[2, :LW],
        small[0, :LW],
        small[1, :LW],
    )


def trade_out(x):
    return trade([x[m] for m in range(4)])


def solution(mesh):
    split = P("rows", "seq", None)
    col = P(None, "seq")
    one = P("seq")
    return jax.shard_map(
        local,
        mesh=mesh,
        in_specs=(split, P("rows", None)) + (P(),) * 20 + (split,),
        out_specs=(split, split, P(None, None, "seq"), one, one, one, one)
        + (col, one, col, col, one, col, one, one, one, col, one, col, one, one, one),
        check_vma=False,
    )
```

time: 717 us -> 535 us (0.75)
  Pallas kernels: 174 us -> 262 us
  waiting for transfers between devices: 183 us -> 110 us
  local copies, waits for them, and re-layouts: 111 us -> 38.3 us
  blocking collectives: 66.5 us -> 0 us
  matrix products: 44.3 us -> 0 us
  other arithmetic: 90.2 us -> 60.3 us
  starting transfers between devices: 39.8 us -> 53.1 us
    pallas_call x6 -> x14, Pallas kernels: 112 us -> 201 us  [the longest x2 32.1 us: conv_back(): pl.pallas_call(skip(lambda *refs: back_kernel(at, *refs), 5 + len(parts),...]
    ppermute x59 -> x51, waiting for transfers between devices: 183 us -> 110 us  [swap(): lax.ppermute(x, axis, [(i, i ^ bit) for i in range(lax.axis_size(axis))])]
    psum x3 -> x0, blocking collectives: 66.5 us -> none  [the longest x1 41.2 us: local(): early = lax.psum(early, ('rows', 'seq'))]
    dot_general x9 -> x0, matrix products: 44.3 us -> none  [the longest x3 22.2 us: dot(): return jnp.dot(a, b, preferred_element_type=F32)]
    unnamed x104 -> x91, local copies, waits for them, and re-layouts: 38.5 us -> 10.6 us
    convert_element_type x4 -> x0, local copies, waits for them, and re-layouts: 24.6 us -> none  [the longest x2 14.3 us: local(): tap_grad = tap_sum.transpose(1, 3, 0, 2).reshape(128, 48, LW).astype(F32)]
    reduce_sum x12 -> x1, other arithmetic: 20.4 us -> 6.52 us  [local(): squares = jnp.sum(jnp.square(tap_dir.astype(F32)), axis=(1, 2))]
    ppermute x59 -> x51, starting transfers between devices: 39.8 us -> 53.1 us  [swap(): lax.ppermute(x, axis, [(i, i ^ bit) for i in range(lax.axis_size(axis))])]
  transfers between devices with their start and end apart: 59 -> 51, of which waited for: 34 -> 22; matrix products, arithmetic and copies ran while one was open for 24% -> 13% of each run, Pallas kernels for 16% -> 30%
where the time goes in v2:
time: 535 us; the launch traced here: 530 us
  Pallas kernels  262 us (49%)
  waiting for transfers between devices  110 us (21%)
  other arithmetic  60.3 us (11%)
  starting transfers between devices  53.1 us (10%)
  local copies, waits for them, and re-layouts  38.3 us (7%)
    ppermute x51, waiting for transfers between devices, swap(): lax.ppermute(x, axis, [(i, i ^ bit) for i in range(lax.axis_size(axis))])  110 us
    ppermute x51, starting transfers between devices, swap(): lax.ppermute(x, axis, [(i, i ^ bit) for i in range(lax.axis_size(axis))])  53.1 us
    pallas_call x1, Pallas kernels, conv_fwd(): pl.pallas_call(conv_fwd_kernel, grid=(pairs, 4), in_specs=[pl.BlockSpec(m...  34.9 us
    pallas_call x2, Pallas kernels, conv_back(): pl.pallas_call(skip(lambda *refs: back_kernel(at, *refs), 5 + len(parts),...  32.1 us
    pallas_call x2, Pallas kernels, attn_bwd(): pl.pallas_call(skip(lambda *refs: attn_bwd_kernel(r, *refs), 11, len(deps...  29.9 us
    pallas_call x1, Pallas kernels, ff(): pl.pallas_call(ff_kernel, grid_spec=pltpu.PrefetchScalarGridSpec(num_scal...  26.7 us
    pallas_call x1, Pallas kernels, tap_grads(): pl.pallas_call(skip(tap_kernel, 10, len(deps)), grid=(pairs, 4), in_specs...  25 us
    pallas_call x2, Pallas kernels, own_taps(): pl.pallas_call(skip(taps_kernel, 3, len(deps)), grid_spec=pltpu.PrefetchS...  17.5 us
  transfers between devices with their start and end apart: 51, of which 22 were waited for; matrix products, arithmetic and copies ran while one was open for 13% of the time, Pallas kernels for 30%

profile of v2, /device:TPU:0, one launch (start us, length us, event | category | flops | bytes accessed | tf_op | source)
XLA Modules:
  0.0 529.6 jit_solution(12380668060266358734)
XLA Ops:
  2.8 2.5 collective-permute-start.2
  6.3 6.5 %multiply_reduce_fusion = f32[128]{0:T(128)S(1)} fusion(bf16[128,48,768]{2,1,0:T(8,128)(2,1)} %refs_2_.1), kind=kLoop, calls=%fused_computation | loop fusion | flops 14155648 | bytes 9437696 | tf_op jit(solution)/shard_map/reduce_sum | solution.py:912
  13.9 9.0 %shard_map.390.t_ref = bf16[6144,192]{1,0:T(8,128)(2,1)} custom-call(s32[1]{0:T(128)} %bitcast.own_ref.idx_ref.refs_0_.refs_1_, f32[128]{0:T(128)} %rsqrt_multiply_fusion.coef_ref, bf16[128,48,768]{2,1,0:T(8,128)(2,1)} %refs_2_.1), custom_call_target="tpu_custom_call" | custom-call | flops 5000000000 | bytes 15000000 | tf_op jit(solution)/shard_map/pallas_call | solution.py:710
  22.9 9.3 %shard_map.391.w_ref.refs_4_ = bf16[4,6400,256]{2,1,0:T(8,128)(2,1)} custom-call(bf16[6144,192]{1,0:T(8,128)(2,1)} %shard_map.390.t_ref), custom_call_target="tpu_custom_call" | custom-call | flops 10000000000 | bytes 30000000 | tf_op jit(solution)/shard_map/pallas_call | solution.py:53
  36.6 34.9 %shard_map.392 = (bf16[1024,384]{1,0:T(8,128)(2,1)}, f32[1,4,512,192]{3,2,1,0:T(8,128)}, bf16[1,4,1280,768]{3,2,1,0:T(8,128)(2,1)}) custom-call(s32[2,8]{1,0:T(2,128)} %reduce_window_sum.11.seg_ref.refs_1_.refs_0_, s32[1]{0:T(128)} %bitcast.own_ref.idx_ref.refs_0_.refs_1_, bf16[256,384]{1,0:T(8,128)(2,1)} %maximum_bitcast_fusion.1.x0_ref, ...), custom_call_target="tpu_custom_call" | custom-call | flops 35000000512 | bytes 105000000 | tf_op jit(solution)/shard_map/pallas_call | solution.py:164
  78.4 13.2 %collective-permute-done.4.f2 = bf16[1024,384]{1,0:T(8,128)(2,1)S(1)} collective-permute-done((bf16[1024,384]{1,0:T(8,128)(2,1)}, bf16[1024,384]{1,0:T(8,128)(2,1)S(1)}, u32[]{:S(2)}, u32[]{:S(2)}) %collective-permute-start.4) | collective-permute-done | bytes 786464 | tf_op jit(solution)/shard_map/ppermute | solution.py:777
  94.6 14.4 %shard_map.393 = (bf16[2,1024,192]{2,1,0:T(8,128)(2,1)}, bf16[2,1024,192]{2,1,0:T(8,128)(2,1)}, bf16[2,1024,192]{2,1,0:T(8,128)(2,1)}, bf16[4,2,1024,192]{3,2,1,0:T(8,128)(2,1)}, f32[2,1024,128]{2,1,0:T(8,128)}) custom-call(bf16[1024,384]{1,0:T(8,128)(2,1)} %get-tuple-element.62.f0.first_ref, bf16[1024,384]{1,0:T(8,128)(2,1)} %copy-done.34, ...), custom_call_target="tpu_custom_call" | custom-call | flops 10000000000 | bytes 30000000 | tf_op jit(solution)/shard_map/pallas_call | solution.py:327
  109.0 17.4 %shard_map.394 = (bf16[4,256,384]{2,1,0:T(8,128)(2,1)}, f32[2,1024,192]{2,1,0:T(8,128)}, f32[2,4,8,256]{3,2,1,0:T(8,128)}) custom-call(s32[1]{0:T(128)} %bitcast.own_ref.idx_ref.refs_0_.refs_1_, s32[2,8]{1,0:T(2,128)} %reduce_window_sum.11.seg_ref.refs_1_.refs_0_, bf16[2,1024,192]{2,1,0:T(8,128)(2,1)} %get-tuple-element.63.q_ref.refs_2_, ...), custom_call_target="tpu_custom_call" | custom-call | flops 17999998976 | bytes 54000000 | tf_op jit(solution)/shard_map/pallas_call | solution.py:363
  131.1 5.1 collective-permute-done.7.a2
  136.2 3.3 collective-permute-done.8.a3
  140.1 26.7 %shard_map.395 = (bf16[512,768]{1,0:T(8,128)(2,1)}, bf16[512,3072]{1,0:T(8,128)(2,1)}, bf16[512,3072]{1,0:T(8,128)(2,1)}, bf16[512,768]{1,0:T(8,128)(2,1)}, bf16...) custom-call(s32[1]{0:T(128)} %bitcast.own_ref.idx_ref.refs_0_.refs_1, ...), custom_call_target="tpu_custom_call" | custom-call | flops 40000000000 | bytes 120000000 | tf_op jit(solution)/shard_map/pallas_call | solution.py:595
  171.0 16.6 %shard_map.397 = (bf16[2,1792,768]{2,1,0:T(8,128)(2,1)}, bf16[2,1792,768]{2,1,0:T(8,128)(2,1)}) custom-call(s32[1]{0:T(128)} %bitcast.own_ref.idx_ref.refs_0_.refs_1_, bf16[512,3072]{1,0:T(8,128)(2,1)} %get-tuple-element.74.act_ref, bf16[512,3072]{1,0:T(8,128)(2,1)} %get-tuple-element.75.din_ref, bf16[512,768]{1,0:T(8,128)(2,1)} %get-tuple-element.76.ml_ref, ...), custom_call_target="tpu_custom_call" | custom-call | flops 15000000512 | bytes 45000000 | tf_op jit(solution)/shard_map/pallas_call | solution.py:685
  188.5 14.9 %shard_map.396 = (bf16[1,1024,192]{2,1,0:T(8,128)(2,1)}, bf16[1,1024,192]{2,1,0:T(8,128)(2,1)}, bf16[1,1024,192]{2,1,0:T(8,128)(2,1)}) custom-call(s32[1]{0:T(128)} %bitcast.own_ref.idx_ref.refs_0_.refs_1_, s32[2,8]{1,0:T(2,128)} %reduce_window_sum.11.seg_ref.refs_1_.refs_0_, bf16[2,1024,192]{2,1,0:T(8,128)(2,1)} %get-tuple-element.63.q_ref.refs_2_, ...), custom_call_target="tpu_custom_call" | custom-call | flops 60000002048 | bytes 180000000 | tf_op jit(solution)/shard_map/pallas_call | solution.py:402
  205.3 5.9 %add_convert_fusion = bf16[2,1792,768]{2,1,0:T(8,128)(2,1)S(1)} fusion(bf16[2,1792,768]{2,1,0:T(8,128)(2,1)} %collective-permute-done.12, bf16[2,1792,768]{2,1,0:T(8,128)(2,1)} %get-tuple-element.82, bf16[]{:T(256)} %bitcast.33), kind=kLoop, calls=%fused_computation.1 | loop fusion | flops 13762560 | bytes 16515074 | tf_op jit(solution)/shard_map/convert_element_type | solution.py:953
  211.1 2.0 broadcast_select_fusion
  217.5 15.0 %shard_map.398 = (bf16[1,1024,192]{2,1,0:T(8,128)(2,1)}, bf16[1,1024,192]{2,1,0:T(8,128)(2,1)}, bf16[1,1024,192]{2,1,0:T(8,128)(2,1)}) custom-call(s32[1]{0:T(128)} %bitcast.own_ref.idx_ref.refs_0_.refs_1_, s32[2,8]{1,0:T(2,128)} %reduce_window_sum.11.seg_ref.refs_1_.refs_0_, bf16[2,1024,192]{2,1,0:T(8,128)(2,1)} %get-tuple-element.63.q_ref.refs_2_, ...), custom_call_target="tpu_custom_call" | custom-call | flops 60000002048 | bytes 180000000 | tf_op jit(solution)/shard_map/pallas_call | solution.py:402
  232.5 16.0 %shard_map.399 = (f32[2,1024,384]{2,1,0:T(8,128)}, bf16[2,1024,384]{2,1,0:T(8,128)(2,1)}, f32[2,4,8,256]{3,2,1,0:T(8,128)}) custom-call(s32[1]{0:T(128)} %bitcast.own_ref.idx_ref.refs_0_.refs_1_, bf16[1,1024,192]{2,1,0:T(8,128)(2,1)} %get-tuple-element.71.q0.refs_0_, bf16[1,1024,192]{2,1,0:T(8,128)(2,1)} %get-tuple-element.72.k0.refs_1_, ...), custom_call_target="tpu_custom_call" | custom-call | flops 12000000000 | bytes 36000000 | tf_op jit(solution)/shard_map/pallas_call | solution.py:441
  249.1 2.8 collective-permute-done.15
  259.0 4.5 add_convert_fusion.1
  271.2 7.1 %shard_map.400 = (bf16[3,192,768]{2,1,0:T(8,128)(2,1)}, f32[8,768]{1,0:T(8,128)}) custom-call(bf16[1,1024,192]{2,1,0:T(8,128)(2,1)} %get-tuple-element.71.q0.refs_0_, bf16[1,1024,192]{2,1,0:T(8,128)(2,1)} %get-tuple-element.72.k0.refs_1_, bf16[1,1024,192]{2,1,0:T(8,128)(2,1)} %get-tuple-element.73.v0.refs_2_, ...), custom_call_target="tpu_custom_call" | custom-call | flops 8000000000 | bytes 24000000 | tf_op jit(solution)/shard_map/pallas_call | solution.py:468
  279.1 9.5 %collective-permute-done.14.e1_ref = bf16[1024,384]{1,0:T(8,128)(2,1)} collective-permute-done((bf16[1024,384]{1,0:T(8,128)(2,1)S(1)}, bf16[1024,384]{1,0:T(8,128)(2,1)}, u32[]{:S(2)}, u32[]{:S(2)}) %collective-permute-start.14) | collective-permute-done | bytes 786464 | tf_op jit(solution)/shard_map/ppermute | solution.py:777
  288.6 25.0 %shard_map.401 = (bf16[1,11,192,768]{3,2,1,0:T(8,128)(2,1)}, bf16[1,4,1280,256]{3,2,1,0:T(8,128)(2,1)}, bf16[1,4,512,192]{3,2,1,0:T(8,128)(2,1)}, f32[1,4,1,192]{3,2,1,0:T(1,128)}, f32[1,8,192]{2,1,0:T(8,128)}) custom-call(s32[2,8]{1,0:T(2,128)} %reduce_window_sum.11.seg_ref.refs_1_.refs_0_, f32[1024,384]{1,0:T(8,128)} %get-tuple-element.125.e0_ref, ...), custom_call_target="tpu_custom_call" | custom-call | flops 24000000000 | bytes 72000000 | tf_op jit(solution)/shard_map/pallas_call | solution.py:225
  323.0 2.6 collective-permute-start.36
  325.9 15.7 %shard_map.402.refs_5_ = f32[1,4,512,192]{3,2,1,0:T(8,128)} custom-call(s32[2,8]{1,0:T(2,128)} %reduce_window_sum.11.seg_ref.refs_1_.refs_0_, s32[1]{0:T(128)} %bitcast.own_ref.idx_ref.refs_0_.refs_1_, bf16[1,4,1280,256]{3,2,1,0:T(8,128)(2,1)} %get-tuple-element.96.refs_2_, bf16[1,4,512,192]{3,2,1,0:T(8,128)(2,1)} %get-tuple-element.97.refs_3_, ...), custom_call_target="tpu_custom_call" | custom-call | flops 15000000512 | bytes 45000000 | tf_op jit(solution)/shard_map/pallas_call | solution.py:289
  344.5 8.7 %collective-permute-done.22 = bf16[512,768]{1,0:T(8,128)(2,1)S(1)} collective-permute-done((bf16[512,768]{1,0:T(8,128)(2,1)}, bf16[512,768]{1,0:T(8,128)(2,1)S(1)}, u32[]{:S(2)}, u32[]{:S(2)}) %collective-permute-start.22) | collective-permute-done | bytes 786464 | tf_op jit(solution)/shard_map/ppermute | solution.py:777
  354.1 2.1 add_convert_fusion.4
  360.8 16.4 %shard_map.403 = bf16[4,256,384]{2,1,0:T(8,128)(2,1)} custom-call(s32[2,8]{1,0:T(2,128)} %reduce_window_sum.11.seg_ref.refs_1_.refs_0_, s32[1]{0:T(128)} %bitcast.own_ref.idx_ref.refs_0_.refs_1_, bf16[1,4,1280,256]{3,2,1,0:T(8,128)(2,1)} %get-tuple-element.96.refs_2_, bf16[1,4,512,192]{3,2,1,0:T(8,128)(2,1)} %get-tuple-element.97.refs_3_, ...), custom_call_target="tpu_custom_call" | custom-call | flops 15000000512 | bytes 45000000 | tf_op jit(solution)/shard_map/pallas_call | solution.py:289
  382.9 4.9 collective-permute-done.47
  391.5 2.5 collective-permute-done.23
  394.0 2.2 collective-permute-start.48
  397.1 2.4 collective-permute-start.44
  404.5 8.5 %shard_map.404.dir_ref = bf16[6144,192]{1,0:T(8,128)(2,1)} custom-call(s32[1]{0:T(128)} %bitcast.own_ref.idx_ref.refs_0_.refs_1_, f32[128]{0:T(128)} %broadcast_in_dim.29.refs_1_, bf16[128,48,768]{2,1,0:T(8,128)(2,1)} %refs_2_.1, bf16[136,768]{1,0:T(8,128)(2,1)} %broadcast_select_fusion.36.refs_3_, bf16[128,768]{1,0:T(8,128)(2,1)} %broadcast_select_fusion.39.refs_4_, ...), custom_call_target="tpu_custom_call" | custom-call | flops 5000000000 | bytes 15000000 | tf_op jit(solution)/shard_map/pallas_call | solution.py:710
  413.1 7.1 %shard_map.405 = f32[8,16,128]{2,1,0:T(8,128)} custom-call(bf16[11,192,768]{2,1,0:T(8,128)(2,1)} %bitcast.147, bf16[6144,192]{1,0:T(8,128)(2,1)} %shard_map.404.dir_ref), custom_call_target="tpu_custom_call" | custom-call | flops 6000000000 | bytes 18000000 | tf_op jit(solution)/shard_map/pallas_call | solution.py:734
  427.2 2.9 collective-permute-done.40
  431.4 4.6 collective-permute-done.41
  438.3 2.4 collective-permute-start.32
  441.3 4.9 copy.55
  448.1 5.7 %collective-permute-done.32 = bf16[128,768]{1,0:T(8,128)(2,1)} collective-permute-done((bf16[128,768]{1,0:T(8,128)(2,1)}, bf16[128,768]{1,0:T(8,128)(2,1)}, u32[]{:S(2)}, u32[]{:S(2)}) %collective-permute-start.32) | collective-permute-done | bytes 196640 | tf_op jit(solution)/shard_map/ppermute | solution.py:777
  454.8 7.5 %collective-permute-done.27 = bf16[136,768]{1,0:T(8,128)(2,1)S(1)} collective-permute-done((bf16[136,768]{1,0:T(8,128)(2,1)S(1)}, bf16[136,768]{1,0:T(8,128)(2,1)S(1)}, u32[]{:S(2)}, u32[]{:S(2)}) %collective-permute-start.27) | collective-permute-done | bytes 208928 | tf_op jit(solution)/shard_map/ppermute | solution.py:777
  462.7 3.0 collective-permute-start.50
  465.9 5.2 collective-permute-done.33
  471.9 2.7 collective-permute-done.28
  474.8 2.1 collective-permute-start.46
  476.8 7.8 %collective-permute-done.34 = bf16[256,768]{1,0:T(8,128)(2,1)S(1)} collective-permute-done((bf16[256,768]{1,0:T(8,128)(2,1)S(1)}, bf16[256,768]{1,0:T(8,128)(2,1)S(1)}, u32[]{:S(2)}, u32[]{:S(2)}) %collective-permute-start.34) | collective-permute-done | bytes 393248 | tf_op jit(solution)/shard_map/ppermute | solution.py:777
  484.9 6.5 %collective-permute-start.35 = (bf16[512,768]{1,0:T(8,128)(2,1)S(1)}, bf16[512,768]{1,0:T(8,128)(2,1)S(1)}, u32[]{:S(2)}, u32[]{:S(2)}) collective-permute-start(bf16[512,768]{1,0:T(8,128)(2,1)S(1)} %pad_maximum_fusion.4), channel_id=1, source_target_pairs={{0,8},{4,12},{8,0},{12,4},{16,24},{20,28},{24,16},{28,20},{1,9},{5... | collective-permute-start | bytes 2359304 | tf_op jit(solution)/shard_map/ppermute | solution.py:777
  492.0 10.1 %collective-permute-done.46 = bf16[448,768]{1,0:T(8,128)(2,1)S(1)} collective-permute-done((bf16[448,768]{1,0:T(8,128)(2,1)S(1)}, bf16[448,768]{1,0:T(8,128)(2,1)S(1)}, u32[]{:S(2)}, u32[]{:S(2)}) %collective-permute-start.46) | collective-permute-done | bytes 688160 | tf_op jit(solution)/shard_map/ppermute | solution.py:777
  508.0 9.1 %collective-permute-done.35 = bf16[512,768]{1,0:T(8,128)(2,1)S(1)} collective-permute-done((bf16[512,768]{1,0:T(8,128)(2,1)S(1)}, bf16[512,768]{1,0:T(8,128)(2,1)S(1)}, u32[]{:S(2)}, u32[]{:S(2)}) %collective-permute-start.35) | collective-permute-done | bytes 786464 | tf_op jit(solution)/shard_map/ppermute | solution.py:777
  521.0 8.3 %shard_map.406 = f32[48,192,128]{2,1,0:T(8,128)} custom-call(bf16[11,192,768]{2,1,0:T(8,128)(2,1)} %bitcast.152, bf16[48,192,128]{2,1,0:T(8,128)(2,1)} %bitcast.155, f32[1,128]{1,0:T(1,128)} %bitcast.181, f32[1,128]{1,0:T(1,128)} %get-tuple-element.201.beta_ref), custom_call_target="tpu_custom_call" | custom-call | flops 8000000000 | bytes 24000000 | tf_op jit(solution)/shard_map/pallas_call | solution.py:764
  (294 shorter events, 107.1 us)
Async XLA Ops:
  2.8 32.4 %collective-permute-start.2 = (bf16[256,384]{1,0:T(8,128)(2,1)S(1)}, bf16[256,384]{1,0:T(8,128)(2,1)S(1)}, u32[]{:S(2)}, u32[]{:S(2)}) collective-permute-start(bf16[256,384]{1,0:T(8,128)(2,1)S(1)} %maximum_bitcast_fusion.4), channel_id=1, source_target_pairs={{0,3},{1,2},{2,1},{3,0},{4,7},{5,6},{6,5},{7,4},{8,11},{9,10},{10,... | collective-permute-start | bytes 589832 | tf_op jit(solution)/shard_map/ppermute | solution.py:777
  5.3 29.9 %collective-permute-start.1 = (bf16[256,384]{1,0:T(8,128)(2,1)S(1)}, bf16[256,384]{1,0:T(8,128)(2,1)S(1)}, u32[]{:S(2)}, u32[]{:S(2)}) collective-permute-start(bf16[256,384]{1,0:T(8,128)(2,1)S(1)} %maximum_bitcast_fusion.3), channel_id=1, source_target_pairs={{0,2},{1,3},{2,0},{3,1},{4,6},{5,7},{6,4},{7,5},{8,10},{9,11},{10,... | collective-permute-start | bytes 589832 | tf_op jit(solution)/shard_map/ppermute | solution.py:777
  6.1 29.2 %collective-permute-start = (bf16[256,384]{1,0:T(8,128)(2,1)S(1)}, bf16[256,384]{1,0:T(8,128)(2,1)S(1)}, u32[]{:S(2)}, u32[]{:S(2)}) collective-permute-start(bf16[256,384]{1,0:T(8,128)(2,1)S(1)} %maximum_bitcast_fusion.2), channel_id=1, source_target_pairs={{0,1},{1,0},{2,3},{3,2},{4,5},{5,4},{6,7},{7,6},{8,9},{9,8},{10,11... | collective-permute-start | bytes 589832 | tf_op jit(solution)/shard_map/ppermute | solution.py:777
  71.5 20.0 %collective-permute-start.4 = (bf16[1024,384]{1,0:T(8,128)(2,1)}, bf16[1024,384]{1,0:T(8,128)(2,1)S(1)}, u32[]{:S(2)}, u32[]{:S(2)}) collective-permute-start(bf16[1024,384]{1,0:T(8,128)(2,1)} %get-tuple-element.62.f0.first_ref), channel_id=1, source_target_pairs={{0,2},{1,3},{2,0},{3,1},{4,6},{5,7},{6,4},{7,5},{8,10},{9,11},{10,... | collective-permute-start | bytes 2359304 | tf_op jit(solution)/shard_map/ppermute | solution.py:777
  78.3 15.4 %collective-permute-start.3 = (bf16[1024,384]{1,0:T(8,128)(2,1)}, bf16[1024,384]{1,0:T(8,128)(2,1)S(1)}, u32[]{:S(2)}, u32[]{:S(2)}) collective-permute-start(bf16[1024,384]{1,0:T(8,128)(2,1)} %get-tuple-element.62.f0.first_ref), channel_id=1, source_target_pairs={{0,1},{1,0},{2,3},{3,2},{4,5},{5,4},{6,7},{7,6},{8,9},{9,8},{10,11... | collective-permute-start | bytes 2359304 | tf_op jit(solution)/shard_map/ppermute | solution.py:777
  128.5 7.7 %collective-permute-start.7 = (bf16[256,384]{1,0:T(8,128)(2,1)S(1)}, bf16[256,384]{1,0:T(8,128)(2,1)S(1)}, u32[]{:S(2)}, u32[]{:S(2)}) collective-permute-start(bf16[256,384]{1,0:T(8,128)(2,1)S(1)} %get-tuple-element.165), channel_id=1, source_target_pairs={{0,2},{1,3},{2,0},{3,1},{4,6},{5,7},{6,4},{7,5},{8,10},{9,11},{10,... | collective-permute-start | bytes 589832 | tf_op jit(solution)/shard_map/ppermute | solution.py:777
  130.0 9.5 %collective-permute-start.8 = (bf16[256,384]{1,0:T(8,128)(2,1)S(1)}, bf16[256,384]{1,0:T(8,128)(2,1)S(1)}, u32[]{:S(2)}, u32[]{:S(2)}) collective-permute-start(bf16[256,384]{1,0:T(8,128)(2,1)S(1)} %get-tuple-element.164), channel_id=1, source_target_pairs={{0,3},{1,2},{2,1},{3,0},{4,7},{5,6},{6,5},{7,4},{8,11},{9,10},{10,... | collective-permute-start | bytes 589832 | tf_op jit(solution)/shard_map/ppermute | solution.py:777
  168.9 18.8 %collective-permute-start.10 = (bf16[256,384]{1,0:T(8,128)(2,1)S(1)}, bf16[256,384]{1,0:T(8,128)(2,1)S(1)}, u32[]{:S(2)}, u32[]{:S(2)}) collective-permute-start(bf16[256,384]{1,0:T(8,128)(2,1)S(1)} %get-tuple-element.161), channel_id=1, source_target_pairs={{0,2},{1,3},{2,0},{3,1},{4,6},{5,7},{6,4},{7,5},{8,10},{9,11},{10,... | collective-permute-start | bytes 589832 | tf_op jit(solution)/shard_map/ppermute | solution.py:777
  170.3 17.4 %collective-permute-start.11 = (bf16[256,384]{1,0:T(8,128)(2,1)S(1)}, bf16[256,384]{1,0:T(8,128)(2,1)S(1)}, u32[]{:S(2)}, u32[]{:S(2)}) collective-permute-start(bf16[256,384]{1,0:T(8,128)(2,1)S(1)} %get-tuple-element.160), channel_id=1, source_target_pairs={{0,3},{1,2},{2,1},{3,0},{4,7},{5,6},{6,5},{7,4},{8,11},{9,10},{10,... | collective-permute-start | bytes 589832 | tf_op jit(solution)/shard_map/ppermute | solution.py:777
  170.5 17.2 %collective-permute-start.9 = (bf16[256,384]{1,0:T(8,128)(2,1)S(1)}, bf16[256,384]{1,0:T(8,128)(2,1)S(1)}, u32[]{:S(2)}, u32[]{:S(2)}) collective-permute-start(bf16[256,384]{1,0:T(8,128)(2,1)S(1)} %get-tuple-element.162), channel_id=1, source_target_pairs={{0,1},{1,0},{2,3},{3,2},{4,5},{5,4},{6,7},{7,6},{8,9},{9,8},{10,11... | collective-permute-start | bytes 589832 | tf_op jit(solution)/shard_map/ppermute | solution.py:777
  187.7 17.6 %collective-permute-start.12 = (bf16[2,1792,768]{2,1,0:T(8,128)(2,1)}, bf16[2,1792,768]{2,1,0:T(8,128)(2,1)}, u32[]{:S(2)}, u32[]{:S(2)}) collective-permute-start(bf16[2,1792,768]{2,1,0:T(8,128)(2,1)} %get-tuple-element.83), channel_id=1, source_target_pairs={{0,1},{1,0},{2,3},{3,2},{4,5},{5,4},{6,7},{7,6},{8,9},{9,8},{10,11... | collective-permute-start | bytes 16515080 | tf_op jit(solution)/shard_map/ppermute | solution.py:777
  214.4 43.5 %collective-permute-start.17 = (bf16[2,448,768]{2,1,0:T(8,128)(2,1)}, bf16[2,448,768]{2,1,0:T(8,128)(2,1)S(1)}, u32[]{:S(2)}, u32[]{:S(2)}) collective-permute-start(bf16[2,448,768]{2,1,0:T(8,128)(2,1)} %get-tuple-element.129.refs_11_), channel_id=1, source_target_pairs={{0,4},{4,0},{8,12},{12,8},{16,20},{20,16},{24,28},{28,24},{1,5},{5... | collective-permute-start | bytes 4128776 | tf_op jit(solution)/shard_map/ppermute | solution.py:777
  215.9 42.0 %collective-permute-start.18 = (bf16[2,448,768]{2,1,0:T(8,128)(2,1)}, bf16[2,448,768]{2,1,0:T(8,128)(2,1)}, u32[]{:S(2)}, u32[]{:S(2)}) collective-permute-start(bf16[2,448,768]{2,1,0:T(8,128)(2,1)} %get-tuple-element.128.refs_12_), channel_id=1, source_target_pairs={{0,8},{4,12},{8,0},{12,4},{16,24},{20,28},{24,16},{28,20},{1,9},{5... | collective-permute-start | bytes 4128776 | tf_op jit(solution)/shard_map/ppermute | solution.py:777
  248.6 17.8 %collective-permute-start.13 = (bf16[2,1024,384]{2,1,0:T(8,128)(2,1)}, bf16[2,1024,384]{2,1,0:T(8,128)(2,1)}, u32[]{:S(2)}, u32[]{:S(2)}) collective-permute-start(bf16[2,1024,384]{2,1,0:T(8,128)(2,1)} %get-tuple-element.90), channel_id=1, source_target_pairs={{0,1},{1,0},{2,3},{3,2},{4,5},{5,4},{6,7},{7,6},{8,9},{9,8},{10,11... | collective-permute-start | bytes 4718600 | tf_op jit(solution)/shard_map/ppermute | solution.py:777
  248.6 3.3 collective-permute-start.15
  252.8 4.4 collective-permute-start.16
  264.5 50.9 %collective-permute-start.20 = (bf16[2,224,768]{2,1,0:T(8,128)(2,1)}, bf16[2,224,768]{2,1,0:T(8,128)(2,1)}, u32[]{:S(2)}, u32[]{:S(2)}) collective-permute-start(bf16[2,224,768]{2,1,0:T(8,128)(2,1)} %broadcast_select_fusion.12.refs_9_), channel_id=1, source_target_pairs={{0,4},{4,0},{8,12},{12,8},{16,20},{20,16},{24,28},{28,24},{1,5},{5... | collective-permute-start | bytes 2064392 | tf_op jit(solution)/shard_map/ppermute | solution.py:777
  266.0 52.7 %collective-permute-start.19 = (bf16[2,224,768]{2,1,0:T(8,128)(2,1)}, bf16[2,224,768]{2,1,0:T(8,128)(2,1)}, u32[]{:S(2)}, u32[]{:S(2)}) collective-permute-start(bf16[2,224,768]{2,1,0:T(8,128)(2,1)} %broadcast_select_fusion.13.refs_8_), channel_id=1, source_target_pairs={{0,8},{4,12},{8,0},{12,4},{16,24},{20,28},{24,16},{28,20},{1,9},{5... | collective-permute-start | bytes 2064392 | tf_op jit(solution)/shard_map/ppermute | solution.py:777
  269.8 18.8 %collective-permute-start.14 = (bf16[1024,384]{1,0:T(8,128)(2,1)S(1)}, bf16[1024,384]{1,0:T(8,128)(2,1)}, u32[]{:S(2)}, u32[]{:S(2)}) collective-permute-start(bf16[1024,384]{1,0:T(8,128)(2,1)S(1)} %get-tuple-element.124.refs_7_), channel_id=1, source_target_pairs={{0,2},{1,3},{2,0},{3,1},{4,6},{5,7},{6,4},{7,5},{8,10},{9,11},{10,... | collective-permute-start | bytes 2359304 | tf_op jit(solution)/shard_map/ppermute | solution.py:777
  320.4 32.8 %collective-permute-start.22 = (bf16[512,768]{1,0:T(8,128)(2,1)}, bf16[512,768]{1,0:T(8,128)(2,1)S(1)}, u32[]{:S(2)}, u32[]{:S(2)}) collective-permute-start(bf16[512,768]{1,0:T(8,128)(2,1)} %broadcast_select_fusion.7.refs_6_), channel_id=1, source_target_pairs={{0,8},{4,12},{8,0},{12,4},{16,24},{20,28},{24,16},{28,20},{1,9},{5... | collective-permute-start | bytes 2359304 | tf_op jit(solution)/shard_map/ppermute | solution.py:777
  321.5 37.0 %collective-permute-start.21 = (bf16[544,768]{1,0:T(8,128)(2,1)S(1)}, bf16[544,768]{1,0:T(8,128)(2,1)}, u32[]{:S(2)}, u32[]{:S(2)}) collective-permute-start(bf16[544,768]{1,0:T(8,128)(2,1)S(1)} %broadcast_select_fusion.4.refs_5_), channel_id=1, source_target_pairs={{0,4},{4,0},{8,12},{12,8},{16,20},{20,16},{24,28},{28,24},{1,5},{5... | collective-permute-start | bytes 2506760 | tf_op jit(solution)/shard_map/ppermute | solution.py:777
  323.0 56.2 %collective-permute-start.36 = (bf16[2,112,768]{2,1,0:T(8,128)(2,1)S(1)}, bf16[2,112,768]{2,1,0:T(8,128)(2,1)}, u32[]{:S(2)}, u32[]{:S(2)}) collective-permute-start(bf16[2,112,768]{2,1,0:T(8,128)(2,1)S(1)} %broadcast_select_fusion.25.refs_7_), channel_id=1, source_target_pairs={{0,16},{4,20},{8,24},{12,28},{16,0},{20,4},{24,8},{28,12},{1,17},{... | collective-permute-start | bytes 1032200 | tf_op jit(solution)/shard_map/ppermute | solution.py:777
  325.6 56.4 %collective-permute-start.37 = (bf16[2,112,768]{2,1,0:T(8,128)(2,1)S(1)}, bf16[2,112,768]{2,1,0:T(8,128)(2,1)S(1)}, u32[]{:S(2)}, u32[]{:S(2)}) collective-permute-start(bf16[2,112,768]{2,1,0:T(8,128)(2,1)S(1)} %broadcast_select_fusion.24.refs_8_), channel_id=1, source_target_pairs={{0,16},{4,20},{8,24},{12,28},{16,0},{20,4},{24,8},{28,12},{1,17},{... | collective-permute-start | bytes 1032200 | tf_op jit(solution)/shard_map/ppermute | solution.py:777
  357.0 43.3 %collective-permute-start.31 = (bf16[256,768]{1,0:T(8,128)(2,1)}, bf16[256,768]{1,0:T(8,128)(2,1)}, u32[]{:S(2)}, u32[]{:S(2)}) collective-permute-start(bf16[256,768]{1,0:T(8,128)(2,1)} %broadcast_select_fusion.19.refs_7_), channel_id=1, source_target_pairs={{0,4},{4,0},{8,12},{12,8},{16,20},{20,16},{24,28},{28,24},{1,5},{5... | collective-permute-start | bytes 1179656 | tf_op jit(solution)/shard_map/ppermute | solution.py:777
  377.2 24.9 %collective-permute-start.26 = (bf16[272,768]{1,0:T(8,128)(2,1)}, bf16[272,768]{1,0:T(8,128)(2,1)}, u32[]{:S(2)}, u32[]{:S(2)}) collective-permute-start(bf16[272,768]{1,0:T(8,128)(2,1)} %broadcast_select_fusion.16.refs_6_), channel_id=1, source_target_pairs={{0,8},{4,12},{8,0},{12,4},{16,24},{20,28},{24,16},{28,20},{1,9},{5... | collective-permute-start | bytes 1253384 | tf_op jit(solution)/shard_map/ppermute | solution.py:777
  380.4 7.4 %collective-permute-start.47 = (bf16[112,768]{1,0:T(8,128)(2,1)S(1)}, bf16[112,768]{1,0:T(8,128)(2,1)S(1)}, u32[]{:S(2)}, u32[]{:S(2)}) collective-permute-start(bf16[112,768]{1,0:T(8,128)(2,1)S(1)} %slice_bitcast_fusion.14), channel_id=1, source_target_pairs={{0,2},{1,3},{2,0},{3,1},{4,6},{5,7},{6,4},{7,5},{8,10},{9,11},{10,... | collective-permute-start | bytes 516104 | tf_op jit(solution)/shard_map/ppermute | solution.py:777
  382.1 9.3 %collective-permute-start.43 = (bf16[112,768]{1,0:T(8,128)(2,1)S(1)}, bf16[112,768]{1,0:T(8,128)(2,1)S(1)}, u32[]{:S(2)}, u32[]{:S(2)}) collective-permute-start(bf16[112,768]{1,0:T(8,128)(2,1)S(1)} %slice_bitcast_fusion.16), channel_id=1, source_target_pairs={{0,2},{1,3},{2,0},{3,1},{4,6},{5,7},{6,4},{7,5},{8,10},{9,11},{10,... | collective-permute-start | bytes 516104 | tf_op jit(solution)/shard_map/ppermute | solution.py:777
  382.8 11.2 %collective-permute-start.23 = (bf16[256,384]{1,0:T(8,128)(2,1)S(1)}, bf16[256,384]{1,0:T(8,128)(2,1)S(1)}, u32[]{:S(2)}, u32[]{:S(2)}) collective-permute-start(bf16[256,384]{1,0:T(8,128)(2,1)S(1)} %get-tuple-element.159), channel_id=1, source_target_pairs={{0,3},{1,2},{2,1},{3,0},{4,7},{5,6},{6,5},{7,4},{8,11},{9,10},{10,... | collective-permute-start | bytes 589832 | tf_op jit(solution)/shard_map/ppermute | solution.py:777
  387.8 9.4 %collective-permute-start.24 = (bf16[256,384]{1,0:T(8,128)(2,1)S(1)}, bf16[256,384]{1,0:T(8,128)(2,1)S(1)}, u32[]{:S(2)}, u32[]{:S(2)}) collective-permute-start(bf16[256,384]{1,0:T(8,128)(2,1)S(1)} %get-tuple-element.158), channel_id=1, source_target_pairs={{0,2},{1,3},{2,0},{3,1},{4,6},{5,7},{6,4},{7,5},{8,10},{9,11},{10,... | collective-permute-start | bytes 589832 | tf_op jit(solution)/shard_map/ppermute | solution.py:777
  391.5 8.1 %collective-permute-start.25 = (bf16[256,384]{1,0:T(8,128)(2,1)S(1)}, bf16[256,384]{1,0:T(8,128)(2,1)S(1)}, u32[]{:S(2)}, u32[]{:S(2)}) collective-permute-start(bf16[256,384]{1,0:T(8,128)(2,1)S(1)} %get-tuple-element.157), channel_id=1, source_target_pairs={{0,1},{1,0},{2,3},{3,2},{4,5},{5,4},{6,7},{7,6},{8,9},{9,8},{10,11... | collective-permute-start | bytes 589832 | tf_op jit(solution)/shard_map/ppermute | solution.py:777
  394.0 30.1 %collective-permute-start.48 = (bf16[112,768]{1,0:T(8,128)(2,1)}, bf16[112,768]{1,0:T(8,128)(2,1)}, u32[]{:S(2)}, u32[]{:S(2)}) collective-permute-start(bf16[112,768]{1,0:T(8,128)(2,1)} %fusion.21), channel_id=1, source_target_pairs={{0,16},{4,20},{8,24},{12,28},{16,0},{20,4},{24,8},{28,12},{1,17},{... | collective-permute-start | bytes 516104 | tf_op jit(solution)/shard_map/ppermute | solution.py:777
  397.1 33.3 %collective-permute-start.44 = (bf16[112,768]{1,0:T(8,128)(2,1)S(1)}, bf16[112,768]{1,0:T(8,128)(2,1)}, u32[]{:S(2)}, u32[]{:S(2)}) collective-permute-start(bf16[112,768]{1,0:T(8,128)(2,1)S(1)} %fusion.22), channel_id=1, source_target_pairs={{0,16},{4,20},{8,24},{12,28},{16,0},{20,4},{24,8},{28,12},{1,17},{... | collective-permute-start | bytes 516104 | tf_op jit(solution)/shard_map/ppermute | solution.py:777
  422.5 3.7 collective-permute-start.39
  426.4 3.7 collective-permute-start.40
  426.7 35.8 %collective-permute-start.49 = (bf16[224,768]{1,0:T(8,128)(2,1)S(1)}, bf16[224,768]{1,0:T(8,128)(2,1)S(1)}, u32[]{:S(2)}, u32[]{:S(2)}) collective-permute-start(bf16[224,768]{1,0:T(8,128)(2,1)S(1)} %pad_maximum_fusion.10), channel_id=1, source_target_pairs={{0,8},{4,12},{8,0},{12,4},{16,24},{20,28},{24,16},{28,20},{1,9},{5... | collective-permute-start | bytes 1032200 | tf_op jit(solution)/shard_map/ppermute | solution.py:777
  430.0 5.9 %collective-permute-start.41 = (f32[16,128]{1,0:T(8,128)S(1)}, f32[16,128]{1,0:T(8,128)S(1)}, u32[]{:S(2)}, u32[]{:S(2)}) collective-permute-start(f32[16,128]{1,0:T(8,128)S(1)} %bitcast_add_fusion), channel_id=1, source_target_pairs={{0,8},{4,12},{8,0},{12,4},{16,24},{20,28},{24,16},{28,20},{1,9},{5... | collective-permute-start | bytes 24584 | tf_op jit(solution)/shard_map/ppermute | solution.py:777
  436.0 10.2 %collective-permute-start.42 = (f32[16,128]{1,0:T(8,128)S(1)}, f32[16,128]{1,0:T(8,128)S(1)}, u32[]{:S(2)}, u32[]{:S(2)}) collective-permute-start(f32[16,128]{1,0:T(8,128)S(1)} %fusion.32), channel_id=1, source_target_pairs={{0,16},{4,20},{8,24},{12,28},{16,0},{20,4},{24,8},{28,12},{1,17},{... | collective-permute-start | bytes 24584 | tf_op jit(solution)/shard_map/ppermute | solution.py:777
  436.6 29.2 %collective-permute-start.45 = (bf16[224,768]{1,0:T(8,128)(2,1)S(1)}, bf16[224,768]{1,0:T(8,128)(2,1)S(1)}, u32[]{:S(2)}, u32[]{:S(2)}) collective-permute-start(bf16[224,768]{1,0:T(8,128)(2,1)S(1)} %pad_maximum_fusion.9), channel_id=1, source_target_pairs={{0,4},{4,0},{8,12},{12,8},{16,20},{20,16},{24,28},{28,24},{1,5},{5... | collective-permute-start | bytes 1032200 | tf_op jit(solution)/shard_map/ppermute | solution.py:777
  438.3 15.4 %collective-permute-start.32 = (bf16[128,768]{1,0:T(8,128)(2,1)}, bf16[128,768]{1,0:T(8,128)(2,1)}, u32[]{:S(2)}, u32[]{:S(2)}) collective-permute-start(bf16[128,768]{1,0:T(8,128)(2,1)} %broadcast_select_fusion.39.refs_4_), channel_id=1, source_target_pairs={{0,16},{4,20},{8,24},{12,28},{16,0},{20,4},{24,8},{28,12},{1,17},{... | collective-permute-start | bytes 589832 | tf_op jit(solution)/shard_map/ppermute | solution.py:777
  440.7 21.6 %collective-permute-start.27 = (bf16[136,768]{1,0:T(8,128)(2,1)S(1)}, bf16[136,768]{1,0:T(8,128)(2,1)S(1)}, u32[]{:S(2)}, u32[]{:S(2)}) collective-permute-start(bf16[136,768]{1,0:T(8,128)(2,1)S(1)} %copy-done.18), channel_id=1, source_target_pairs={{0,16},{4,20},{8,24},{12,28},{16,0},{20,4},{24,8},{28,12},{1,17},{... | collective-permute-start | bytes 626696 | tf_op jit(solution)/shard_map/ppermute | solution.py:777
  454.8 16.3 %collective-permute-start.33 = (bf16[128,768]{1,0:T(8,128)(2,1)S(1)}, bf16[128,768]{1,0:T(8,128)(2,1)S(1)}, u32[]{:S(2)}, u32[]{:S(2)}) collective-permute-start(bf16[128,768]{1,0:T(8,128)(2,1)S(1)} %add_convert_fusion.12), channel_id=1, source_target_pairs={{0,16},{4,20},{8,24},{12,28},{16,0},{20,4},{24,8},{28,12},{1,17},{... | collective-permute-start | bytes 589832 | tf_op jit(solution)/shard_map/ppermute | solution.py:777
  462.4 12.1 %collective-permute-start.28 = (bf16[136,768]{1,0:T(8,128)(2,1)S(1)}, bf16[136,768]{1,0:T(8,128)(2,1)S(1)}, u32[]{:S(2)}, u32[]{:S(2)}) collective-permute-start(bf16[136,768]{1,0:T(8,128)(2,1)S(1)} %add_convert_fusion.11), channel_id=1, source_target_pairs={{0,16},{4,20},{8,24},{12,28},{16,0},{20,4},{24,8},{28,12},{1,17},{... | collective-permute-start | bytes 626696 | tf_op jit(solution)/shard_map/ppermute | solution.py:777
  462.7 41.1 %collective-permute-start.50 = (bf16[448,768]{1,0:T(8,128)(2,1)S(1)}, bf16[448,768]{1,0:T(8,128)(2,1)S(1)}, u32[]{:S(2)}, u32[]{:S(2)}) collective-permute-start(bf16[448,768]{1,0:T(8,128)(2,1)S(1)} %pad_maximum_fusion.6), channel_id=1, source_target_pairs={{0,4},{4,0},{8,12},{12,8},{16,20},{20,16},{24,28},{28,24},{1,5},{5... | collective-permute-start | bytes 2064392 | tf_op jit(solution)/shard_map/ppermute | solution.py:777
  471.1 13.5 %collective-permute-start.34 = (bf16[256,768]{1,0:T(8,128)(2,1)S(1)}, bf16[256,768]{1,0:T(8,128)(2,1)S(1)}, u32[]{:S(2)}, u32[]{:S(2)}) collective-permute-start(bf16[256,768]{1,0:T(8,128)(2,1)S(1)} %pad_maximum_fusion.8), channel_id=1, source_target_pairs={{0,4},{4,0},{8,12},{12,8},{16,20},{20,16},{24,28},{28,24},{1,5},{5... | collective-permute-start | bytes 1179656 | tf_op jit(solution)/shard_map/ppermute | solution.py:777
  474.6 16.7 %collective-permute-start.29 = (bf16[272,768]{1,0:T(8,128)(2,1)S(1)}, bf16[272,768]{1,0:T(8,128)(2,1)S(1)}, u32[]{:S(2)}, u32[]{:S(2)}) collective-permute-start(bf16[272,768]{1,0:T(8,128)(2,1)S(1)} %pad_maximum_fusion.7), channel_id=1, source_target_pairs={{0,8},{4,12},{8,0},{12,4},{16,24},{20,28},{24,16},{28,20},{1,9},{5... | collective-permute-start | bytes 1253384 | tf_op jit(solution)/shard_map/ppermute | solution.py:777
  474.8 27.3 %collective-permute-start.46 = (bf16[448,768]{1,0:T(8,128)(2,1)S(1)}, bf16[448,768]{1,0:T(8,128)(2,1)S(1)}, u32[]{:S(2)}, u32[]{:S(2)}) collective-permute-start(bf16[448,768]{1,0:T(8,128)(2,1)S(1)} %pad_maximum_fusion.5), channel_id=1, source_target_pairs={{0,8},{4,12},{8,0},{12,4},{16,24},{20,28},{24,16},{28,20},{1,9},{5... | collective-permute-start | bytes 2064392 | tf_op jit(solution)/shard_map/ppermute | solution.py:777
  484.9 32.1 %collective-permute-start.35 = (bf16[512,768]{1,0:T(8,128)(2,1)S(1)}, bf16[512,768]{1,0:T(8,128)(2,1)S(1)}, u32[]{:S(2)}, u32[]{:S(2)}) collective-permute-start(bf16[512,768]{1,0:T(8,128)(2,1)S(1)} %pad_maximum_fusion.4), channel_id=1, source_target_pairs={{0,8},{4,12},{8,0},{12,4},{16,24},{20,28},{24,16},{28,20},{1,9},{5... | collective-permute-start | bytes 2359304 | tf_op jit(solution)/shard_map/ppermute | solution.py:777
  491.6 25.7 %collective-permute-start.30 = (bf16[544,768]{1,0:T(8,128)(2,1)S(1)}, bf16[544,768]{1,0:T(8,128)(2,1)S(1)}, u32[]{:S(2)}, u32[]{:S(2)}) collective-permute-start(bf16[544,768]{1,0:T(8,128)(2,1)S(1)} %pad_maximum_fusion.3), channel_id=1, source_target_pairs={{0,4},{4,0},{8,12},{12,8},{16,20},{20,16},{24,28},{28,24},{1,5},{5... | collective-permute-start | bytes 2506760 | tf_op jit(solution)/shard_map/ppermute | solution.py:777
  (48 other events, 465.6 us)
